TPU v7x, 32 devices: a whole 2x2x4 slice. The times are simulated.
32 devices in a mesh: grp: 4 (over y, core), seq: 8 (over z, x).
Axes of the slice: x: 2, y: 2, z: 4, core: 2. Of those that a mesh axis runs over, the one named last changes fastest.
Arguments:
- query: bfloat16 [4, 4096, 640], P('grp', 'seq'), may hold values from -64 to 64
- resp_kv: bfloat16 [4, 4096, 256], P('grp', 'seq'), may hold values from -6 to 6
- prompt_kv: bfloat16 [4, 2048, 256], P('grp', 'seq'), may hold values from -64 to 64
- grad_out: bfloat16 [4, 4096, 640], P('grp', 'seq'), may hold values from -6 to 6
- rewards: float32 [4, 16], P('grp'), may hold values from -4 to 4
- lengths: int32 [4, 16], P('grp'), may hold values from 1 to 256, as said below
- block_order: int32 [4, 32], P('grp'), may hold values from 0 to 31, each once within a row
Outputs:
- grad_query: bfloat16 [4, 4096, 640], P('grp', 'seq')
- grad_stream: bfloat16 [4, 4096, 256], P('grp', 'seq')
- grad_prompt: bfloat16 [4, 2048, 256], P('grp', 'seq')
Inputs may be any that keep to these rules, and one draw needn't show every extreme that they name: `lengths`: each response has 1 to 256 tokens; some response has exactly 256. Each row of block_order names every response block of its group once.
All inputs are finite; a program needn't handle non-finite values.
Results may differ from a plain program's by a relative error of at most 0.015.
Values may be sent and summed in bfloat16 or wider, within the bound.
No kernel may reach another device: no remote copies, remote signals or barrier semaphores. Data moves between devices by JAX's collectives and lax.ppermute only.
A program may use at most 128 MiB of HBM per device.

v0:
```python
from functools import partial

import jax
import jax.numpy as jnp
from jax import lax
from jax.sharding import PartitionSpec as P

RESP = 16
BLK = 128
NB = 2


LOSS_SCALE = 32.0
BIG_NEGATIVE = -1e30


def product(pattern, first_operand, second_operand):
    return jnp.einsum(pattern, first_operand, second_operand, preferred_element_type=jnp.float32)


def block_terms(query_block, weighted, prompt_pairs, own_pairs, positions):
    half_width = prompt_pairs.shape[1] // 2
    score_scale = half_width ** (-0.5)
    prompt_keys = prompt_pairs[:, :half_width]
    prompt_values = prompt_pairs[:, half_width:]
    own_keys = own_pairs[:, :half_width]
    own_values = own_pairs[:, half_width:]
    visible = (jnp.arange(own_pairs.shape[0], dtype=jnp.int32)[None, :] <= positions[:, None])[None]
    scores_prompt = product("thd,kd->htk", query_block, prompt_keys) * score_scale
    scores_own = jnp.where(
        visible, product("thd,kd->htk", query_block, own_keys) * score_scale, BIG_NEGATIVE
    )
    peak_score = jnp.maximum(jnp.max(scores_prompt, axis=2), jnp.max(scores_own, axis=2))
    expo_prompt = jnp.exp(scores_prompt - peak_score[..., None])
    expo_own = jnp.where(visible, jnp.exp(scores_own - peak_score[..., None]), 0.0)
    prob_total = jnp.sum(expo_prompt, axis=2) + jnp.sum(expo_own, axis=2)
    probs_prompt = expo_prompt / prob_total[..., None]
    probs_own = expo_own / prob_total[..., None]
    low_prompt = probs_prompt.astype(jnp.bfloat16)
    low_own = probs_own.astype(jnp.bfloat16)
    attended = product("htk,kd->thd", low_prompt, prompt_values) + product(
        "htk,kd->thd", low_own, own_values
    )
    row_delta = jnp.einsum("thd,thd->ht", weighted.astype(jnp.float32), attended)
    grad_prompt_scores = (
        probs_prompt * (product("thd,kd->htk", weighted, prompt_values) - row_delta[..., None])
    ).astype(jnp.bfloat16)
    grad_own_scores = (
        probs_own * (product("thd,kd->htk", weighted, own_values) - row_delta[..., None])
    ).astype(jnp.bfloat16)
    grad_query = (
        product("htk,kd->thd", grad_prompt_scores, prompt_keys)
        + product("htk,kd->thd", grad_own_scores, own_keys)
    ) * score_scale
    prompt_term = jnp.concatenate(
        [
            product("htk,thd->kd", grad_prompt_scores, query_block) * score_scale,
            product("htk,thd->kd", low_prompt, weighted),
        ],
        axis=1,
    )
    own_term = jnp.concatenate(
        [
            product("htk,thd->kd", grad_own_scores, query_block) * score_scale,
            product("htk,thd->kd", low_own, weighted),
        ],
        axis=1,
    )
    return (grad_query, prompt_term, own_term, peak_score, prob_total, row_delta)


def local(query, resp_kv, prompt_kv, grad_out, rewards, lengths, block_order):
    head_width = resp_kv.shape[2] // 2
    head_count = query.shape[2] // head_width
    row_count = query.shape[1]
    local_blocks = row_count // BLK
    capacity = NB * BLK
    group_count = lax.axis_size("grp")
    seq_count = lax.axis_size("seq")
    count = lax.psum(jnp.sum(lengths[0]).astype(jnp.float32), "grp")
    advantage = rewards[0] - jnp.mean(rewards[0])
    factor = advantage * (LOSS_SCALE * group_count * RESP * capacity) / count
    block_plan = block_order[0]
    inverse = jnp.argsort(block_plan)
    prompt_all = lax.all_gather(prompt_kv[0], "seq", axis=0, tiled=True)
    stream_all = lax.all_gather(resp_kv[0], "seq", axis=0, tiled=True)
    blocks = stream_all.reshape(block_plan.shape[0], BLK, 2 * head_width)
    stored = lax.axis_index("seq") * local_blocks + jnp.arange(local_blocks, dtype=jnp.int32)
    stream_block = block_plan[stored]
    response = stream_block // NB
    positions = (stream_block % NB)[:, None] * BLK + jnp.arange(BLK, dtype=jnp.int32)[None, :]
    token_weight = jnp.where(
        positions < lengths[0][response][:, None], factor[response][:, None], 0.0
    )
    weighted = (
        grad_out[0].reshape(local_blocks, BLK, head_count * head_width).astype(jnp.float32)
        * token_weight[..., None]
    ).astype(jnp.bfloat16)
    weighted = weighted.reshape(local_blocks, BLK, head_count, head_width)
    queries = query[0].reshape(local_blocks, BLK, head_count, head_width)
    slot_table = inverse.reshape(RESP, NB)[response]
    block_items = (queries, weighted, slot_table, positions)

    def block_step(with_prompt, carried, block_item):
        prompt_sum, stream_sum = carried
        query_block, weight_block, slot_index, block_positions = block_item
        own_pairs = jnp.take(blocks, slot_index, axis=0).reshape(capacity, 2 * head_width)
        grad_query, prompt_term, own_term, peak_score, prob_total, row_delta = block_terms(
            query_block, weight_block, prompt_all, own_pairs, block_positions
        )
        stream_sum = stream_sum.at[slot_index].add(own_term.reshape(NB, BLK, 2 * head_width))
        prompt_sum = prompt_sum + prompt_term
        return (
            (prompt_sum, stream_sum),
            (grad_query.astype(jnp.bfloat16), peak_score, prob_total, row_delta),
        )

    stream_zero = jnp.zeros((block_plan.shape[0], BLK, 2 * head_width), jnp.float32)
    initial = (jnp.zeros((prompt_all.shape[0], 2 * head_width), jnp.float32), stream_zero)
    (prompt_sum, stream_sum), block_outputs = lax.scan(
        partial(block_step, True), initial, block_items
    )
    prompt_grad = lax.psum_scatter(
        prompt_sum.astype(jnp.bfloat16), "seq", scatter_dimension=0, tiled=True
    )
    grad_rows = block_outputs[0]
    outgoing = stream_sum.reshape(seq_count, local_blocks * BLK, 2 * head_width)
    incoming = lax.all_to_all(
        outgoing.astype(jnp.bfloat16), "seq", split_axis=0, concat_axis=0, tiled=True
    ).astype(outgoing.dtype)
    stream_grad = jnp.sum(incoming, axis=0)
    grad_query = grad_rows.reshape(row_count, head_count * head_width)
    return (grad_query[None], stream_grad.astype(jnp.bfloat16)[None], prompt_grad[None])


def solution(mesh):
    in_specs = (
        P("grp", "seq", None),
        P("grp", "seq", None),
        P("grp", "seq", None),
        P("grp", "seq", None),
        P("grp", None),
        P("grp", None),
        P("grp", None),
    )
    out_specs = (P("grp", "seq", None), P("grp", "seq", None), P("grp", "seq", None))
    return jax.shard_map(local, mesh=mesh, in_specs=in_specs, out_specs=out_specs, check_vma=False)
```

profile of v0, /device:TPU:0, one launch (start us, length us, event | category | flops | bytes accessed | tf_op | source)
XLA Modules:
  0.0 314.5 jit_solution(9408043584607266406)
XLA Ops:
  8.6 1.3 reduce_sum.49
  10.6 8.9 %psum.7 = f32[]{:T(128)} all-reduce(f32[]{:T(128)S(6)} %convert_element_type.43), channel_id=1, replica_groups=mesh['grp'=4,'seq'=8] {'grp'}, use_global_device_ids=true, to_apply=%region_2.0 | all-reduce | flops 1 | bytes 8 | tf_op jit(solution)/shard_map/psum | solution.py:80
  19.5 2.3 sort.17
  21.7 1.3 gather_fusion.1
  23.0 1.3 reduce_sum.48
  25.0 1.3 divide_bitcast_fusion
  26.9 1.3 gather_fusion.3
  28.9 1.8 reshape.309
  31.7 2.4 copy.33
  34.1 2.7 reshape.239
  36.8 1.6 multiply_convert_fusion
  38.5 1.5 copy.35
  40.0 13.2 %all-gather.5.cloned.1.call-done = bf16[1,2048,256]{2,1,0:T(8,128)(2,1)} async-done(((bf16[1,256,256]{2,1,0:T(8,128)(2,1)}), bf16[1,2048,256]{2,1,0:T(8,128)(2,1)}) %all-gather.5.cloned.1.call-update) | async-done | bytes 1048592 | tf_op jit(solution)/shard_map/all_gather | solution.py:85
  53.3 50.2 %all-gather.7.cloned.1.call-done = bf16[1,4096,256]{2,1,0:T(8,128)(2,1)} async-done(((bf16[1,512,256]{2,1,0:T(8,128)(2,1)}), bf16[1,4096,256]{2,1,0:T(8,128)(2,1)}) %all-gather.7.cloned.1.call-update) | async-done | bytes 2097168 | tf_op jit(solution)/shard_map/all_gather | solution.py:86
  103.5 2.5 broadcast_in_dim.83
  106.0 105.7 %while.15 = (s32[]{:T(128)}, f32[2048,256]{0,1:T(8,128)S(1)}, f32[32,128,256]{2,1,0:T(8,128)}, bf16[4,128,5,128]{3,1,2,0:T(8,128)(2,1)}, bf16[4,128,5,128]{3,1,2...) while((s32[]{:T(128)}, f32[2048,256]{0,1:T(8,128)S(1)}, ...), condition=%wide.region_10.11_spmd.clone, body=%wide.region_4.10_spmd.clone.sunk | while | flops 2295774208 | bytes 104755160 | solution.py:120
  106.1 2.1 gather_fusion
  108.4 1.2 fusion.127
  109.6 2.1 bitcast_reduce_fusion.2
  113.7 1.1 fusion.130
  115.7 1.2 fusion.135
  117.6 1.9 copy.62
  119.4 4.0 %convolution_bitcast_fusion.11 = f32[2048,128]{0,1:T(8,128)S(1)} fusion(bf16[4,128,5,128]{3,1,2,0:T(8,128)(2,1)} %get-tuple-element.234, s32[]{:T(128)S(6)} %copy.69, f32[128,5,2048]{2,0,1:T(8,128)} %copy-done, f32[5,128]{1,0:T(8,128)S(1)} %add.183, f32[5,128]{1,0:T(8,128)S(1)} %max.9), kind=kOutput, calls=%fused_computation.14.clone.1 | convolution fusion | flops 340787200 | bytes 6460420 | tf_op jit(solution)/shard_map/while/body/eval_jaxpr/htk,thd->kd/dot_general | solution.py:18
  123.5 2.4 fusion.132
  126.8 1.6 fusion.133
  130.1 2.3 scatter_fusion
  132.5 2.1 gather_fusion
  134.8 1.2 fusion.127
  136.0 2.1 bitcast_reduce_fusion.2
  140.1 1.1 fusion.130
  142.1 1.2 fusion.135
  144.0 1.9 copy.62
  145.9 4.0 %convolution_bitcast_fusion.11 = f32[2048,128]{0,1:T(8,128)S(1)} fusion(bf16[4,128,5,128]{3,1,2,0:T(8,128)(2,1)} %get-tuple-element.234, s32[]{:T(128)S(6)} %copy.69, f32[128,5,2048]{2,0,1:T(8,128)} %copy-done, f32[5,128]{1,0:T(8,128)S(1)} %add.183, f32[5,128]{1,0:T(8,128)S(1)} %max.9), kind=kOutput, calls=%fused_computation.14.clone.1 | convolution fusion | flops 340787200 | bytes 6460420 | tf_op jit(solution)/shard_map/while/body/eval_jaxpr/htk,thd->kd/dot_general | solution.py:18
  149.9 2.4 fusion.132
  153.2 1.6 fusion.133
  156.5 2.3 scatter_fusion
  158.9 2.1 gather_fusion
  161.2 1.2 fusion.127
  162.5 2.1 bitcast_reduce_fusion.2
  166.6 1.1 fusion.130
  168.5 1.2 fusion.135
  170.4 1.9 copy.62
  172.3 4.0 %convolution_bitcast_fusion.11 = f32[2048,128]{0,1:T(8,128)S(1)} fusion(bf16[4,128,5,128]{3,1,2,0:T(8,128)(2,1)} %get-tuple-element.234, s32[]{:T(128)S(6)} %copy.69, f32[128,5,2048]{2,0,1:T(8,128)} %copy-done, f32[5,128]{1,0:T(8,128)S(1)} %add.183, f32[5,128]{1,0:T(8,128)S(1)} %max.9), kind=kOutput, calls=%fused_computation.14.clone.1 | convolution fusion | flops 340787200 | bytes 6460420 | tf_op jit(solution)/shard_map/while/body/eval_jaxpr/htk,thd->kd/dot_general | solution.py:18
  176.4 2.4 fusion.132
  179.6 1.6 fusion.133
  182.9 2.3 scatter_fusion
  185.4 2.1 gather_fusion
  187.7 1.2 fusion.127
  188.9 2.1 bitcast_reduce_fusion.2
  193.0 1.1 fusion.130
  194.9 1.2 fusion.135
  196.9 1.9 copy.62
  198.7 4.0 %convolution_bitcast_fusion.11 = f32[2048,128]{0,1:T(8,128)S(1)} fusion(bf16[4,128,5,128]{3,1,2,0:T(8,128)(2,1)} %get-tuple-element.234, s32[]{:T(128)S(6)} %copy.69, f32[128,5,2048]{2,0,1:T(8,128)} %copy-done, f32[5,128]{1,0:T(8,128)S(1)} %add.183, f32[5,128]{1,0:T(8,128)S(1)} %max.9), kind=kOutput, calls=%fused_computation.14.clone.1 | convolution fusion | flops 340787200 | bytes 6460420 | tf_op jit(solution)/shard_map/while/body/eval_jaxpr/htk,thd->kd/dot_general | solution.py:18
  202.8 2.4 fusion.132
  206.1 1.6 fusion.133
  209.4 2.3 scatter_fusion
  211.7 3.8 %convert_element_type.45 = bf16[32,128,256]{2,1,0:T(8,128)(2,1)} convert(f32[32,128,256]{2,1,0:T(8,128)} %get-tuple-element.60) | non-fusion elementwise | flops 1048576 | bytes 6291456 | tf_op jit(solution)/shard_map/convert_element_type | solution.py:129
  215.5 4.4 %all-to-all-start = ((bf16[8,512,256]{2,1,0:T(8,128)(2,1)}), bf16[8,512,256]{2,1,0:T(8,128)(2,1)}, u32[]{:S(2)}, u32[]{:S(2)}) async-start(bf16[8,512,256]{2,1,0:T(8,128)(2,1)} %bitcast.269), calls=%async_computation | async-start | bytes 4194304 | tf_op jit(solution)/shard_map/all_to_all | solution.py:128
  220.0 1.4 copy.37
  221.4 1.6 copy.56
  223.0 1.6 reshape.310
  224.6 51.3 %all-to-all-done = bf16[8,512,256]{2,1,0:T(8,128)(2,1)} async-done(((bf16[8,512,256]{2,1,0:T(8,128)(2,1)}), bf16[8,512,256]{2,1,0:T(8,128)(2,1)}, u32[]{:S(2)}, u32[]{:S(2)}) %all-to-all-start) | async-done | bytes 2097184 | tf_op jit(solution)/shard_map/all_to_all | solution.py:128
  275.8 2.7 reduce_sum.50
  278.5 29.4 %reduce-scatter.2.cloned.1.call-done = bf16[256,256]{1,0:T(8,128)(2,1)} async-done(((bf16[2048,256]{1,0:T(8,128)(2,1)}), bf16[256,256]{1,0:T(8,128)(2,1)}) %reduce-scatter.2.cloned.1.call-update) | async-done | bytes 131088 | tf_op jit(solution)/shard_map/reduce_scatter | solution.py:123
  (168 shorter events, 29.1 us)
Async XLA Ops:
  7.2 46.1 %all-gather.5.cloned.1.call-start = ((), (), s32[]{:S(2)}) async-start(), calls=%async_computation.3 | async-start | bytes 1179648 | tf_op jit(solution)/shard_map/all_gather | solution.py:85
  7.9 95.6 %all-gather.7.cloned.1.call-start = ((), (), s32[]{:S(2)}) async-start(), calls=%async_computation.4 | async-start | bytes 2359296 | tf_op jit(solution)/shard_map/all_gather | solution.py:86
  108.4 7.0 %copy-start.2 = (bf16[256,256]{1,0:T(8,128)(2,1)}, bf16[256,256]{1,0:T(8,128)(2,1)S(1)}, u32[]{:S(2)}) copy-start(bf16[256,256]{1,0:T(8,128)(2,1)S(1)} %bitcast_select_fusion.2) | copy-start | bytes 393220 | tf_op jit(solution)/shard_map/while
  109.6 3.3 %copy-start.6 = (bf16[4,128,5,128]{3,1,2,0:T(8,128)(2,1)S(1)}, bf16[4,128,5,128]{3,1,2,0:T(8,128)(2,1)}, u32[]{:S(2)}) copy-start(bf16[4,128,5,128]{3,1,2,0:T(8,128)(2,1)} %get-tuple-element.234) | copy-start | bytes 1966084 | tf_op jit(solution)/shard_map/while
  111.7 3.2 %copy-start = (f32[128,5,2048]{2,0,1:T(8,128)}, f32[128,5,2048]{2,0,1:T(8,128)S(1)}, u32[]{:S(2)}) copy-start(f32[128,5,2048]{2,0,1:T(8,128)S(1)} %get-tuple-element.197) | copy-start | bytes 15728644 | tf_op jit(solution)/shard_map/while
  111.8 2.0 copy-start.4
  117.6 5.8 %slice-start = ((s8[5242880]{0:T(1024)(128)(4,1)}), s8[1048576]{0:T(1024)(128)(4,1)S(1)}, s32[]{:S(2)}) async-start(s8[5242880]{0:T(1024)(128)(4,1)} %bitcast.266), calls=%async_computation.5 | async-start | bytes 2097152 | tf_op jit(solution)/shard_map/while
  119.4 4.0 %slice-start.1 = ((s8[5242880]{0:T(1024)(128)(4,1)}), s8[4194304]{0:T(1024)(128)(4,1)S(1)}, s32[]{:S(2)}) async-start(s8[5242880]{0:T(1024)(128)(4,1)} %bitcast.266), calls=%async_computation.6 | async-start | bytes 8388608 | tf_op jit(solution)/shard_map/while
  119.4 4.1 %copy-start.5 = (bf16[2048,256]{1,0:T(8,128)(2,1)S(1)}, bf16[2048,256]{1,0:T(8,128)(2,1)}, u32[]{:S(2)}) copy-start(bf16[2048,256]{1,0:T(8,128)(2,1)} %get-tuple-element.230) | copy-start | bytes 3145732 | tf_op jit(solution)/shard_map/while
  125.9 2.5 copy-start.3
  126.8 3.3 %copy-start.1 = (f32[256,256]{1,0:T(8,128)S(1)}, f32[256,256]{1,0:T(8,128)}, u32[]{:S(2)}) copy-start(f32[256,256]{1,0:T(8,128)} %copy.62) | copy-start | bytes 786436 | tf_op jit(solution)/shard_map/while
  134.8 7.0 %copy-start.2 = (bf16[256,256]{1,0:T(8,128)(2,1)}, bf16[256,256]{1,0:T(8,128)(2,1)S(1)}, u32[]{:S(2)}) copy-start(bf16[256,256]{1,0:T(8,128)(2,1)S(1)} %bitcast_select_fusion.2) | copy-start | bytes 393220 | tf_op jit(solution)/shard_map/while
  136.0 3.3 %copy-start.6 = (bf16[4,128,5,128]{3,1,2,0:T(8,128)(2,1)S(1)}, bf16[4,128,5,128]{3,1,2,0:T(8,128)(2,1)}, u32[]{:S(2)}) copy-start(bf16[4,128,5,128]{3,1,2,0:T(8,128)(2,1)} %get-tuple-element.234) | copy-start | bytes 1966084 | tf_op jit(solution)/shard_map/while
  138.2 3.2 %copy-start = (f32[128,5,2048]{2,0,1:T(8,128)}, f32[128,5,2048]{2,0,1:T(8,128)S(1)}, u32[]{:S(2)}) copy-start(f32[128,5,2048]{2,0,1:T(8,128)S(1)} %get-tuple-element.197) | copy-start | bytes 15728644 | tf_op jit(solution)/shard_map/while
  138.2 2.0 copy-start.4
  144.0 5.8 %slice-start = ((s8[5242880]{0:T(1024)(128)(4,1)}), s8[1048576]{0:T(1024)(128)(4,1)S(1)}, s32[]{:S(2)}) async-start(s8[5242880]{0:T(1024)(128)(4,1)} %bitcast.266), calls=%async_computation.5 | async-start | bytes 2097152 | tf_op jit(solution)/shard_map/while
  145.8 4.0 %slice-start.1 = ((s8[5242880]{0:T(1024)(128)(4,1)}), s8[4194304]{0:T(1024)(128)(4,1)S(1)}, s32[]{:S(2)}) async-start(s8[5242880]{0:T(1024)(128)(4,1)} %bitcast.266), calls=%async_computation.6 | async-start | bytes 8388608 | tf_op jit(solution)/shard_map/while
  145.9 4.1 %copy-start.5 = (bf16[2048,256]{1,0:T(8,128)(2,1)S(1)}, bf16[2048,256]{1,0:T(8,128)(2,1)}, u32[]{:S(2)}) copy-start(bf16[2048,256]{1,0:T(8,128)(2,1)} %get-tuple-element.230) | copy-start | bytes 3145732 | tf_op jit(solution)/shard_map/while
  152.3 2.5 copy-start.3
  153.2 3.3 %copy-start.1 = (f32[256,256]{1,0:T(8,128)S(1)}, f32[256,256]{1,0:T(8,128)}, u32[]{:S(2)}) copy-start(f32[256,256]{1,0:T(8,128)} %copy.62) | copy-start | bytes 786436 | tf_op jit(solution)/shard_map/while
  161.2 7.0 %copy-start.2 = (bf16[256,256]{1,0:T(8,128)(2,1)}, bf16[256,256]{1,0:T(8,128)(2,1)S(1)}, u32[]{:S(2)}) copy-start(bf16[256,256]{1,0:T(8,128)(2,1)S(1)} %bitcast_select_fusion.2) | copy-start | bytes 393220 | tf_op jit(solution)/shard_map/while
  162.5 3.3 %copy-start.6 = (bf16[4,128,5,128]{3,1,2,0:T(8,128)(2,1)S(1)}, bf16[4,128,5,128]{3,1,2,0:T(8,128)(2,1)}, u32[]{:S(2)}) copy-start(bf16[4,128,5,128]{3,1,2,0:T(8,128)(2,1)} %get-tuple-element.234) | copy-start | bytes 1966084 | tf_op jit(solution)/shard_map/while
  164.6 3.2 %copy-start = (f32[128,5,2048]{2,0,1:T(8,128)}, f32[128,5,2048]{2,0,1:T(8,128)S(1)}, u32[]{:S(2)}) copy-start(f32[128,5,2048]{2,0,1:T(8,128)S(1)} %get-tuple-element.197) | copy-start | bytes 15728644 | tf_op jit(solution)/shard_map/while
  164.6 2.0 copy-start.4
  170.4 5.8 %slice-start = ((s8[5242880]{0:T(1024)(128)(4,1)}), s8[1048576]{0:T(1024)(128)(4,1)S(1)}, s32[]{:S(2)}) async-start(s8[5242880]{0:T(1024)(128)(4,1)} %bitcast.266), calls=%async_computation.5 | async-start | bytes 2097152 | tf_op jit(solution)/shard_map/while
  172.3 4.0 %slice-start.1 = ((s8[5242880]{0:T(1024)(128)(4,1)}), s8[4194304]{0:T(1024)(128)(4,1)S(1)}, s32[]{:S(2)}) async-start(s8[5242880]{0:T(1024)(128)(4,1)} %bitcast.266), calls=%async_computation.6 | async-start | bytes 8388608 | tf_op jit(solution)/shard_map/while
  172.3 4.1 %copy-start.5 = (bf16[2048,256]{1,0:T(8,128)(2,1)S(1)}, bf16[2048,256]{1,0:T(8,128)(2,1)}, u32[]{:S(2)}) copy-start(bf16[2048,256]{1,0:T(8,128)(2,1)} %get-tuple-element.230) | copy-start | bytes 3145732 | tf_op jit(solution)/shard_map/while
  178.8 2.5 copy-start.3
  179.6 3.3 %copy-start.1 = (f32[256,256]{1,0:T(8,128)S(1)}, f32[256,256]{1,0:T(8,128)}, u32[]{:S(2)}) copy-start(f32[256,256]{1,0:T(8,128)} %copy.62) | copy-start | bytes 786436 | tf_op jit(solution)/shard_map/while
  187.6 7.0 %copy-start.2 = (bf16[256,256]{1,0:T(8,128)(2,1)}, bf16[256,256]{1,0:T(8,128)(2,1)S(1)}, u32[]{:S(2)}) copy-start(bf16[256,256]{1,0:T(8,128)(2,1)S(1)} %bitcast_select_fusion.2) | copy-start | bytes 393220 | tf_op jit(solution)/shard_map/while
  188.9 3.3 %copy-start.6 = (bf16[4,128,5,128]{3,1,2,0:T(8,128)(2,1)S(1)}, bf16[4,128,5,128]{3,1,2,0:T(8,128)(2,1)}, u32[]{:S(2)}) copy-start(bf16[4,128,5,128]{3,1,2,0:T(8,128)(2,1)} %get-tuple-element.234) | copy-start | bytes 1966084 | tf_op jit(solution)/shard_map/while
  191.0 3.2 %copy-start = (f32[128,5,2048]{2,0,1:T(8,128)}, f32[128,5,2048]{2,0,1:T(8,128)S(1)}, u32[]{:S(2)}) copy-start(f32[128,5,2048]{2,0,1:T(8,128)S(1)} %get-tuple-element.197) | copy-start | bytes 15728644 | tf_op jit(solution)/shard_map/while
  191.0 2.0 copy-start.4
  196.8 5.8 %slice-start = ((s8[5242880]{0:T(1024)(128)(4,1)}), s8[1048576]{0:T(1024)(128)(4,1)S(1)}, s32[]{:S(2)}) async-start(s8[5242880]{0:T(1024)(128)(4,1)} %bitcast.266), calls=%async_computation.5 | async-start | bytes 2097152 | tf_op jit(solution)/shard_map/while
  198.7 4.0 %slice-start.1 = ((s8[5242880]{0:T(1024)(128)(4,1)}), s8[4194304]{0:T(1024)(128)(4,1)S(1)}, s32[]{:S(2)}) async-start(s8[5242880]{0:T(1024)(128)(4,1)} %bitcast.266), calls=%async_computation.6 | async-start | bytes 8388608 | tf_op jit(solution)/shard_map/while
  198.7 4.1 %copy-start.5 = (bf16[2048,256]{1,0:T(8,128)(2,1)S(1)}, bf16[2048,256]{1,0:T(8,128)(2,1)}, u32[]{:S(2)}) copy-start(bf16[2048,256]{1,0:T(8,128)(2,1)} %get-tuple-element.230) | copy-start | bytes 3145732 | tf_op jit(solution)/shard_map/while
  205.2 2.5 copy-start.3
  206.1 3.3 %copy-start.1 = (f32[256,256]{1,0:T(8,128)S(1)}, f32[256,256]{1,0:T(8,128)}, u32[]{:S(2)}) copy-start(f32[256,256]{1,0:T(8,128)} %copy.62) | copy-start | bytes 786436 | tf_op jit(solution)/shard_map/while
  215.5 60.3 %all-to-all-start = ((bf16[8,512,256]{2,1,0:T(8,128)(2,1)}), bf16[8,512,256]{2,1,0:T(8,128)(2,1)}, u32[]{:S(2)}, u32[]{:S(2)}) async-start(bf16[8,512,256]{2,1,0:T(8,128)(2,1)} %bitcast.269), calls=%async_computation | async-start | bytes 4194304 | tf_op jit(solution)/shard_map/all_to_all | solution.py:128
  219.9 88.0 %reduce-scatter.2.cloned.1.call-start = ((), (), s32[]{:S(2)}) async-start(), calls=%async_computation.2 | async-start | bytes 1179648 | tf_op jit(solution)/shard_map/reduce_scatter | solution.py:123
Sparse Core Ops, SparseCore 0:
  10.1 43.0 all-gather.4
  55.4 48.0 all-gather.6
  224.7 83.1 reduce-scatter.1
where the time goes:
time: 316 us; the launch traced here: 314 us
  waiting for transfers between devices  146 us (46%)
  matrix products  66 us (21%)
  local copies, waits for them, and re-layouts  39.1 us (12%)
  other arithmetic  34.5 us (11%)
  between operations  15.1 us (5%)
  blocking collectives  8.86 us (3%)
  starting transfers between devices  4.49 us (1%)
    dot_general x48, matrix products, product(): jnp.einsum(pattern, first_operand, second_operand, preferred_element_type...  66 us
    all_to_all x1, waiting for transfers between devices, local(): lax.all_to_all(outgoing.astype(jnp.bfloat16), 'seq', split_axis=0, concat...  51.3 us
    all_gather x1, waiting for transfers between devices, local(): stream_all = lax.all_gather(resp_kv[0], 'seq', axis=0, tiled=True)  50.2 us
    reduce_scatter x1, waiting for transfers between devices, local(): lax.psum_scatter(prompt_sum.astype(jnp.bfloat16), 'seq', scatter_dimensio...  29.4 us
    all_gather x1, waiting for transfers between devices, local(): prompt_all = lax.all_gather(prompt_kv[0], 'seq', axis=0, tiled=True)  13.2 us
    scatter-add x4, other arithmetic, block_step(): stream_sum.at[slot_index].add(own_term.reshape(NB, BLK, 2 * head_width))  9.24 us
    psum x1, blocking collectives, local(): count = lax.psum(jnp.sum(lengths[0]).astype(jnp.float32), 'grp')  8.86 us
    gather x4, local copies, waits for them, and re-layouts, block_step(): jnp.take(blocks, slot_index, axis=0).reshape(capacity, 2 * head_width)  8.58 us
  transfers between devices with their start and end apart: 4, of which 4 were waited for; matrix products, arithmetic and copies ran while one was open for 9% of the time, Pallas kernels for 0%

commit v1 on v0

v1 whole, which is shorter than its diff:
```python
from functools import partial

import jax
import jax.numpy as jnp
from jax import lax
from jax.experimental import pallas as pl
from jax.experimental.pallas import tpu as pltpu
from jax.sharding import PartitionSpec as P

RESP = 16
BLK = 128
NB = 2
LOSS_SCALE = 32.0
BIG_NEGATIVE = -1e30
LOG2E = 1.4426950408889634

F32 = jnp.float32
BF16 = jnp.bfloat16
NT = (((1,), (1,)), ((), ()))
TN = (((0,), (0,)), ((), ()))
NN = (((1,), (0,)), ((), ()))
TILE = 2 * BLK
VMEM = pl.BlockSpec(memory_space=pltpu.VMEM)
SMEM = pl.BlockSpec(memory_space=pltpu.SMEM)


def dot(a, b, dims):
    return lax.dot_general(a, b, dims, preferred_element_type=F32)


def call(kernel, name, out_shape, specs, args, scratch=(), flops=0, aliases=None):
    moved = sum(a.size * a.dtype.itemsize for a in args)
    return pl.pallas_call(
        kernel,
        name=name,
        out_shape=out_shape,
        in_specs=specs,
        out_specs=jax.tree.map(lambda _: VMEM, out_shape),
        scratch_shapes=list(scratch),
        input_output_aliases=aliases or {},
        compiler_params=pltpu.CompilerParams(vmem_limit_bytes=48 * 2**20),
        cost_estimate=pl.CostEstimate(flops=flops, bytes_accessed=moved, transcendentals=0),
    )(*args)


def split_kernel(count, kv_ref, *out_refs):
    me = lax.axis_index("seq")
    for k in range(count):
        for s in range(kv_ref.shape[0]):
            out_refs[k][s] = kv_ref[s, lax.bitwise_xor(me, k)]


def route_kernel(count, plan_ref, *refs):
    pieces, outs = refs[:count], refs[count : 2 * count]
    held, inverse = refs[2 * count :]
    me = lax.axis_index("seq")
    local = pieces[0].shape[0]
    for k in range(count):
        for s in range(local):
            held[lax.bitwise_xor(me, k) * local + s] = pieces[k][s]
    for j in range(plan_ref.shape[1]):
        inverse[plan_ref[0, j]] = j
    for k in range(count):
        for s in range(local):
            block = plan_ref[0, lax.bitwise_xor(me, k) * local + s]
            outs[k][s] = held[inverse[lax.bitwise_xor(block, 1)]]


def weight_kernel(groups, plan_ref, rewards_ref, grad_ref, *refs):
    lengths, out_ref = refs[:groups], refs[groups]
    me = lax.axis_index("seq")
    local = grad_ref.shape[0] // BLK
    total = jnp.int32(0)
    for ref in lengths:
        for r in range(RESP):
            total = total + ref[0, r]
    reward_sum = rewards_ref[0, 0]
    for r in range(1, RESP):
        reward_sum = reward_sum + rewards_ref[0, r]
    mean = reward_sum * (1.0 / RESP)
    count = jnp.full((BLK, 1), total.astype(F32))
    row = lax.broadcasted_iota(jnp.int32, (BLK, 1), 0)
    for s in range(local):
        block = plan_ref[0, me * local + s]
        response = lax.div(block, NB)
        first = lax.rem(block, NB) * BLK
        scaled = (rewards_ref[0, response] - mean) * (LOSS_SCALE * groups * RESP * NB * BLK)
        weight = jnp.where(row + first < lengths[0][0, response], scaled / count, 0.0)
        rows = slice(s * BLK, (s + 1) * BLK)
        out_ref[rows] = (grad_ref[rows].astype(F32) * weight).astype(BF16)


def head_tiles(q_ref):
    halves = q_ref.shape[0] // TILE
    return [
        (h * halves + r, r, slice(r * TILE, (r + 1) * TILE), slice(h * BLK, (h + 1) * BLK))
        for h in range(q_ref.shape[1] // BLK)
        for r in range(halves)
    ]


def by_block(pairs, side, rows, tile_rows):
    return jnp.concatenate(
        [
            dot(
                pairs[tile_rows * TILE + b * BLK : tile_rows * TILE + (b + 1) * BLK, side],
                rows[b * BLK : (b + 1) * BLK],
                NT,
            )
            for b in range(2)
        ],
        axis=1,
    )


KEYS = slice(0, BLK)
VALUES = slice(BLK, 2 * BLK)


def causal_mask():
    key = lax.broadcasted_iota(jnp.int32, (BLK, TILE), 0)
    row = lax.rem(lax.broadcasted_iota(jnp.int32, (BLK, TILE), 1), BLK)
    return key <= row


def odd_lanes(plan_ref, tile_rows, local):
    me = lax.axis_index("seq")
    lane = lax.broadcasted_iota(jnp.int32, (1, TILE), 1)
    odd = [lax.rem(plan_ref[0, me * local + 2 * tile_rows + b], NB) for b in range(2)]
    return jnp.where(lane < BLK, odd[0], odd[1]) > 0


def join_pieces(pieces, out_ref):
    count = len(pieces)
    me = lax.axis_index("seq")
    for k in range(count):
        for s in range(pieces[k].shape[0]):
            out_ref[s, lax.bitwise_xor(me, k)] = pieces[k][s]


def whole_blocks(held):
    local, count, rows, width = held.shape
    if rows % 16 == 0:
        return held[...].reshape(local * count * rows, width)
    return held[...].astype(F32).reshape(local * count * rows, width).astype(BF16)


def stats_kernel(scale, shards, own, parts, carried, *refs):
    refs = list(refs)
    plan_ref = refs.pop(0) if parts else None
    q_ref, w_ref = refs.pop(0), refs.pop(0)
    before = refs.pop(0) if carried else None
    kv = [refs.pop(0) for _ in range(shards)]
    own_ref = refs.pop(0) if own else None
    pieces = [refs.pop(0) for _ in range(parts)]
    out_ref = refs.pop(0)
    if parts:
        blocks_ref, held = refs
        join_pieces(pieces, held)
        blocks_ref[...] = whole_blocks(held)
    visible = causal_mask() if own else None
    for t, r, rows, cols in head_tiles(q_ref):
        q, w = q_ref[rows, cols], w_ref[rows, cols]
        if carried:
            m, l, d = before[t, 0:1], before[t, 1:2], before[t, 2:3]
        else:
            m = jnp.full((1, TILE), BIG_NEGATIVE, F32)
            l = d = jnp.zeros((1, TILE), F32)
        work = [(dot(ref[:, KEYS], q, NT), dot(ref[:, VALUES], w, NT)) for ref in kv]
        if own:
            s = by_block(own_ref, KEYS, q, r)
            work.append((jnp.where(visible, s, BIG_NEGATIVE), by_block(own_ref, VALUES, w, r)))
        if parts:
            s = by_block(blocks_ref, KEYS, q, r)
            seen = odd_lanes(plan_ref, r, q_ref.shape[0] // BLK)
            work.append((jnp.where(seen, s, BIG_NEGATIVE), by_block(blocks_ref, VALUES, w, r)))
        for s, dp in work:
            peak = jnp.maximum(m, jnp.max(s, axis=0, keepdims=True))
            shrink = jnp.exp2((m - peak) * scale)
            e = jnp.exp2(s * scale - peak * scale)
            l = l * shrink + jnp.sum(e, axis=0, keepdims=True)
            d = d * shrink + jnp.sum(e * dp, axis=0, keepdims=True)
            m = peak
        out_ref[t, 0:1] = m
        out_ref[t, 1:2] = l
        out_ref[t, 2:3] = d


def grad_kernel(scale, shards, inits, own, partner, carried, last, *refs):
    refs = list(refs)
    plan_ref = refs.pop(0) if partner else None
    q_ref, w_ref, stats_ref = refs.pop(0), refs.pop(0), refs.pop(0)
    before = refs.pop(0) if carried else None
    kv = [refs.pop(0) for _ in range(shards)]
    init = [[refs.pop(0) for _ in range(n)] for n in inits]
    own_ref = refs.pop(0) if own else None
    part_ref = refs.pop(0) if partner else None
    dq_ref = refs.pop(0)
    kv_out = [refs.pop(0) for _ in range(shards)]
    blocks_ref = own_ref if own else part_ref
    blocks_out = refs.pop(0) if own or partner else None
    kv_sum = refs.pop(0) if shards else None
    blocks_sum = refs.pop(0) if own or partner else None
    back = scale / LOG2E
    visible = causal_mask() if own else None
    per = kv[0].shape[0] if shards else 0
    if shards:
        keys = jnp.concatenate([ref[:, KEYS] for ref in kv], axis=0)
        values = jnp.concatenate([ref[:, VALUES] for ref in kv], axis=0)
    for t, r, rows, cols in head_tiles(q_ref):
        q, w = q_ref[rows, cols], w_ref[rows, cols]
        peak = stats_ref[t, 0:1] * scale
        inverse = 1.0 / stats_ref[t, 1:2]
        delta = stats_ref[t, 2:3] * inverse

        def grads(s, dp):
            p = jnp.exp2(s * scale - peak) * inverse
            return p.astype(BF16), (p * (dp - delta)).astype(BF16)

        dq = None
        if shards:
            p, ds = grads(dot(keys, q, NT), dot(values, w, NT))
            dk, dv = dot(ds, q, NN), dot(p, w, NN)
            if t == 0:
                kv_sum[:, KEYS] = dk
                kv_sum[:, VALUES] = dv
            else:
                kv_sum[:, KEYS] += dk
                kv_sum[:, VALUES] += dv
            dq = dot(ds, keys, TN)
        if own or partner:
            s = by_block(blocks_ref, KEYS, q, r)
            seen = visible if own else odd_lanes(plan_ref, r, q_ref.shape[0] // BLK)
            s = jnp.where(seen, s, BIG_NEGATIVE)
            p, ds = grads(s, by_block(blocks_ref, VALUES, w, r))
            turned = []
            for b in range(2):
                lanes = slice(b * BLK, (b + 1) * BLK)
                place = slice(r * TILE + b * BLK, r * TILE + (b + 1) * BLK)
                dk, dv = dot(ds[:, lanes], q[lanes], NN), dot(p[:, lanes], w[lanes], NN)
                if cols.start == 0:
                    blocks_sum[place, KEYS] = dk
                    blocks_sum[place, VALUES] = dv
                else:
                    blocks_sum[place, KEYS] += dk
                    blocks_sum[place, VALUES] += dv
                turned.append(dot(ds[:, lanes], blocks_ref[place, KEYS], TN))
            turned = jnp.concatenate(turned, axis=0)
            dq = turned if dq is None else dq + turned
        if carried:
            dq = dq + before[rows, cols]
        dq_ref[rows, cols] = (dq * back).astype(BF16) if last else dq
    for i in range(shards):
        place = slice(i * per, (i + 1) * per)
        for side, factor in ((KEYS, back), (VALUES, 1.0)):
            total = kv_sum[place, side] * factor
            for ref in init[i]:
                total = total + ref[:, side].astype(F32)
            kv_out[i][:, side] = total.astype(kv_out[i].dtype)
    if own or partner:
        for side, factor in ((KEYS, back), (VALUES, 1.0)):
            total = blocks_sum[:, side] * factor
            blocks_out[:, side] = total.astype(blocks_out.dtype)


def finish_kernel(count, plan_ref, own_ref, *refs):
    pieces, out_ref, held = refs[:count], refs[count], refs[count + 1]
    me = lax.axis_index("seq")
    local = own_ref.shape[0] // BLK
    join_pieces(pieces, held)
    joined = whole_blocks(held)
    for s in range(local):
        rows = slice(s * BLK, (s + 1) * BLK)
        odd = lax.rem(plan_ref[0, me * local + s], NB)
        odd_rows = jnp.full((BLK, 2 * BLK), odd, jnp.int32) > 0
        extra = jnp.where(odd_rows, 0.0, joined[rows].astype(F32))
        out_ref[rows] = (own_ref[rows] + extra).astype(BF16)


def total_kernel(*refs):
    total = refs[0][...]
    for ref in refs[1:-1]:
        total = total + ref[...].astype(F32)
    refs[-1][...] = total.astype(BF16)


def local(query, resp_kv, prompt_kv, grad_out, rewards, lengths, block_order):
    groups = lax.axis_size("grp")
    count = lax.axis_size("seq")
    q, resp, prompt, grad = query[0], resp_kv[0], prompt_kv[0], grad_out[0]
    rows, width = resp.shape
    blocks = rows // BLK
    heads = q.shape[1] // BLK
    scale = LOG2E * BLK**-0.5
    piece = jax.ShapeDtypeStruct((blocks, BLK // count, width), BF16)
    apart = pltpu.VMEM((blocks, count, BLK // count, width), BF16)

    def swap(x, axis, k):
        size = lax.axis_size(axis)
        return lax.ppermute(x, axis, [(i, i ^ k) for i in range(size)])

    def exchange(sent):
        return [sent[0]] + [swap(sent[k], "seq", k) for k in range(1, count)]

    def route(name, arrived):
        return call(
            partial(route_kernel, count),
            name,
            [piece] * count,
            [SMEM] + [VMEM] * count,
            [block_order, *arrived],
            [
                pltpu.VMEM((blocks * count, BLK // count, width), BF16),
                pltpu.SMEM((block_order.shape[1],), jnp.int32),
            ],
        )

    def split(name, x):
        return call(
            partial(split_kernel, count),
            name,
            [piece] * count,
            [VMEM],
            [x.reshape(blocks, count, BLK // count, width)],
        )

    lengths_all = [lengths] + [swap(lengths, "grp", k) for k in range(1, groups)]
    pieces = exchange(split("split_pairs", resp))
    column = {0: prompt}
    for k in range(2, count, 2):
        column[k] = swap(prompt, "seq", k)
    across = {k: swap(column[k], "seq", 1) for k in column}
    weighted = call(
        partial(weight_kernel, groups),
        "weight_rows",
        jax.ShapeDtypeStruct(grad.shape, BF16),
        [SMEM, SMEM, VMEM] + [SMEM] * groups,
        [block_order, rewards, grad, *lengths_all],
    )
    arrived = exchange(route("route_pairs", pieces))

    stats_shape = jax.ShapeDtypeStruct((heads * rows // TILE, 8, TILE), F32)
    product_flops = 2 * rows * heads * BLK

    def stats(name, before, kv, own=None, parts=()):
        args, specs = [], []
        if parts:
            args, specs = [block_order], [SMEM]
        args += [q, weighted]
        args += [before] if before is not None else []
        args += list(kv) + ([own] if own is not None else []) + list(parts)
        specs += [VMEM] * (len(args) - len(specs))
        keys = sum(x.shape[0] for x in kv) + BLK * ((own is not None) + bool(parts))
        out = stats_shape
        scratch = []
        if parts:
            out = [stats_shape, jax.ShapeDtypeStruct(resp.shape, BF16)]
            scratch = [apart]
        return call(
            partial(stats_kernel, scale, len(kv), own is not None, len(parts), before is not None),
            name,
            out,
            specs,
            args,
            scratch,
            flops=2 * keys * product_flops,
        )

    state = stats("stats_own", None, [prompt], own=resp)
    for k in range(2, count, 2):
        state = stats("stats_prompt", state, [across[k - 2], column[k]])
    state, partner = stats("stats_last", state, [across[count - 2]], parts=arrived)

    def grads(name, before, kv, init=None, own=None, part=None, last=False, kinds=None):
        init = init or [[] for _ in kv]
        args, specs = ([block_order], [SMEM]) if part is not None else ([], [])
        args += [q, weighted, state]
        args += [before] if before is not None else []
        args += list(kv) + [x for xs in init for x in xs]
        args += [own] if own is not None else []
        args += [part] if part is not None else []
        specs += [VMEM] * (len(args) - len(specs))
        out = [jax.ShapeDtypeStruct(q.shape, BF16 if last else F32)]
        out += [jax.ShapeDtypeStruct(x.shape, d) for x, d in zip(kv, kinds or [BF16] * len(kv))]
        scratch = []
        keys = sum(x.shape[0] for x in kv)
        if kv:
            scratch.append(pltpu.VMEM((keys, width), F32))
        if own is not None or part is not None:
            out.append(jax.ShapeDtypeStruct(resp.shape, F32 if own is not None else BF16))
            scratch.append(pltpu.VMEM(resp.shape, F32))
            keys += BLK
        return call(
            partial(
                grad_kernel,
                scale,
                len(kv),
                tuple(len(xs) for xs in init),
                own is not None,
                part is not None,
                before is not None,
                last,
            ),
            name,
            out,
            specs,
            args,
            scratch,
            flops=5 * keys * product_flops,
        )

    dq, partner_terms = grads("grads_partner", None, [], part=partner)
    backward = exchange(split("split_terms", partner_terms))
    even = list(range(0, count, 2))
    dq, *far = grads("grads_across", dq, [across[k] for k in even])
    far = {k: swap(x, "seq", 1) for k, x in zip(even, far)}
    dq, *mid = grads(
        "grads_column", dq, [column[k] for k in even[1:]], init=[[far[k]] for k in even[1:]]
    )
    mid = [swap(x, "seq", k) for k, x in zip(even[1:], mid)]
    returned = exchange(route("route_terms", backward))
    dq, near, own_terms = grads(
        "grads_own", dq, [prompt], init=[[far[0]]], own=resp, last=True, kinds=[F32]
    )
    grad_prompt = call(
        total_kernel,
        "sum_prompt",
        jax.ShapeDtypeStruct(prompt.shape, BF16),
        [VMEM] * (1 + len(mid)),
        [near, *mid],
    )
    grad_stream = call(
        partial(finish_kernel, count),
        "sum_stream",
        jax.ShapeDtypeStruct(resp.shape, BF16),
        [SMEM, VMEM] + [VMEM] * count,
        [block_order, own_terms, *returned],
        [apart],
    )
    return dq[None], grad_stream[None], grad_prompt[None]


def solution(mesh):
    in_specs = (
        P("grp", "seq", None),
        P("grp", "seq", None),
        P("grp", "seq", None),
        P("grp", "seq", None),
        P("grp", None),
        P("grp", None),
        P("grp", None),
    )
    out_specs = (P("grp", "seq", None), P("grp", "seq", None), P("grp", "seq", None))
    return jax.shard_map(local, mesh=mesh, in_specs=in_specs, out_specs=out_specs, check_vma=False)
```

time: 316 us -> 132 us (0.42)
  waiting for transfers between devices: 146 us -> 19.2 us
  starting transfers between devices: 4.49 us -> 70.7 us
  matrix products: 66 us -> 0 us
  Pallas kernels: 0 us -> 36.8 us
  local copies, waits for them, and re-layouts: 39.1 us -> 4.01 us
  other arithmetic: 34.5 us -> 0 us
  between operations: 15.1 us -> 0.85 us
  blocking collectives: 8.86 us -> 0 us
    ppermute x0 -> x45, starting transfers between devices: none -> 70.7 us  [swap(): return lax.ppermute(x, axis, [(i, i ^ k) for i in range(size)])]
    dot_general x48 -> x0, matrix products: 66 us -> none  [product(): jnp.einsum(pattern, first_operand, second_operand, preferred_element_type...]
    all_gather x2 -> x0, waiting for transfers between devices: 63.4 us -> none  [the longest x1 50.2 us: local(): stream_all = lax.all_gather(resp_kv[0], 'seq', axis=0, tiled=True)]
    all_to_all x1 -> x0, waiting for transfers between devices: 51.3 us -> none  [local(): lax.all_to_all(outgoing.astype(jnp.bfloat16), 'seq', split_axis=0, concat...]
    pallas_call x0 -> x16, Pallas kernels: none -> 36.8 us  [call(): pl.pallas_call(kernel, name=name, out_shape=out_shape, in_specs=specs, ou...]
    reduce_scatter x1 -> x0, waiting for transfers between devices: 29.4 us -> none  [local(): lax.psum_scatter(prompt_sum.astype(jnp.bfloat16), 'seq', scatter_dimensio...]
    ppermute x0 -> x45, waiting for transfers between devices: none -> 19.2 us  [swap(): return lax.ppermute(x, axis, [(i, i ^ k) for i in range(size)])]
    gather x8 -> x0, local copies, waits for them, and re-layouts: 12.4 us -> none  [the longest x4 8.58 us: block_step(): jnp.take(blocks, slot_index, axis=0).reshape(capacity, 2 * head_width)]
  transfers between devices with their start and end apart: 4 -> 45, of which waited for: 4 -> 11; matrix products, arithmetic and copies ran while one was open for 9% -> 0% of each run, Pallas kernels for 0% -> 23%
where the time goes in v1:
time: 132 us
  starting transfers between devices  70.7 us (54%)
  Pallas kernels  36.8 us (28%)
  waiting for transfers between devices  19.2 us (15%)
  local copies, waits for them, and re-layouts  4.01 us (3%)
    ppermute x45, starting transfers between devices, swap(): return lax.ppermute(x, axis, [(i, i ^ k) for i in range(size)])  70.7 us
    pallas_call x16, Pallas kernels, call(): pl.pallas_call(kernel, name=name, out_shape=out_shape, in_specs=specs, ou...  36.8 us
    ppermute x45, waiting for transfers between devices, swap(): return lax.ppermute(x, axis, [(i, i ^ k) for i in range(size)])  19.2 us
    unnamed x16, local copies, waits for them, and re-layouts  4.01 us
  transfers between devices with their start and end apart: 45, of which 11 were waited for; matrix products, arithmetic and copies ran while one was open for 0% of the time, Pallas kernels for 23%

profile of v1, /device:TPU:0, one launch (start us, length us, event | category | flops | bytes accessed | tf_op | source)
XLA Modules:
  0.0 131.6 jit_solution(10997103154825560094)
XLA Ops:
  0.6 3.1 %collective-permute-start.4 = (bf16[256,256]{1,0:T(8,128)(2,1)}, bf16[256,256]{1,0:T(8,128)(2,1)S(1)}, u32[]{:S(2)}, u32[]{:S(2)}) collective-permute-start(bf16[256,256]{1,0:T(8,128)(2,1)} %bitcast.23), channel_id=1, source_target_pairs={{0,2},{1,3},{2,0},{3,1},{4,6},{5,7},{6,4},{7,5},{8,10},{9,11},{10,... | collective-permute-start | bytes 393224 | tf_op jit(solution)/shard_map/ppermute | solution.py:300
  3.7 0.9 copy-done.2
  4.7 1.6 %collective-permute-start.10 = (bf16[4,16,256]{2,1,0:T(8,128)(2,1)S(1)}, bf16[4,16,256]{2,1,0:T(8,128)(2,1)S(1)}, u32[]{:S(2)}, u32[]{:S(2)}) collective-permute-start(bf16[4,16,256]{2,1,0:T(8,128)(2,1)S(1)} %get-tuple-element.52), channel_id=1, source_target_pairs={{0,1},{1,0},{2,3},{3,2},{4,5},{5,4},{6,7},{7,6},{8,9},{9,8},{10,11... | collective-permute-start | bytes 98312 | tf_op jit(solution)/shard_map/ppermute | solution.py:300
  6.3 2.6 %collective-permute-start.6 = (bf16[256,256]{1,0:T(8,128)(2,1)}, bf16[256,256]{1,0:T(8,128)(2,1)S(1)}, u32[]{:S(2)}, u32[]{:S(2)}) collective-permute-start(bf16[256,256]{1,0:T(8,128)(2,1)} %bitcast.24), channel_id=1, source_target_pairs={{0,4},{1,5},{2,6},{3,7},{4,0},{5,1},{6,2},{7,3},{8,12},{9,13},{10,... | collective-permute-start | bytes 393224 | tf_op jit(solution)/shard_map/ppermute | solution.py:300
  8.8 1.5 %collective-permute-start.1 = (s32[1,16]{1,0:T(1,128)}, s32[1,16]{1,0:T(1,128)S(1)}, u32[]{:S(2)}, u32[]{:S(2)}) collective-permute-start(s32[1,16]{1,0:T(1,128)} %refs_0_.3), channel_id=1, source_target_pairs={{0,16},{8,24},{16,0},{24,8},{1,17},{9,25},{17,1},{25,9},{2,18},{10... | collective-permute-start | bytes 200 | tf_op jit(solution)/shard_map/ppermute | solution.py:300
  10.4 2.2 %collective-permute-done.1.refs_2_ = s32[1,16]{1,0:T(1,128)S(1)} collective-permute-done((s32[1,16]{1,0:T(1,128)}, s32[1,16]{1,0:T(1,128)S(1)}, u32[]{:S(2)}, u32[]{:S(2)}) %collective-permute-start.1) | collective-permute-done | bytes 96 | tf_op jit(solution)/shard_map/ppermute | solution.py:300
  12.5 0.5 collective-permute-start.11
  13.0 2.6 %collective-permute-done.2.refs_3_ = s32[1,16]{1,0:T(1,128)S(1)} collective-permute-done((s32[1,16]{1,0:T(1,128)}, s32[1,16]{1,0:T(1,128)S(1)}, u32[]{:S(2)}, u32[]{:S(2)}) %collective-permute-start.2) | collective-permute-done | bytes 96 | tf_op jit(solution)/shard_map/ppermute | solution.py:300
  15.6 0.4 collective-permute-start.12
  16.1 0.4 collective-permute-done.11.refs_2_
  16.4 3.5 %collective-permute-start.8 = (bf16[256,256]{1,0:T(8,128)(2,1)}, bf16[256,256]{1,0:T(8,128)(2,1)S(1)}, u32[]{:S(2)}, u32[]{:S(2)}) collective-permute-start(bf16[256,256]{1,0:T(8,128)(2,1)} %bitcast.25), channel_id=1, source_target_pairs={{0,6},{1,7},{2,4},{3,5},{4,2},{5,3},{6,0},{7,1},{8,14},{9,15},{10,... | collective-permute-start | bytes 393224 | tf_op jit(solution)/shard_map/ppermute | solution.py:300
  20.0 0.8 collective-permute-done.12.refs_3_
  20.8 0.7 collective-permute-start.3
  21.5 3.7 %collective-permute-start.14 = (bf16[4,16,256]{2,1,0:T(8,128)(2,1)S(1)}, bf16[4,16,256]{2,1,0:T(8,128)(2,1)S(1)}, u32[]{:S(2)}, u32[]{:S(2)}) collective-permute-start(bf16[4,16,256]{2,1,0:T(8,128)(2,1)S(1)} %get-tuple-element.56), channel_id=1, source_target_pairs={{0,5},{1,4},{2,7},{3,6},{4,1},{5,0},{6,3},{7,2},{8,13},{9,12},{10,... | collective-permute-start | bytes 98312 | tf_op jit(solution)/shard_map/ppermute | solution.py:300
  25.2 3.4 %collective-permute-done.14.refs_5_ = bf16[4,16,256]{2,1,0:T(8,128)(2,1)S(1)} collective-permute-done((bf16[4,16,256]{2,1,0:T(8,128)(2,1)S(1)}, bf16[4,16,256]{2,1,0:T(8,128)(2,1)S(1)}, u32[]{:S(2)}, u32[]{:S(2)}) %collective-permute-start.14) | collective-permute-done | bytes 32800 | tf_op jit(solution)/shard_map/ppermute | solution.py:300
  28.6 1.5 %collective-permute-start.15 = (bf16[4,16,256]{2,1,0:T(8,128)(2,1)S(1)}, bf16[4,16,256]{2,1,0:T(8,128)(2,1)S(1)}, u32[]{:S(2)}, u32[]{:S(2)}) collective-permute-start(bf16[4,16,256]{2,1,0:T(8,128)(2,1)S(1)} %get-tuple-element.57), channel_id=1, source_target_pairs={{0,6},{1,7},{2,4},{3,5},{4,2},{5,3},{6,0},{7,1},{8,14},{9,15},{10,... | collective-permute-start | bytes 98312 | tf_op jit(solution)/shard_map/ppermute | solution.py:300
  30.1 2.1 %collective-permute-start.5 = (bf16[256,256]{1,0:T(8,128)(2,1)S(1)}, bf16[256,256]{1,0:T(8,128)(2,1)S(1)}, u32[]{:S(2)}, u32[]{:S(2)}) collective-permute-start(bf16[256,256]{1,0:T(8,128)(2,1)S(1)} %collective-permute-done.4.refs_4_), channel_id=1, source_target_pairs={{0,1},{1,0},{2,3},{3,2},{4,5},{5,4},{6,7},{7,6},{8,9},{9,8},{10,11... | collective-permute-start | bytes 393224 | tf_op jit(solution)/shard_map/ppermute | solution.py:300
  32.1 1.1 copy-done.1
  33.2 0.7 copy-done.4
  33.9 0.7 copy-done.5
  34.5 0.7 copy-done.6
  35.2 0.8 weight_rows.1.refs_1_.refs_2_
  36.0 3.3 %collective-permute-start.16 = (bf16[4,16,256]{2,1,0:T(8,128)(2,1)S(1)}, bf16[4,16,256]{2,1,0:T(8,128)(2,1)S(1)}, u32[]{:S(2)}, u32[]{:S(2)}) collective-permute-start(bf16[4,16,256]{2,1,0:T(8,128)(2,1)S(1)} %get-tuple-element.58), channel_id=1, source_target_pairs={{0,7},{1,6},{2,5},{3,4},{4,3},{5,2},{6,1},{7,0},{8,15},{9,14},{10,... | collective-permute-start | bytes 98312 | tf_op jit(solution)/shard_map/ppermute | solution.py:300
  39.3 2.0 %collective-permute-start.7 = (bf16[256,256]{1,0:T(8,128)(2,1)S(1)}, bf16[256,256]{1,0:T(8,128)(2,1)S(1)}, u32[]{:S(2)}, u32[]{:S(2)}) collective-permute-start(bf16[256,256]{1,0:T(8,128)(2,1)S(1)} %collective-permute-done.6.refs_4_.refs_5_), channel_id=1, source_target_pairs={{0,1},{1,0},{2,3},{3,2},{4,5},{5,4},{6,7},{7,6},{8,9},{9,8},{10,11... | collective-permute-start | bytes 393224 | tf_op jit(solution)/shard_map/ppermute | solution.py:300
  41.4 2.1 %stats_own.1.refs_2_ = f32[10,8,256]{2,1,0:T(8,128)S(1)} custom-call(bf16[512,640]{1,0:T(8,128)(2,1)S(1)} %bitcast.9, bf16[512,640]{1,0:T(8,128)(2,1)S(1)} %weight_rows.1.refs_1_.refs_2_, bf16[256,256]{1,0:T(8,128)(2,1)S(1)} %bitcast.27, bf16[512,256]{1,0:T(8,128)(2,1)S(1)} %bitcast.20), custom_call_target="tpu_custom_call" | custom-call | flops 503316480 | bytes 1703936 | tf_op jit(solution)/shard_map/stats_own/pallas_call | solution.py:33
  43.5 0.7 route_pairs.1
  44.2 1.1 collective-permute-start.17
  45.3 1.0 collective-permute-start.9
  46.3 1.8 %stats_prompt.3.refs_2_ = f32[10,8,256]{2,1,0:T(8,128)S(1)} custom-call(bf16[512,640]{1,0:T(8,128)(2,1)S(1)} %bitcast.10, bf16[512,640]{1,0:T(8,128)(2,1)S(1)} %weight_rows.1.refs_1_.refs_2_, f32[10,8,256]{2,1,0:T(8,128)S(1)} %stats_own.1.refs_2_, bf16[256,256]{1,0:T(8,128)(2,1)S(1)} %collective-permute-done.3.refs_3_.refs_4_, ...), custom_call_target="tpu_custom_call" | custom-call | flops 671088640 | bytes 1654784 | tf_op jit(solution)/shard_map/stats_prompt/pallas_call | solution.py:33
  48.2 2.5 %collective-permute-start.19 = (bf16[4,16,256]{2,1,0:T(8,128)(2,1)S(1)}, bf16[4,16,256]{2,1,0:T(8,128)(2,1)S(1)}, u32[]{:S(2)}, u32[]{:S(2)}) collective-permute-start(bf16[4,16,256]{2,1,0:T(8,128)(2,1)S(1)} %get-tuple-element.62), channel_id=1, source_target_pairs={{0,3},{1,2},{2,1},{3,0},{4,7},{5,6},{6,5},{7,4},{8,11},{9,10},{10,... | collective-permute-start | bytes 98312 | tf_op jit(solution)/shard_map/ppermute | solution.py:300
  50.7 1.8 %stats_prompt.4.refs_2_ = f32[10,8,256]{2,1,0:T(8,128)S(1)} custom-call(bf16[512,640]{1,0:T(8,128)(2,1)S(1)} %bitcast.11, bf16[512,640]{1,0:T(8,128)(2,1)S(1)} %weight_rows.1.refs_1_.refs_2_, f32[10,8,256]{2,1,0:T(8,128)S(1)} %stats_prompt.3.refs_2_, bf16[256,256]{1,0:T(8,128)(2,1)S(1)} %collective-permute-done.5.refs_3_.refs_5_, ...), custom_call_target="tpu_custom_call" | custom-call | flops 671088640 | bytes 1654784 | tf_op jit(solution)/shard_map/stats_prompt/pallas_call | solution.py:33
  52.5 1.2 collective-permute-start.20
  53.7 2.2 %collective-permute-start.21 = (bf16[4,16,256]{2,1,0:T(8,128)(2,1)S(1)}, bf16[4,16,256]{2,1,0:T(8,128)(2,1)S(1)}, u32[]{:S(2)}, u32[]{:S(2)}) collective-permute-start(bf16[4,16,256]{2,1,0:T(8,128)(2,1)S(1)} %get-tuple-element.64), channel_id=1, source_target_pairs={{0,5},{1,4},{2,7},{3,6},{4,1},{5,0},{6,3},{7,2},{8,13},{9,12},{10,... | collective-permute-start | bytes 98312 | tf_op jit(solution)/shard_map/ppermute | solution.py:300
  55.9 3.1 %collective-permute-start.22 = (bf16[4,16,256]{2,1,0:T(8,128)(2,1)S(1)}, bf16[4,16,256]{2,1,0:T(8,128)(2,1)S(1)}, u32[]{:S(2)}, u32[]{:S(2)}) collective-permute-start(bf16[4,16,256]{2,1,0:T(8,128)(2,1)S(1)} %get-tuple-element.65), channel_id=1, source_target_pairs={{0,6},{1,7},{2,4},{3,5},{4,2},{5,3},{6,0},{7,1},{8,14},{9,15},{10,... | collective-permute-start | bytes 98312 | tf_op jit(solution)/shard_map/ppermute | solution.py:300
  59.0 1.3 collective-permute-start.23
  60.2 1.8 %stats_prompt.5.refs_3_ = f32[10,8,256]{2,1,0:T(8,128)S(1)} custom-call(bf16[512,640]{1,0:T(8,128)(2,1)S(1)} %bitcast.12, bf16[512,640]{1,0:T(8,128)(2,1)S(1)} %weight_rows.1.refs_1_.refs_2_, f32[10,8,256]{2,1,0:T(8,128)S(1)} %stats_prompt.4.refs_2_, bf16[256,256]{1,0:T(8,128)(2,1)S(1)} %collective-permute-done.7.refs_3_.refs_6_, ...), custom_call_target="tpu_custom_call" | custom-call | flops 671088640 | bytes 1654784 | tf_op jit(solution)/shard_map/stats_prompt/pallas_call | solution.py:33
  62.1 3.5 %collective-permute-done.23.refs_12_ = bf16[4,16,256]{2,1,0:T(8,128)(2,1)S(1)} collective-permute-done((bf16[4,16,256]{2,1,0:T(8,128)(2,1)S(1)}, bf16[4,16,256]{2,1,0:T(8,128)(2,1)S(1)}, u32[]{:S(2)}, u32[]{:S(2)}) %collective-permute-start.23) | collective-permute-done | bytes 32800 | tf_op jit(solution)/shard_map/ppermute | solution.py:300
  65.6 2.6 %stats_last.1 = (f32[10,8,256]{2,1,0:T(8,128)S(1)}, bf16[512,256]{1,0:T(8,128)(2,1)S(1)}) custom-call(s32[1,32]{1,0:T(1,128)S(1)} %copy-done.4, bf16[512,640]{1,0:T(8,128)(2,1)S(1)} %bitcast.13, bf16[512,640]{1,0:T(8,128)(2,1)S(1)} %weight_rows.1.refs_1_.refs_2_, f32[10,8,256]{2,1,0:T(8,128)S(1)} %stats_prompt.5.refs_3_, ...), custom_call_target="tpu_custom_call" | custom-call | flops 503316480 | bytes 1785984 | tf_op jit(solution)/shard_map/stats_last/pallas_call | solution.py:33
  68.2 3.6 %grads_partner.1 = (f32[512,640]{1,0:T(8,128)S(1)}, bf16[512,256]{1,0:T(8,128)(2,1)S(1)}) custom-call(s32[1,32]{1,0:T(1,128)S(1)} %copy-done.4, bf16[512,640]{1,0:T(8,128)(2,1)S(1)} %bitcast.14, bf16[512,640]{1,0:T(8,128)(2,1)S(1)} %weight_rows.1.refs_1_.refs_2_, f32[10,8,256]{2,1,0:T(8,128)S(1)} %get-tuple-element.67.refs_3_.refs_2_, ...), custom_call_target="tpu_custom_call" | custom-call | flops 419430400 | bytes 1654912 | tf_op jit(solution)/shard_map/grads_partner/pallas_call | solution.py:33
  71.9 0.3 collective-permute-start.28
  72.2 3.3 %collective-permute-start.30 = (bf16[4,16,256]{2,1,0:T(8,128)(2,1)S(1)}, bf16[4,16,256]{2,1,0:T(8,128)(2,1)S(1)}, u32[]{:S(2)}, u32[]{:S(2)}) collective-permute-start(bf16[4,16,256]{2,1,0:T(8,128)(2,1)S(1)} %get-tuple-element.82), channel_id=1, source_target_pairs={{0,3},{1,2},{2,1},{3,0},{4,7},{5,6},{6,5},{7,4},{8,11},{9,10},{10,... | collective-permute-start | bytes 98312 | tf_op jit(solution)/shard_map/ppermute | solution.py:300
  75.5 7.0 %grads_across.1 = (f32[512,640]{1,0:T(8,128)S(1)}, bf16[256,256]{1,0:T(8,128)(2,1)S(1)}, bf16[256,256]{1,0:T(8,128)(2,1)S(1)}, bf16[256,256]{1,0:T(8,128)(2,1)S(1)}, bf16[256,256]{1,0:T(8,128)(2,1)S(1)}) custom-call(bf16[512,640]{1,0:T(8,128)(2,1)S(1)} %bitcast.15, bf16[512,640]{1,0:T(8,128)(2,1)S(1)} %weight_rows.1.refs_1_.refs_2_, ...), custom_call_target="tpu_custom_call" | custom-call | flops 3355443200 | bytes 3227648 | tf_op jit(solution)/shard_map/grads_across/pallas_call | solution.py:33
  82.8 1.8 %collective-permute-start.25 = (bf16[256,256]{1,0:T(8,128)(2,1)S(1)}, bf16[256,256]{1,0:T(8,128)(2,1)S(1)}, u32[]{:S(2)}, u32[]{:S(2)}) collective-permute-start(bf16[256,256]{1,0:T(8,128)(2,1)S(1)} %get-tuple-element.72), channel_id=1, source_target_pairs={{0,1},{1,0},{2,3},{3,2},{4,5},{5,4},{6,7},{7,6},{8,9},{9,8},{10,11... | collective-permute-start | bytes 393224 | tf_op jit(solution)/shard_map/ppermute | solution.py:300
  84.9 4.1 %collective-permute-start.32 = (bf16[4,16,256]{2,1,0:T(8,128)(2,1)S(1)}, bf16[4,16,256]{2,1,0:T(8,128)(2,1)S(1)}, u32[]{:S(2)}, u32[]{:S(2)}) collective-permute-start(bf16[4,16,256]{2,1,0:T(8,128)(2,1)S(1)} %get-tuple-element.84), channel_id=1, source_target_pairs={{0,5},{1,4},{2,7},{3,6},{4,1},{5,0},{6,3},{7,2},{8,13},{9,12},{10,... | collective-permute-start | bytes 98312 | tf_op jit(solution)/shard_map/ppermute | solution.py:300
  89.0 0.8 collective-permute-done.31.refs_4_
  89.8 1.4 %collective-permute-start.33 = (bf16[4,16,256]{2,1,0:T(8,128)(2,1)S(1)}, bf16[4,16,256]{2,1,0:T(8,128)(2,1)S(1)}, u32[]{:S(2)}, u32[]{:S(2)}) collective-permute-start(bf16[4,16,256]{2,1,0:T(8,128)(2,1)S(1)} %get-tuple-element.85), channel_id=1, source_target_pairs={{0,6},{1,7},{2,4},{3,5},{4,2},{5,3},{6,0},{7,1},{8,14},{9,15},{10,... | collective-permute-start | bytes 98312 | tf_op jit(solution)/shard_map/ppermute | solution.py:300
  91.3 3.4 %collective-permute-start.34 = (bf16[4,16,256]{2,1,0:T(8,128)(2,1)S(1)}, bf16[4,16,256]{2,1,0:T(8,128)(2,1)S(1)}, u32[]{:S(2)}, u32[]{:S(2)}) collective-permute-start(bf16[4,16,256]{2,1,0:T(8,128)(2,1)S(1)} %get-tuple-element.86), channel_id=1, source_target_pairs={{0,7},{1,6},{2,5},{3,4},{4,3},{5,2},{6,1},{7,0},{8,15},{9,14},{10,... | collective-permute-start | bytes 98312 | tf_op jit(solution)/shard_map/ppermute | solution.py:300
  94.7 1.0 collective-permute-done.33.refs_6_
  95.7 2.4 %collective-permute-done.34.refs_7_ = bf16[4,16,256]{2,1,0:T(8,128)(2,1)S(1)} collective-permute-done((bf16[4,16,256]{2,1,0:T(8,128)(2,1)S(1)}, bf16[4,16,256]{2,1,0:T(8,128)(2,1)S(1)}, u32[]{:S(2)}, u32[]{:S(2)}) %collective-permute-start.34) | collective-permute-done | bytes 32800 | tf_op jit(solution)/shard_map/ppermute | solution.py:300
  98.1 0.6 route_terms.1
  98.7 1.4 %collective-permute-start.35 = (bf16[4,16,256]{2,1,0:T(8,128)(2,1)S(1)}, bf16[4,16,256]{2,1,0:T(8,128)(2,1)S(1)}, u32[]{:S(2)}, u32[]{:S(2)}) collective-permute-start(bf16[4,16,256]{2,1,0:T(8,128)(2,1)S(1)} %get-tuple-element.88), channel_id=1, source_target_pairs={{0,1},{1,0},{2,3},{3,2},{4,5},{5,4},{6,7},{7,6},{8,9},{9,8},{10,11... | collective-permute-start | bytes 98312 | tf_op jit(solution)/shard_map/ppermute | solution.py:300
  100.1 0.7 collective-permute-start.27
  100.8 1.9 %collective-permute-done.35.refs_1_ = bf16[4,16,256]{2,1,0:T(8,128)(2,1)S(1)} collective-permute-done((bf16[4,16,256]{2,1,0:T(8,128)(2,1)S(1)}, bf16[4,16,256]{2,1,0:T(8,128)(2,1)S(1)}, u32[]{:S(2)}, u32[]{:S(2)}) %collective-permute-start.35) | collective-permute-done | bytes 32800 | tf_op jit(solution)/shard_map/ppermute | solution.py:300
  102.7 2.8 %collective-permute-start.37 = (bf16[4,16,256]{2,1,0:T(8,128)(2,1)S(1)}, bf16[4,16,256]{2,1,0:T(8,128)(2,1)S(1)}, u32[]{:S(2)}, u32[]{:S(2)}) collective-permute-start(bf16[4,16,256]{2,1,0:T(8,128)(2,1)S(1)} %get-tuple-element.90), channel_id=1, source_target_pairs={{0,3},{1,2},{2,1},{3,0},{4,7},{5,6},{6,5},{7,4},{8,11},{9,10},{10,... | collective-permute-start | bytes 98312 | tf_op jit(solution)/shard_map/ppermute | solution.py:300
  105.5 1.0 collective-permute-start.38
  106.5 2.1 %collective-permute-start.39 = (bf16[4,16,256]{2,1,0:T(8,128)(2,1)S(1)}, bf16[4,16,256]{2,1,0:T(8,128)(2,1)S(1)}, u32[]{:S(2)}, u32[]{:S(2)}) collective-permute-start(bf16[4,16,256]{2,1,0:T(8,128)(2,1)S(1)} %get-tuple-element.92), channel_id=1, source_target_pairs={{0,5},{1,4},{2,7},{3,6},{4,1},{5,0},{6,3},{7,2},{8,13},{9,12},{10,... | collective-permute-start | bytes 98312 | tf_op jit(solution)/shard_map/ppermute | solution.py:300
  108.6 5.5 %grads_column.1 = (f32[512,640]{1,0:T(8,128)S(1)}, bf16[256,256]{1,0:T(8,128)(2,1)S(1)}, bf16[256,256]{1,0:T(8,128)(2,1)S(1)}, bf16[256,256]{1,0:T(8,128)(2,1)S(1)}) custom-call(bf16[512,640]{1,0:T(8,128)(2,1)S(1)} %bitcast.16, bf16[512,640]{1,0:T(8,128)(2,1)S(1)} %weight_rows.1.refs_1_.refs_2_, f32[10,8,256]{2,1,0:T(8,128)S(1)} %get-tuple-element.67.refs_3_.refs_2_, ...), custom_call_target="tpu_custom_call" | custom-call | flops 2516582400 | bytes 3489792 | tf_op jit(solution)/shard_map/grads_column/pallas_call | solution.py:33
  114.2 2.7 %collective-permute-start.43 = (bf16[256,256]{1,0:T(8,128)(2,1)S(1)}, bf16[256,256]{1,0:T(8,128)(2,1)S(1)}, u32[]{:S(2)}, u32[]{:S(2)}) collective-permute-start(bf16[256,256]{1,0:T(8,128)(2,1)S(1)} %get-tuple-element.97), channel_id=1, source_target_pairs={{0,4},{1,5},{2,6},{3,7},{4,0},{5,1},{6,2},{7,3},{8,12},{9,13},{10,... | collective-permute-start | bytes 393224 | tf_op jit(solution)/shard_map/ppermute | solution.py:300
  116.9 1.7 %collective-permute-start.44 = (bf16[256,256]{1,0:T(8,128)(2,1)S(1)}, bf16[256,256]{1,0:T(8,128)(2,1)S(1)}, u32[]{:S(2)}, u32[]{:S(2)}) collective-permute-start(bf16[256,256]{1,0:T(8,128)(2,1)S(1)} %get-tuple-element.98), channel_id=1, source_target_pairs={{0,6},{1,7},{2,4},{3,5},{4,2},{5,3},{6,0},{7,1},{8,14},{9,15},{10,... | collective-permute-start | bytes 393224 | tf_op jit(solution)/shard_map/ppermute | solution.py:300
  118.6 2.1 %collective-permute-start.40 = (bf16[4,16,256]{2,1,0:T(8,128)(2,1)S(1)}, bf16[4,16,256]{2,1,0:T(8,128)(2,1)S(1)}, u32[]{:S(2)}, u32[]{:S(2)}) collective-permute-start(bf16[4,16,256]{2,1,0:T(8,128)(2,1)S(1)} %get-tuple-element.93), channel_id=1, source_target_pairs={{0,6},{1,7},{2,4},{3,5},{4,2},{5,3},{6,0},{7,1},{8,14},{9,15},{10,... | collective-permute-start | bytes 98312 | tf_op jit(solution)/shard_map/ppermute | solution.py:300
  120.7 2.5 %collective-permute-start.41 = (bf16[4,16,256]{2,1,0:T(8,128)(2,1)S(1)}, bf16[4,16,256]{2,1,0:T(8,128)(2,1)S(1)}, u32[]{:S(2)}, u32[]{:S(2)}) collective-permute-start(bf16[4,16,256]{2,1,0:T(8,128)(2,1)S(1)} %get-tuple-element.94), channel_id=1, source_target_pairs={{0,7},{1,6},{2,5},{3,4},{4,3},{5,2},{6,1},{7,0},{8,15},{9,14},{10,... | collective-permute-start | bytes 98312 | tf_op jit(solution)/shard_map/ppermute | solution.py:300
  123.2 6.3 %grads_own.1 = (bf16[512,640]{1,0:T(8,128)(2,1)}, f32[256,256]{1,0:T(8,128)S(1)}, f32[512,256]{1,0:T(8,128)S(1)}) custom-call(bf16[512,640]{1,0:T(8,128)(2,1)S(1)} %bitcast.17, bf16[512,640]{1,0:T(8,128)(2,1)S(1)} %weight_rows.1.refs_1_.refs_2_, f32[10,8,256]{2,1,0:T(8,128)S(1)} %get-tuple-element.67.refs_3_.refs_2_, ...), custom_call_target="tpu_custom_call" | custom-call | flops 1258291200 | bytes 3227648 | tf_op jit(solution)/shard_map/grads_own/pallas_call | solution.py:33
  129.5 1.3 %sum_stream.1 = bf16[512,256]{1,0:T(8,128)(2,1)} custom-call(s32[1,32]{1,0:T(1,128)S(1)} %copy-done.4, f32[512,256]{1,0:T(8,128)S(1)} %get-tuple-element.77.own_ref, bf16[4,16,256]{2,1,0:T(8,128)(2,1)S(1)} %get-tuple-element.87.refs_0_, bf16[4,16,256]{2,1,0:T(8,128)(2,1)S(1)} %collective-permute-done.35.refs_1_, ...), custom_call_target="tpu_custom_call" | custom-call | bytes 786560 | tf_op jit(solution)/shard_map/sum_stream/pallas_call | solution.py:33
  130.9 0.7 sum_prompt.1
  (58 shorter events, 1.0 us)
Async XLA Ops:
  0.6 40.7 %copy-start = (bf16[1,512,640]{2,1,0:T(8,128)(2,1)S(1)}, bf16[1,512,640]{2,1,0:T(8,128)(2,1)}, u32[]{:S(2)}) copy-start(bf16[1,512,640]{2,1,0:T(8,128)(2,1)} %param.7) | copy-start | bytes 1966084
  0.6 29.4 %collective-permute-start.4 = (bf16[256,256]{1,0:T(8,128)(2,1)}, bf16[256,256]{1,0:T(8,128)(2,1)S(1)}, u32[]{:S(2)}, u32[]{:S(2)}) collective-permute-start(bf16[256,256]{1,0:T(8,128)(2,1)} %bitcast.23), channel_id=1, source_target_pairs={{0,2},{1,3},{2,0},{3,1},{4,6},{5,7},{6,4},{7,5},{8,10},{9,11},{10,... | collective-permute-start | bytes 393224 | tf_op jit(solution)/shard_map/ppermute | solution.py:300
  3.7 0.9 copy-start.2
  4.7 11.3 %collective-permute-start.10 = (bf16[4,16,256]{2,1,0:T(8,128)(2,1)S(1)}, bf16[4,16,256]{2,1,0:T(8,128)(2,1)S(1)}, u32[]{:S(2)}, u32[]{:S(2)}) collective-permute-start(bf16[4,16,256]{2,1,0:T(8,128)(2,1)S(1)} %get-tuple-element.52), channel_id=1, source_target_pairs={{0,1},{1,0},{2,3},{3,2},{4,5},{5,4},{6,7},{7,6},{8,9},{9,8},{10,11... | collective-permute-start | bytes 98312 | tf_op jit(solution)/shard_map/ppermute | solution.py:300
  6.3 33.1 %collective-permute-start.6 = (bf16[256,256]{1,0:T(8,128)(2,1)}, bf16[256,256]{1,0:T(8,128)(2,1)S(1)}, u32[]{:S(2)}, u32[]{:S(2)}) collective-permute-start(bf16[256,256]{1,0:T(8,128)(2,1)} %bitcast.24), channel_id=1, source_target_pairs={{0,4},{1,5},{2,6},{3,7},{4,0},{5,1},{6,2},{7,3},{8,12},{9,13},{10,... | collective-permute-start | bytes 393224 | tf_op jit(solution)/shard_map/ppermute | solution.py:300
  8.8 3.7 %collective-permute-start.1 = (s32[1,16]{1,0:T(1,128)}, s32[1,16]{1,0:T(1,128)S(1)}, u32[]{:S(2)}, u32[]{:S(2)}) collective-permute-start(s32[1,16]{1,0:T(1,128)} %refs_0_.3), channel_id=1, source_target_pairs={{0,16},{8,24},{16,0},{24,8},{1,17},{9,25},{17,1},{25,9},{2,18},{10... | collective-permute-start | bytes 200 | tf_op jit(solution)/shard_map/ppermute | solution.py:300
  10.4 2.2 %collective-permute-start = (s32[1,16]{1,0:T(1,128)}, s32[1,16]{1,0:T(1,128)S(1)}, u32[]{:S(2)}, u32[]{:S(2)}) collective-permute-start(s32[1,16]{1,0:T(1,128)} %refs_0_.3), channel_id=1, source_target_pairs={{0,8},{8,0},{16,24},{24,16},{1,9},{9,1},{17,25},{25,17},{2,10},{10... | collective-permute-start | bytes 200 | tf_op jit(solution)/shard_map/ppermute | solution.py:300
  12.5 3.1 %collective-permute-start.2 = (s32[1,16]{1,0:T(1,128)}, s32[1,16]{1,0:T(1,128)S(1)}, u32[]{:S(2)}, u32[]{:S(2)}) collective-permute-start(s32[1,16]{1,0:T(1,128)} %refs_0_.3), channel_id=1, source_target_pairs={{0,24},{8,16},{16,8},{24,0},{1,25},{9,17},{17,9},{25,1},{2,26},{10... | collective-permute-start | bytes 200 | tf_op jit(solution)/shard_map/ppermute | solution.py:300
  12.5 3.9 %collective-permute-start.11 = (bf16[4,16,256]{2,1,0:T(8,128)(2,1)S(1)}, bf16[4,16,256]{2,1,0:T(8,128)(2,1)S(1)}, u32[]{:S(2)}, u32[]{:S(2)}) collective-permute-start(bf16[4,16,256]{2,1,0:T(8,128)(2,1)S(1)} %get-tuple-element.53), channel_id=1, source_target_pairs={{0,2},{1,3},{2,0},{3,1},{4,6},{5,7},{6,4},{7,5},{8,10},{9,11},{10,... | collective-permute-start | bytes 98312 | tf_op jit(solution)/shard_map/ppermute | solution.py:300
  15.6 5.2 %collective-permute-start.12 = (bf16[4,16,256]{2,1,0:T(8,128)(2,1)S(1)}, bf16[4,16,256]{2,1,0:T(8,128)(2,1)S(1)}, u32[]{:S(2)}, u32[]{:S(2)}) collective-permute-start(bf16[4,16,256]{2,1,0:T(8,128)(2,1)S(1)} %get-tuple-element.54), channel_id=1, source_target_pairs={{0,3},{1,2},{2,1},{3,0},{4,7},{5,6},{6,5},{7,4},{8,11},{9,10},{10,... | collective-permute-start | bytes 98312 | tf_op jit(solution)/shard_map/ppermute | solution.py:300
  16.0 5.4 %collective-permute-start.13 = (bf16[4,16,256]{2,1,0:T(8,128)(2,1)S(1)}, bf16[4,16,256]{2,1,0:T(8,128)(2,1)S(1)}, u32[]{:S(2)}, u32[]{:S(2)}) collective-permute-start(bf16[4,16,256]{2,1,0:T(8,128)(2,1)S(1)} %get-tuple-element.55), channel_id=1, source_target_pairs={{0,4},{1,5},{2,6},{3,7},{4,0},{5,1},{6,2},{7,3},{8,12},{9,13},{10,... | collective-permute-start | bytes 98312 | tf_op jit(solution)/shard_map/ppermute | solution.py:300
  16.4 28.9 %collective-permute-start.8 = (bf16[256,256]{1,0:T(8,128)(2,1)}, bf16[256,256]{1,0:T(8,128)(2,1)S(1)}, u32[]{:S(2)}, u32[]{:S(2)}) collective-permute-start(bf16[256,256]{1,0:T(8,128)(2,1)} %bitcast.25), channel_id=1, source_target_pairs={{0,6},{1,7},{2,4},{3,5},{4,2},{5,3},{6,0},{7,1},{8,14},{9,15},{10,... | collective-permute-start | bytes 393224 | tf_op jit(solution)/shard_map/ppermute | solution.py:300
  20.8 24.5 %collective-permute-start.3 = (bf16[256,256]{1,0:T(8,128)(2,1)}, bf16[256,256]{1,0:T(8,128)(2,1)S(1)}, u32[]{:S(2)}, u32[]{:S(2)}) collective-permute-start(bf16[256,256]{1,0:T(8,128)(2,1)} %bitcast.26), channel_id=1, source_target_pairs={{0,1},{1,0},{2,3},{3,2},{4,5},{5,4},{6,7},{7,6},{8,9},{9,8},{10,11... | collective-permute-start | bytes 393224 | tf_op jit(solution)/shard_map/ppermute | solution.py:300
  21.5 7.1 %collective-permute-start.14 = (bf16[4,16,256]{2,1,0:T(8,128)(2,1)S(1)}, bf16[4,16,256]{2,1,0:T(8,128)(2,1)S(1)}, u32[]{:S(2)}, u32[]{:S(2)}) collective-permute-start(bf16[4,16,256]{2,1,0:T(8,128)(2,1)S(1)} %get-tuple-element.56), channel_id=1, source_target_pairs={{0,5},{1,4},{2,7},{3,6},{4,1},{5,0},{6,3},{7,2},{8,13},{9,12},{10,... | collective-permute-start | bytes 98312 | tf_op jit(solution)/shard_map/ppermute | solution.py:300
  28.6 7.4 %collective-permute-start.15 = (bf16[4,16,256]{2,1,0:T(8,128)(2,1)S(1)}, bf16[4,16,256]{2,1,0:T(8,128)(2,1)S(1)}, u32[]{:S(2)}, u32[]{:S(2)}) collective-permute-start(bf16[4,16,256]{2,1,0:T(8,128)(2,1)S(1)} %get-tuple-element.57), channel_id=1, source_target_pairs={{0,6},{1,7},{2,4},{3,5},{4,2},{5,3},{6,0},{7,1},{8,14},{9,15},{10,... | collective-permute-start | bytes 98312 | tf_op jit(solution)/shard_map/ppermute | solution.py:300
  30.1 18.1 %collective-permute-start.5 = (bf16[256,256]{1,0:T(8,128)(2,1)S(1)}, bf16[256,256]{1,0:T(8,128)(2,1)S(1)}, u32[]{:S(2)}, u32[]{:S(2)}) collective-permute-start(bf16[256,256]{1,0:T(8,128)(2,1)S(1)} %collective-permute-done.4.refs_4_), channel_id=1, source_target_pairs={{0,1},{1,0},{2,3},{3,2},{4,5},{5,4},{6,7},{7,6},{8,9},{9,8},{10,11... | collective-permute-start | bytes 393224 | tf_op jit(solution)/shard_map/ppermute | solution.py:300
  32.1 1.1 copy-start.1
  33.2 0.7 copy-start.4
  33.9 0.7 copy-start.5
  34.5 0.7 copy-start.6
  35.2 6.2 %copy-start.3 = (bf16[1,512,256]{2,1,0:T(8,128)(2,1)S(1)}, bf16[1,512,256]{2,1,0:T(8,128)(2,1)}, u32[]{:S(2)}) copy-start(bf16[1,512,256]{2,1,0:T(8,128)(2,1)} %param.8) | copy-start | bytes 786436
  35.2 6.2 %copy-start.7 = (bf16[1,256,256]{2,1,0:T(8,128)(2,1)S(1)}, bf16[1,256,256]{2,1,0:T(8,128)(2,1)}, u32[]{:S(2)}) copy-start(bf16[1,256,256]{2,1,0:T(8,128)(2,1)} %param.9) | copy-start | bytes 393220
  36.0 7.5 %collective-permute-start.16 = (bf16[4,16,256]{2,1,0:T(8,128)(2,1)S(1)}, bf16[4,16,256]{2,1,0:T(8,128)(2,1)S(1)}, u32[]{:S(2)}, u32[]{:S(2)}) collective-permute-start(bf16[4,16,256]{2,1,0:T(8,128)(2,1)S(1)} %get-tuple-element.58), channel_id=1, source_target_pairs={{0,7},{1,6},{2,5},{3,4},{4,3},{5,2},{6,1},{7,0},{8,15},{9,14},{10,... | collective-permute-start | bytes 98312 | tf_op jit(solution)/shard_map/ppermute | solution.py:300
  39.3 19.7 %collective-permute-start.7 = (bf16[256,256]{1,0:T(8,128)(2,1)S(1)}, bf16[256,256]{1,0:T(8,128)(2,1)S(1)}, u32[]{:S(2)}, u32[]{:S(2)}) collective-permute-start(bf16[256,256]{1,0:T(8,128)(2,1)S(1)} %collective-permute-done.6.refs_4_.refs_5_), channel_id=1, source_target_pairs={{0,1},{1,0},{2,3},{3,2},{4,5},{5,4},{6,7},{7,6},{8,9},{9,8},{10,11... | collective-permute-start | bytes 393224 | tf_op jit(solution)/shard_map/ppermute | solution.py:300
  44.2 8.3 %collective-permute-start.17 = (bf16[4,16,256]{2,1,0:T(8,128)(2,1)S(1)}, bf16[4,16,256]{2,1,0:T(8,128)(2,1)S(1)}, u32[]{:S(2)}, u32[]{:S(2)}) collective-permute-start(bf16[4,16,256]{2,1,0:T(8,128)(2,1)S(1)} %get-tuple-element.60), channel_id=1, source_target_pairs={{0,1},{1,0},{2,3},{3,2},{4,5},{5,4},{6,7},{7,6},{8,9},{9,8},{10,11... | collective-permute-start | bytes 98312 | tf_op jit(solution)/shard_map/ppermute | solution.py:300
  45.3 8.4 %collective-permute-start.18 = (bf16[4,16,256]{2,1,0:T(8,128)(2,1)S(1)}, bf16[4,16,256]{2,1,0:T(8,128)(2,1)S(1)}, u32[]{:S(2)}, u32[]{:S(2)}) collective-permute-start(bf16[4,16,256]{2,1,0:T(8,128)(2,1)S(1)} %get-tuple-element.61), channel_id=1, source_target_pairs={{0,2},{1,3},{2,0},{3,1},{4,6},{5,7},{6,4},{7,5},{8,10},{9,11},{10,... | collective-permute-start | bytes 98312 | tf_op jit(solution)/shard_map/ppermute | solution.py:300
  45.3 20.3 %collective-permute-start.9 = (bf16[256,256]{1,0:T(8,128)(2,1)S(1)}, bf16[256,256]{1,0:T(8,128)(2,1)S(1)}, u32[]{:S(2)}, u32[]{:S(2)}) collective-permute-start(bf16[256,256]{1,0:T(8,128)(2,1)S(1)} %collective-permute-done.8.refs_4_.refs_6_), channel_id=1, source_target_pairs={{0,1},{1,0},{2,3},{3,2},{4,5},{5,4},{6,7},{7,6},{8,9},{9,8},{10,11... | collective-permute-start | bytes 393224 | tf_op jit(solution)/shard_map/ppermute | solution.py:300
  48.2 7.7 %collective-permute-start.19 = (bf16[4,16,256]{2,1,0:T(8,128)(2,1)S(1)}, bf16[4,16,256]{2,1,0:T(8,128)(2,1)S(1)}, u32[]{:S(2)}, u32[]{:S(2)}) collective-permute-start(bf16[4,16,256]{2,1,0:T(8,128)(2,1)S(1)} %get-tuple-element.62), channel_id=1, source_target_pairs={{0,3},{1,2},{2,1},{3,0},{4,7},{5,6},{6,5},{7,4},{8,11},{9,10},{10,... | collective-permute-start | bytes 98312 | tf_op jit(solution)/shard_map/ppermute | solution.py:300
  52.5 9.5 %collective-permute-start.20 = (bf16[4,16,256]{2,1,0:T(8,128)(2,1)S(1)}, bf16[4,16,256]{2,1,0:T(8,128)(2,1)S(1)}, u32[]{:S(2)}, u32[]{:S(2)}) collective-permute-start(bf16[4,16,256]{2,1,0:T(8,128)(2,1)S(1)} %get-tuple-element.63), channel_id=1, source_target_pairs={{0,4},{1,5},{2,6},{3,7},{4,0},{5,1},{6,2},{7,3},{8,12},{9,13},{10,... | collective-permute-start | bytes 98312 | tf_op jit(solution)/shard_map/ppermute | solution.py:300
  53.7 8.4 %collective-permute-start.21 = (bf16[4,16,256]{2,1,0:T(8,128)(2,1)S(1)}, bf16[4,16,256]{2,1,0:T(8,128)(2,1)S(1)}, u32[]{:S(2)}, u32[]{:S(2)}) collective-permute-start(bf16[4,16,256]{2,1,0:T(8,128)(2,1)S(1)} %get-tuple-element.64), channel_id=1, source_target_pairs={{0,5},{1,4},{2,7},{3,6},{4,1},{5,0},{6,3},{7,2},{8,13},{9,12},{10,... | collective-permute-start | bytes 98312 | tf_op jit(solution)/shard_map/ppermute | solution.py:300
  55.9 6.2 %collective-permute-start.22 = (bf16[4,16,256]{2,1,0:T(8,128)(2,1)S(1)}, bf16[4,16,256]{2,1,0:T(8,128)(2,1)S(1)}, u32[]{:S(2)}, u32[]{:S(2)}) collective-permute-start(bf16[4,16,256]{2,1,0:T(8,128)(2,1)S(1)} %get-tuple-element.65), channel_id=1, source_target_pairs={{0,6},{1,7},{2,4},{3,5},{4,2},{5,3},{6,0},{7,1},{8,14},{9,15},{10,... | collective-permute-start | bytes 98312 | tf_op jit(solution)/shard_map/ppermute | solution.py:300
  59.0 6.6 %collective-permute-start.23 = (bf16[4,16,256]{2,1,0:T(8,128)(2,1)S(1)}, bf16[4,16,256]{2,1,0:T(8,128)(2,1)S(1)}, u32[]{:S(2)}, u32[]{:S(2)}) collective-permute-start(bf16[4,16,256]{2,1,0:T(8,128)(2,1)S(1)} %get-tuple-element.66), channel_id=1, source_target_pairs={{0,7},{1,6},{2,5},{3,4},{4,3},{5,2},{6,1},{7,0},{8,15},{9,14},{10,... | collective-permute-start | bytes 98312 | tf_op jit(solution)/shard_map/ppermute | solution.py:300
  71.9 12.7 %collective-permute-start.28 = (bf16[4,16,256]{2,1,0:T(8,128)(2,1)S(1)}, bf16[4,16,256]{2,1,0:T(8,128)(2,1)S(1)}, u32[]{:S(2)}, u32[]{:S(2)}) collective-permute-start(bf16[4,16,256]{2,1,0:T(8,128)(2,1)S(1)} %get-tuple-element.80), channel_id=1, source_target_pairs={{0,1},{1,0},{2,3},{3,2},{4,5},{5,4},{6,7},{7,6},{8,9},{9,8},{10,11... | collective-permute-start | bytes 98312 | tf_op jit(solution)/shard_map/ppermute | solution.py:300
  72.2 12.6 %collective-permute-start.29 = (bf16[4,16,256]{2,1,0:T(8,128)(2,1)S(1)}, bf16[4,16,256]{2,1,0:T(8,128)(2,1)S(1)}, u32[]{:S(2)}, u32[]{:S(2)}) collective-permute-start(bf16[4,16,256]{2,1,0:T(8,128)(2,1)S(1)} %get-tuple-element.81), channel_id=1, source_target_pairs={{0,2},{1,3},{2,0},{3,1},{4,6},{5,7},{6,4},{7,5},{8,10},{9,11},{10,... | collective-permute-start | bytes 98312 | tf_op jit(solution)/shard_map/ppermute | solution.py:300
  72.2 12.7 %collective-permute-start.30 = (bf16[4,16,256]{2,1,0:T(8,128)(2,1)S(1)}, bf16[4,16,256]{2,1,0:T(8,128)(2,1)S(1)}, u32[]{:S(2)}, u32[]{:S(2)}) collective-permute-start(bf16[4,16,256]{2,1,0:T(8,128)(2,1)S(1)} %get-tuple-element.82), channel_id=1, source_target_pairs={{0,3},{1,2},{2,1},{3,0},{4,7},{5,6},{6,5},{7,4},{8,11},{9,10},{10,... | collective-permute-start | bytes 98312 | tf_op jit(solution)/shard_map/ppermute | solution.py:300
  82.5 20.2 %collective-permute-start.24 = (bf16[256,256]{1,0:T(8,128)(2,1)S(1)}, bf16[256,256]{1,0:T(8,128)(2,1)S(1)}, u32[]{:S(2)}, u32[]{:S(2)}) collective-permute-start(bf16[256,256]{1,0:T(8,128)(2,1)S(1)} %get-tuple-element.71), channel_id=1, source_target_pairs={{0,1},{1,0},{2,3},{3,2},{4,5},{5,4},{6,7},{7,6},{8,9},{9,8},{10,11... | collective-permute-start | bytes 393224 | tf_op jit(solution)/shard_map/ppermute | solution.py:300
  82.8 22.8 %collective-permute-start.25 = (bf16[256,256]{1,0:T(8,128)(2,1)S(1)}, bf16[256,256]{1,0:T(8,128)(2,1)S(1)}, u32[]{:S(2)}, u32[]{:S(2)}) collective-permute-start(bf16[256,256]{1,0:T(8,128)(2,1)S(1)} %get-tuple-element.72), channel_id=1, source_target_pairs={{0,1},{1,0},{2,3},{3,2},{4,5},{5,4},{6,7},{7,6},{8,9},{9,8},{10,11... | collective-permute-start | bytes 393224 | tf_op jit(solution)/shard_map/ppermute | solution.py:300
  84.6 21.9 %collective-permute-start.26 = (bf16[256,256]{1,0:T(8,128)(2,1)S(1)}, bf16[256,256]{1,0:T(8,128)(2,1)S(1)}, u32[]{:S(2)}, u32[]{:S(2)}) collective-permute-start(bf16[256,256]{1,0:T(8,128)(2,1)S(1)} %get-tuple-element.73), channel_id=1, source_target_pairs={{0,1},{1,0},{2,3},{3,2},{4,5},{5,4},{6,7},{7,6},{8,9},{9,8},{10,11... | collective-permute-start | bytes 393224 | tf_op jit(solution)/shard_map/ppermute | solution.py:300
  84.8 5.0 %collective-permute-start.31 = (bf16[4,16,256]{2,1,0:T(8,128)(2,1)S(1)}, bf16[4,16,256]{2,1,0:T(8,128)(2,1)S(1)}, u32[]{:S(2)}, u32[]{:S(2)}) collective-permute-start(bf16[4,16,256]{2,1,0:T(8,128)(2,1)S(1)} %get-tuple-element.83), channel_id=1, source_target_pairs={{0,4},{1,5},{2,6},{3,7},{4,0},{5,1},{6,2},{7,3},{8,12},{9,13},{10,... | collective-permute-start | bytes 98312 | tf_op jit(solution)/shard_map/ppermute | solution.py:300
  84.9 6.4 %collective-permute-start.32 = (bf16[4,16,256]{2,1,0:T(8,128)(2,1)S(1)}, bf16[4,16,256]{2,1,0:T(8,128)(2,1)S(1)}, u32[]{:S(2)}, u32[]{:S(2)}) collective-permute-start(bf16[4,16,256]{2,1,0:T(8,128)(2,1)S(1)} %get-tuple-element.84), channel_id=1, source_target_pairs={{0,5},{1,4},{2,7},{3,6},{4,1},{5,0},{6,3},{7,2},{8,13},{9,12},{10,... | collective-permute-start | bytes 98312 | tf_op jit(solution)/shard_map/ppermute | solution.py:300
  89.8 5.9 %collective-permute-start.33 = (bf16[4,16,256]{2,1,0:T(8,128)(2,1)S(1)}, bf16[4,16,256]{2,1,0:T(8,128)(2,1)S(1)}, u32[]{:S(2)}, u32[]{:S(2)}) collective-permute-start(bf16[4,16,256]{2,1,0:T(8,128)(2,1)S(1)} %get-tuple-element.85), channel_id=1, source_target_pairs={{0,6},{1,7},{2,4},{3,5},{4,2},{5,3},{6,0},{7,1},{8,14},{9,15},{10,... | collective-permute-start | bytes 98312 | tf_op jit(solution)/shard_map/ppermute | solution.py:300
  91.3 6.8 %collective-permute-start.34 = (bf16[4,16,256]{2,1,0:T(8,128)(2,1)S(1)}, bf16[4,16,256]{2,1,0:T(8,128)(2,1)S(1)}, u32[]{:S(2)}, u32[]{:S(2)}) collective-permute-start(bf16[4,16,256]{2,1,0:T(8,128)(2,1)S(1)} %get-tuple-element.86), channel_id=1, source_target_pairs={{0,7},{1,6},{2,5},{3,4},{4,3},{5,2},{6,1},{7,0},{8,15},{9,14},{10,... | collective-permute-start | bytes 98312 | tf_op jit(solution)/shard_map/ppermute | solution.py:300
  98.7 4.0 %collective-permute-start.35 = (bf16[4,16,256]{2,1,0:T(8,128)(2,1)S(1)}, bf16[4,16,256]{2,1,0:T(8,128)(2,1)S(1)}, u32[]{:S(2)}, u32[]{:S(2)}) collective-permute-start(bf16[4,16,256]{2,1,0:T(8,128)(2,1)S(1)} %get-tuple-element.88), channel_id=1, source_target_pairs={{0,1},{1,0},{2,3},{3,2},{4,5},{5,4},{6,7},{7,6},{8,9},{9,8},{10,11... | collective-permute-start | bytes 98312 | tf_op jit(solution)/shard_map/ppermute | solution.py:300
  100.1 20.6 %collective-permute-start.27 = (bf16[256,256]{1,0:T(8,128)(2,1)S(1)}, bf16[256,256]{1,0:T(8,128)(2,1)S(1)}, u32[]{:S(2)}, u32[]{:S(2)}) collective-permute-start(bf16[256,256]{1,0:T(8,128)(2,1)S(1)} %get-tuple-element.75), channel_id=1, source_target_pairs={{0,1},{1,0},{2,3},{3,2},{4,5},{5,4},{6,7},{7,6},{8,9},{9,8},{10,11... | collective-permute-start | bytes 393224 | tf_op jit(solution)/shard_map/ppermute | solution.py:300
  102.7 11.4 %collective-permute-start.36 = (bf16[4,16,256]{2,1,0:T(8,128)(2,1)S(1)}, bf16[4,16,256]{2,1,0:T(8,128)(2,1)S(1)}, u32[]{:S(2)}, u32[]{:S(2)}) collective-permute-start(bf16[4,16,256]{2,1,0:T(8,128)(2,1)S(1)} %get-tuple-element.89), channel_id=1, source_target_pairs={{0,2},{1,3},{2,0},{3,1},{4,6},{5,7},{6,4},{7,5},{8,10},{9,11},{10,... | collective-permute-start | bytes 98312 | tf_op jit(solution)/shard_map/ppermute | solution.py:300
  102.7 11.5 %collective-permute-start.37 = (bf16[4,16,256]{2,1,0:T(8,128)(2,1)S(1)}, bf16[4,16,256]{2,1,0:T(8,128)(2,1)S(1)}, u32[]{:S(2)}, u32[]{:S(2)}) collective-permute-start(bf16[4,16,256]{2,1,0:T(8,128)(2,1)S(1)} %get-tuple-element.90), channel_id=1, source_target_pairs={{0,3},{1,2},{2,1},{3,0},{4,7},{5,6},{6,5},{7,4},{8,11},{9,10},{10,... | collective-permute-start | bytes 98312 | tf_op jit(solution)/shard_map/ppermute | solution.py:300
  105.5 11.4 %collective-permute-start.38 = (bf16[4,16,256]{2,1,0:T(8,128)(2,1)S(1)}, bf16[4,16,256]{2,1,0:T(8,128)(2,1)S(1)}, u32[]{:S(2)}, u32[]{:S(2)}) collective-permute-start(bf16[4,16,256]{2,1,0:T(8,128)(2,1)S(1)} %get-tuple-element.91), channel_id=1, source_target_pairs={{0,4},{1,5},{2,6},{3,7},{4,0},{5,1},{6,2},{7,3},{8,12},{9,13},{10,... | collective-permute-start | bytes 98312 | tf_op jit(solution)/shard_map/ppermute | solution.py:300
  106.5 12.1 %collective-permute-start.39 = (bf16[4,16,256]{2,1,0:T(8,128)(2,1)S(1)}, bf16[4,16,256]{2,1,0:T(8,128)(2,1)S(1)}, u32[]{:S(2)}, u32[]{:S(2)}) collective-permute-start(bf16[4,16,256]{2,1,0:T(8,128)(2,1)S(1)} %get-tuple-element.92), channel_id=1, source_target_pairs={{0,5},{1,4},{2,7},{3,6},{4,1},{5,0},{6,3},{7,2},{8,13},{9,12},{10,... | collective-permute-start | bytes 98312 | tf_op jit(solution)/shard_map/ppermute | solution.py:300
  114.1 16.7 %collective-permute-start.42 = (bf16[256,256]{1,0:T(8,128)(2,1)S(1)}, bf16[256,256]{1,0:T(8,128)(2,1)S(1)}, u32[]{:S(2)}, u32[]{:S(2)}) collective-permute-start(bf16[256,256]{1,0:T(8,128)(2,1)S(1)} %get-tuple-element.96), channel_id=1, source_target_pairs={{0,2},{1,3},{2,0},{3,1},{4,6},{5,7},{6,4},{7,5},{8,10},{9,11},{10,... | collective-permute-start | bytes 393224 | tf_op jit(solution)/shard_map/ppermute | solution.py:300
  114.2 16.6 %collective-permute-start.43 = (bf16[256,256]{1,0:T(8,128)(2,1)S(1)}, bf16[256,256]{1,0:T(8,128)(2,1)S(1)}, u32[]{:S(2)}, u32[]{:S(2)}) collective-permute-start(bf16[256,256]{1,0:T(8,128)(2,1)S(1)} %get-tuple-element.97), channel_id=1, source_target_pairs={{0,4},{1,5},{2,6},{3,7},{4,0},{5,1},{6,2},{7,3},{8,12},{9,13},{10,... | collective-permute-start | bytes 393224 | tf_op jit(solution)/shard_map/ppermute | solution.py:300
  116.9 14.0 %collective-permute-start.44 = (bf16[256,256]{1,0:T(8,128)(2,1)S(1)}, bf16[256,256]{1,0:T(8,128)(2,1)S(1)}, u32[]{:S(2)}, u32[]{:S(2)}) collective-permute-start(bf16[256,256]{1,0:T(8,128)(2,1)S(1)} %get-tuple-element.98), channel_id=1, source_target_pairs={{0,6},{1,7},{2,4},{3,5},{4,2},{5,3},{6,0},{7,1},{8,14},{9,15},{10,... | collective-permute-start | bytes 393224 | tf_op jit(solution)/shard_map/ppermute | solution.py:300
  118.6 10.9 %collective-permute-start.40 = (bf16[4,16,256]{2,1,0:T(8,128)(2,1)S(1)}, bf16[4,16,256]{2,1,0:T(8,128)(2,1)S(1)}, u32[]{:S(2)}, u32[]{:S(2)}) collective-permute-start(bf16[4,16,256]{2,1,0:T(8,128)(2,1)S(1)} %get-tuple-element.93), channel_id=1, source_target_pairs={{0,6},{1,7},{2,4},{3,5},{4,2},{5,3},{6,0},{7,1},{8,14},{9,15},{10,... | collective-permute-start | bytes 98312 | tf_op jit(solution)/shard_map/ppermute | solution.py:300
  120.7 8.8 %collective-permute-start.41 = (bf16[4,16,256]{2,1,0:T(8,128)(2,1)S(1)}, bf16[4,16,256]{2,1,0:T(8,128)(2,1)S(1)}, u32[]{:S(2)}, u32[]{:S(2)}) collective-permute-start(bf16[4,16,256]{2,1,0:T(8,128)(2,1)S(1)} %get-tuple-element.94), channel_id=1, source_target_pairs={{0,7},{1,6},{2,5},{3,4},{4,3},{5,2},{6,1},{7,0},{8,15},{9,14},{10,... | collective-permute-start | bytes 98312 | tf_op jit(solution)/shard_map/ppermute | solution.py:300

commit v2 on v1

v2 whole, which is shorter than its diff:
```python
from functools import partial

import jax
import jax.numpy as jnp
from jax import lax
from jax.experimental import pallas as pl
from jax.experimental.pallas import tpu as pltpu
from jax.sharding import PartitionSpec as P

RESP = 16
BLK = 128
NB = 2
LOSS_SCALE = 32.0
BIG_NEGATIVE = -1e30
LOG2E = 1.4426950408889634

F32 = jnp.float32
BF16 = jnp.bfloat16
NT = (((1,), (1,)), ((), ()))
TN = (((0,), (0,)), ((), ()))
NN = (((1,), (0,)), ((), ()))
TILE = 2 * BLK
VMEM = pl.BlockSpec(memory_space=pltpu.VMEM)
SMEM = pl.BlockSpec(memory_space=pltpu.SMEM)


def dot(a, b, dims):
    return lax.dot_general(a, b, dims, preferred_element_type=F32)


def call(kernel, name, out_shape, specs, args, scratch=(), flops=0, aliases=None):
    moved = sum(a.size * a.dtype.itemsize for a in args)
    return pl.pallas_call(
        kernel,
        name=name,
        out_shape=out_shape,
        in_specs=specs,
        out_specs=jax.tree.map(lambda _: VMEM, out_shape),
        scratch_shapes=list(scratch),
        input_output_aliases=aliases or {},
        compiler_params=pltpu.CompilerParams(vmem_limit_bytes=24 * 2**20),
        cost_estimate=pl.CostEstimate(flops=4 * flops, bytes_accessed=moved, transcendentals=0),
    )(*args)


def write_pieces(pairs_ref, out_refs):
    line = lax.div(lax.axis_index("seq"), 2)
    rows = BLK // len(out_refs)
    for k, out_ref in enumerate(out_refs):
        first = lax.bitwise_xor(line, k) * rows
        for s in range(out_ref.shape[0]):
            place = pl.ds(pl.multiple_of(s * BLK + first, rows), rows)
            out_ref[s] = pairs_ref[place].astype(BF16)


def split_kernel(kv_ref, *out_refs):
    write_pieces(kv_ref, out_refs)


def stack_kernel(*refs):
    for k, ref in enumerate(refs[:-1]):
        refs[-1][k] = ref[...]


def route_kernel(plan_ref, mine_ref, other_ref, *refs):
    outs, held, inverse = refs[:-2], refs[-2], refs[-1]
    me = lax.axis_index("seq")
    line, side = lax.div(me, 2), lax.rem(me, 2)
    held[side] = mine_ref[...]
    held[1 - side] = other_ref[...]
    local = mine_ref.shape[1]
    for j in range(plan_ref.shape[1]):
        inverse[plan_ref[0, j]] = j
    for k, out_ref in enumerate(outs):
        device = lax.bitwise_xor(line, k) * 2 + side
        for s in range(local):
            partner = inverse[lax.bitwise_xor(plan_ref[0, device * local + s], 1)]
            owner = lax.div(partner, local)
            place = lax.bitwise_xor(lax.div(owner, 2), line)
            out_ref[s] = held[lax.rem(owner, 2), place, lax.rem(partner, local)]


def join_pieces(pieces, out_ref):
    line = lax.div(lax.axis_index("seq"), 2)
    rows = BLK // len(pieces)
    for k, ref in enumerate(pieces):
        first = lax.bitwise_xor(line, k) * rows
        for s in range(ref.shape[0]):
            out_ref[pl.ds(pl.multiple_of(s * BLK + first, rows), rows)] = ref[s]


def weight_kernel(groups, plan_ref, rewards_ref, grad_ref, *refs):
    lengths, out_ref = refs[:groups], refs[groups]
    me = lax.axis_index("seq")
    local = grad_ref.shape[0] // BLK
    total = jnp.int32(0)
    for ref in lengths:
        for r in range(RESP):
            total = total + ref[0, r]
    reward_sum = rewards_ref[0, 0]
    for r in range(1, RESP):
        reward_sum = reward_sum + rewards_ref[0, r]
    mean = reward_sum * (1.0 / RESP)
    count = jnp.full((BLK, 1), total.astype(F32))
    row = lax.broadcasted_iota(jnp.int32, (BLK, 1), 0)
    for s in range(local):
        block = plan_ref[0, me * local + s]
        response = lax.div(block, NB)
        first = lax.rem(block, NB) * BLK
        scaled = (rewards_ref[0, response] - mean) * (LOSS_SCALE * groups * RESP * NB * BLK)
        weight = jnp.where(row + first < lengths[0][0, response], scaled / count, 0.0)
        rows = slice(s * BLK, (s + 1) * BLK)
        out_ref[rows] = (grad_ref[rows].astype(F32) * weight).astype(BF16)


def head_tiles(q_ref):
    halves = q_ref.shape[0] // TILE
    return [
        (h * halves + r, r, slice(r * TILE, (r + 1) * TILE), slice(h * BLK, (h + 1) * BLK))
        for h in range(q_ref.shape[1] // BLK)
        for r in range(halves)
    ]


KEYS = slice(0, BLK)
VALUES = slice(BLK, 2 * BLK)


def block_rows(ref, j):
    rows = slice(j * BLK, (j + 1) * BLK)
    heads = ref.shape[1] // BLK
    return jnp.concatenate([ref[rows, h * BLK : (h + 1) * BLK] for h in range(heads)], axis=0)


def block_seen(plan_ref, j, local, heads):
    if plan_ref is None:
        key = lax.broadcasted_iota(jnp.int32, (BLK, BLK), 0)
        row = lax.broadcasted_iota(jnp.int32, (BLK, BLK), 1)
        return jnp.concatenate([key <= row] * heads, axis=1)
    me = lax.axis_index("seq")
    odd = lax.rem(plan_ref[0, me * local + j], NB)
    return jnp.full((BLK, heads * BLK), odd, jnp.int32) > 0


def merged(scale, first, second):
    peak = jnp.maximum(first[0], second[0])
    a, b = jnp.exp2((first[0] - peak) * scale), jnp.exp2((second[0] - peak) * scale)
    return peak, first[1] * a + second[1] * b, first[2] * a + second[2] * b


def score_stats(scale, s, dp):
    peak = jnp.max(s, axis=0, keepdims=True)
    e = jnp.exp2(s * scale - peak * scale)
    return peak, jnp.sum(e, axis=0, keepdims=True), jnp.sum(e * dp, axis=0, keepdims=True)


def stats_kernel(scale, shards, own, parts, carried, *refs):
    refs = list(refs)
    plan_ref = refs.pop(0) if parts else None
    q_ref, w_ref = refs.pop(0), refs.pop(0)
    before = refs.pop(0) if carried else None
    kv = [refs.pop(0) for _ in range(shards)]
    own_ref = refs.pop(0) if own else None
    pieces = [refs.pop(0) for _ in range(parts)]
    out_ref = refs.pop(0)
    heads, local = q_ref.shape[1] // BLK, q_ref.shape[0] // BLK
    block_stats = None
    if parts:
        own_ref = refs.pop(0)
        join_pieces(pieces, own_ref)
    if own_ref is not None:
        block_stats = []
        for j in range(local):
            pairs = own_ref[j * BLK : (j + 1) * BLK]
            s = dot(pairs[:, KEYS], block_rows(q_ref, j), NT)
            dp = dot(pairs[:, VALUES], block_rows(w_ref, j), NT)
            s = jnp.where(block_seen(plan_ref, j, local, heads), s, BIG_NEGATIVE)
            block_stats.append(score_stats(scale, s, dp))
    for t, r, rows, cols in head_tiles(q_ref):
        q, w = q_ref[rows, cols], w_ref[rows, cols]
        state = None
        if carried:
            state = tuple(before[t, i : i + 1] for i in range(3))
        if block_stats is not None:
            pair = block_stats[2 * r : 2 * r + 2]
            more = tuple(jnp.concatenate([x[i][:, cols] for x in pair], axis=1) for i in range(3))
            state = more if state is None else merged(scale, state, more)
        for ref in kv:
            s, dp = dot(ref[:, KEYS], q, NT), dot(ref[:, VALUES], w, NT)
            if state is None:
                state = score_stats(scale, s, dp)
                continue
            m, l, d = state
            peak = jnp.maximum(m, jnp.max(s, axis=0, keepdims=True))
            shrink = jnp.exp2((m - peak) * scale)
            e = jnp.exp2(s * scale - peak * scale)
            l = l * shrink + jnp.sum(e, axis=0, keepdims=True)
            d = d * shrink + jnp.sum(e * dp, axis=0, keepdims=True)
            state = peak, l, d
        for i in range(3):
            out_ref[t, i : i + 1] = state[i]


def grad_kernel(scale, shards, inits, own, partner, carried, last, *refs):
    refs = list(refs)
    plan_ref = refs.pop(0) if partner else None
    q_ref, w_ref, stats_ref = refs.pop(0), refs.pop(0), refs.pop(0)
    before = refs.pop(0) if carried else None
    kv = [refs.pop(0) for _ in range(shards)]
    init = [refs.pop(0) for _ in range(inits)]
    blocks_ref = refs.pop(0) if own or partner else None
    dq_ref = refs.pop(0)
    kv_out = refs.pop(0) if shards else None
    blocks_out = refs if partner else refs.pop(0) if own else None
    if partner:
        blocks_out, blocks_sum = refs[:partner], refs[partner]
    elif own:
        blocks_sum = blocks_out
    kv_sum, dq_part = (refs[0], refs[1]) if shards and own else (refs[0] if shards else None, dq_ref)
    heads, local = q_ref.shape[1] // BLK, q_ref.shape[0] // BLK
    halves = q_ref.shape[0] // TILE
    back = scale / LOG2E

    def factors(rows):
        inverse = 1.0 / rows[1]
        return rows[0] * scale, inverse, rows[2] * inverse

    def grads(s, dp, rows):
        peak, inverse, delta = rows
        p = jnp.exp2(s * scale - peak) * inverse
        return p.astype(BF16), (p * (dp - delta)).astype(BF16)

    if blocks_ref is not None:
        for j in range(local):
            place = slice(j * BLK, (j + 1) * BLK)
            lanes = slice((j % 2) * BLK, (j % 2 + 1) * BLK)
            rows = [
                jnp.concatenate(
                    [stats_ref[h * halves + j // 2, i : i + 1, lanes] for h in range(heads)], axis=1
                )
                for i in range(3)
            ]
            q, w = block_rows(q_ref, j), block_rows(w_ref, j)
            keys = blocks_ref[place, KEYS]
            s = jnp.where(block_seen(plan_ref, j, local, heads), dot(keys, q, NT), BIG_NEGATIVE)
            p, ds = grads(s, dot(blocks_ref[place, VALUES], w, NT), factors(rows))
            blocks_sum[place, KEYS] = dot(ds, q, NN) * back
            blocks_sum[place, VALUES] = dot(p, w, NN)
            dq = dot(ds, keys, TN)
            for h in range(heads):
                dq_part[place, h * BLK : (h + 1) * BLK] = dq[h * BLK : (h + 1) * BLK]
        if partner:
            write_pieces(blocks_sum, blocks_out)
    if not shards:
        return
    per = kv[0].shape[0]
    keys = jnp.concatenate([ref[:, KEYS] for ref in kv], axis=0)
    values = jnp.concatenate([ref[:, VALUES] for ref in kv], axis=0)
    for t, r, rows, cols in head_tiles(q_ref):
        q, w = q_ref[rows, cols], w_ref[rows, cols]
        state = factors([stats_ref[t, i : i + 1] for i in range(3)])
        p, ds = grads(dot(keys, q, NT), dot(values, w, NT), state)
        dk, dv = dot(ds, q, NN), dot(p, w, NN)
        if t == 0:
            kv_sum[:, KEYS] = dk
            kv_sum[:, VALUES] = dv
        else:
            kv_sum[:, KEYS] += dk
            kv_sum[:, VALUES] += dv
        dq = dot(ds, keys, TN)
        if own:
            dq = dq + dq_part[rows, cols]
        if carried:
            dq = dq + before[rows, cols]
        dq_ref[rows, cols] = (dq * back).astype(BF16) if last else dq
    for side, factor in ((KEYS, back), (VALUES, 1.0)):
        total = kv_sum[:, side] * factor
        for ref in init:
            total = total + ref[:, side].astype(F32)
        kv_out[:, side] = total.astype(kv_out.dtype)


def finish_kernel(plan_ref, own_ref, *refs):
    pieces, out_ref, held = refs[:-2], refs[-2], refs[-1]
    me = lax.axis_index("seq")
    local = own_ref.shape[0] // BLK
    join_pieces(pieces, held)
    for s in range(local):
        rows = slice(s * BLK, (s + 1) * BLK)
        odd = lax.rem(plan_ref[0, me * local + s], NB)
        odd_rows = jnp.full((BLK, 2 * BLK), odd, jnp.int32) > 0
        extra = jnp.where(odd_rows, 0.0, held[rows].astype(F32))
        out_ref[rows] = (own_ref[rows] + extra).astype(BF16)


def pick_kernel(per, parts, picked, *refs):
    out_ref = refs[-1]
    where = []
    for ref in refs[:parts]:
        where += [(ref, i) for i in range(ref.shape[0] // per)]
    for n, i in enumerate(picked):
        ref, at = where[i]
        total = ref[at * per : (at + 1) * per].astype(F32)
        for other in refs[parts:-1]:
            total = total + other[i * per : (i + 1) * per].astype(F32)
        out_ref[n * per : (n + 1) * per] = total.astype(out_ref.dtype)


def local(query, resp_kv, prompt_kv, grad_out, rewards, lengths, block_order):
    groups = lax.axis_size("grp")
    count = lax.axis_size("seq")
    q, resp, prompt, grad = query[0], resp_kv[0], prompt_kv[0], grad_out[0]
    rows, width = resp.shape
    blocks = rows // BLK
    heads = q.shape[1] // BLK
    line = count // 2
    scale = LOG2E * BLK**-0.5
    piece = jax.ShapeDtypeStruct((blocks, BLK // line, width), BF16)
    stack = jax.ShapeDtypeStruct((line, *piece.shape), BF16)

    def swap(x, axis, k):
        size = lax.axis_size(axis)
        return lax.ppermute(x, axis, [(i, i ^ k) for i in range(size)])

    def along(sent):
        return [sent[0]] + [swap(sent[k], "seq", 2 * k) for k in range(1, line)]

    def route(name, sent):
        mine = call(stack_kernel, name + "_stack", stack, [VMEM] * line, along(sent))
        other = swap(mine, "seq", 1)
        routed = call(
            route_kernel,
            name + "_route",
            [piece] * line,
            [SMEM, VMEM, VMEM],
            [block_order, mine, other],
            [pltpu.VMEM((2, *stack.shape), BF16), pltpu.SMEM((block_order.shape[1],), jnp.int32)],
        )
        return along(routed)

    lengths_all = [lengths] + [swap(lengths, "grp", k) for k in range(1, groups)]
    arrived = route("pairs", call(split_kernel, "pairs_split", [piece] * line, [VMEM], [resp]))
    column = {0: prompt}
    bit = count // 2
    while bit > 1:
        column.update({k ^ bit: swap(x, "seq", bit) for k, x in column.items()})
        bit //= 2
    across = {k: swap(x, "seq", 1) for k, x in column.items()}
    weighted = call(
        partial(weight_kernel, groups),
        "weight_rows",
        jax.ShapeDtypeStruct(grad.shape, BF16),
        [SMEM, SMEM, VMEM] + [SMEM] * groups,
        [block_order, rewards, grad, *lengths_all],
    )

    stats_shape = jax.ShapeDtypeStruct((heads * rows // TILE, 8, TILE), F32)
    product_flops = 2 * rows * heads * BLK

    def stats(name, before, kv, own=None, parts=()):
        args = [block_order] if parts else []
        specs = [SMEM] * len(args)
        args += [q, weighted] + ([before] if before is not None else []) + list(kv)
        args += ([own] if own is not None else []) + list(parts)
        specs += [VMEM] * (len(args) - len(specs))
        keys = sum(x.shape[0] for x in kv) + BLK * ((own is not None) + bool(parts))
        return call(
            partial(stats_kernel, scale, len(kv), own is not None, len(parts), before is not None),
            name,
            [stats_shape, jax.ShapeDtypeStruct(resp.shape, BF16)] if parts else stats_shape,
            specs,
            args,
            flops=2 * keys * product_flops,
        )

    state = stats("stats_own", None, [prompt], own=resp)
    coming = [x for k, x in column.items() if k] + list(across.values())
    while len(coming) > 1:
        state = stats("stats_prompt", state, coming[:2])
        coming = coming[2:]
    state, partner = stats("stats_last", state, coming, parts=arrived)

    def grads(name, before, kv, init=(), own=None, part=None, last=False, kind=BF16):
        args = [block_order] if part is not None else []
        specs = [SMEM] * len(args)
        args += [q, weighted, state] + ([before] if before is not None else [])
        args += list(kv) + list(init) + [x for x in (own, part) if x is not None]
        specs += [VMEM] * (len(args) - len(specs))
        keys = sum(x.shape[0] for x in kv)
        out = [jax.ShapeDtypeStruct(q.shape, BF16 if last else F32)]
        out += [jax.ShapeDtypeStruct((keys, width), kind)] if kv else []
        scratch = [pltpu.VMEM((keys, width), F32)] if kv else []
        if own is not None:
            out.append(jax.ShapeDtypeStruct(resp.shape, F32))
            scratch.append(pltpu.VMEM(q.shape, F32))
        if part is not None:
            out += [piece] * line
            scratch.append(pltpu.VMEM(resp.shape, F32))
        body = partial(
            grad_kernel,
            scale,
            len(kv),
            len(init),
            own is not None,
            line if part is not None else 0,
            before is not None,
            last,
        )
        flops = 5 * (keys + BLK * ((own is not None) + (part is not None))) * product_flops
        return call(body, name, out, specs, args, scratch, flops=flops)

    per = prompt.shape[0]
    near = [k for k in column if k & 2]
    rest = [k for k in column if not k & 2]
    dq, *terms = grads("grads_partner", None, [], part=partner)
    returned = route("terms", terms)
    dq, far_near = grads("grads_across", dq, [across[k] for k in near])
    far_near = swap(far_near, "seq", 1)
    dq, far_rest = grads("grads_across", dq, [across[k] for k in rest])
    far_rest = swap(far_rest, "seq", 1)
    dq, sums = grads("grads_near", dq, [column[k] for k in near], init=[far_near])
    sums = swap(sums, "seq", 2)
    held = rest
    dq, mine, own_terms = grads("grads_own", dq, [column[k] for k in rest[:1]], own=resp, kind=F32)
    dq, others = grads("grads_rest", dq, [column[k] for k in rest[1:]], last=True, kind=F32)
    parts = [mine, others]
    extra = [far_rest, sums]
    raise_to = 4
    grad_prompt = None
    while raise_to < count:
        keep = [i for i, k in enumerate(held) if not k & raise_to]
        send = [i for i, k in enumerate(held) if k & raise_to]
        sent = call(
            partial(pick_kernel, per, len(parts), tuple(send)),
            "sum_far",
            jax.ShapeDtypeStruct((per * len(send), width), BF16),
            [VMEM] * (len(parts) + len(extra)),
            [*parts, *extra],
        )
        received = swap(sent, "seq", raise_to)
        kept = call(
            partial(pick_kernel, per, len(parts), tuple(keep)),
            "sum_near",
            jax.ShapeDtypeStruct((per * len(keep), width), F32),
            [VMEM] * (len(parts) + len(extra)),
            [*parts, *extra],
        )
        held, parts, extra = [held[i] for i in keep], [kept], [received]
        raise_to *= 2
    grad_prompt = call(
        partial(pick_kernel, per, len(parts), (0,)),
        "sum_prompt",
        jax.ShapeDtypeStruct(prompt.shape, BF16),
        [VMEM] * (len(parts) + len(extra)),
        [*parts, *extra],
    )
    grad_stream = call(
        finish_kernel,
        "sum_stream",
        jax.ShapeDtypeStruct(resp.shape, BF16),
        [SMEM, VMEM] + [VMEM] * line,
        [block_order, own_terms, *returned],
        [pltpu.VMEM(resp.shape, BF16)],
    )
    return dq[None], grad_stream[None], grad_prompt[None]


def solution(mesh):
    in_specs = (
        P("grp", "seq", None),
        P("grp", "seq", None),
        P("grp", "seq", None),
        P("grp", "seq", None),
        P("grp", None),
        P("grp", None),
        P("grp", None),
    )
    out_specs = (P("grp", "seq", None), P("grp", "seq", None), P("grp", "seq", None))
    return jax.shard_map(local, mesh=mesh, in_specs=in_specs, out_specs=out_specs, check_vma=False)
```

time: 132 us -> 90.9 us (0.69)
  starting transfers between devices: 70.7 us -> 34.8 us
  waiting for transfers between devices: 19.2 us -> 14.8 us
    ppermute x45 -> x28, starting transfers between devices: 70.7 us -> 34.8 us  [swap(): return lax.ppermute(x, axis, [(i, i ^ k) for i in range(size)])]
    ppermute x45 -> x28, waiting for transfers between devices: 19.2 us -> 14.8 us  [swap(): return lax.ppermute(x, axis, [(i, i ^ k) for i in range(size)])]
    pallas_call x16 -> x21, Pallas kernels: 36.8 us -> 35.9 us  [call(): pl.pallas_call(kernel, name=name, out_shape=out_shape, in_specs=specs, ou...]
    unnamed x16 -> x18, local copies, waits for them, and re-layouts: 4.01 us -> 4.32 us
  transfers between devices with their start and end apart: 45 -> 28, of which waited for: 11 -> 9; matrix products, arithmetic and copies ran while one was open for 0% -> 0% of each run, Pallas kernels for 23% -> 34%
where the time goes in v2:
time: 90.9 us; the launch traced here: 90.7 us
  Pallas kernels  35.9 us (39%)
  starting transfers between devices  34.8 us (38%)
  waiting for transfers between devices  14.8 us (16%)
  local copies, waits for them, and re-layouts  4.32 us (5%)
    pallas_call x21, Pallas kernels, call(): pl.pallas_call(kernel, name=name, out_shape=out_shape, in_specs=specs, ou...  35.9 us
    ppermute x28, starting transfers between devices, swap(): return lax.ppermute(x, axis, [(i, i ^ k) for i in range(size)])  34.8 us
    ppermute x28, waiting for transfers between devices, swap(): return lax.ppermute(x, axis, [(i, i ^ k) for i in range(size)])  14.8 us
    unnamed x18, local copies, waits for them, and re-layouts  4.32 us
  transfers between devices with their start and end apart: 28, of which 9 were waited for; matrix products, arithmetic and copies ran while one was open for 0% of the time, Pallas kernels for 34%

profile of v2, /device:TPU:0, one launch (start us, length us, event | category | flops | bytes accessed | tf_op | source)
XLA Modules:
  0.0 90.7 jit_solution(3335221221308079754)
XLA Ops:
  0.6 3.0 %collective-permute-start.1 = (s32[1,16]{1,0:T(1,128)}, s32[1,16]{1,0:T(1,128)S(1)}, u32[]{:S(2)}, u32[]{:S(2)}) collective-permute-start(s32[1,16]{1,0:T(1,128)} %refs_0_.3), channel_id=1, source_target_pairs={{0,16},{8,24},{16,0},{24,8},{1,17},{9,25},{17,1},{25,9},{2,18},{10... | collective-permute-start | bytes 200 | tf_op jit(solution)/shard_map/ppermute | solution.py:323
  3.7 0.0 collective-permute-start
  3.7 0.2 collective-permute-start.2
  3.9 2.0 %collective-permute-start.4 = (bf16[256,256]{1,0:T(8,128)(2,1)}, bf16[256,256]{1,0:T(8,128)(2,1)S(1)}, u32[]{:S(2)}, u32[]{:S(2)}) collective-permute-start(bf16[256,256]{1,0:T(8,128)(2,1)} %bitcast.22), channel_id=1, source_target_pairs={{0,2},{1,3},{2,0},{3,1},{4,6},{5,7},{6,4},{7,5},{8,10},{9,11},{10,... | collective-permute-start | bytes 393224 | tf_op jit(solution)/shard_map/ppermute | solution.py:323
  5.9 2.6 %collective-permute-start.3 = (bf16[256,256]{1,0:T(8,128)(2,1)}, bf16[256,256]{1,0:T(8,128)(2,1)S(1)}, u32[]{:S(2)}, u32[]{:S(2)}) collective-permute-start(bf16[256,256]{1,0:T(8,128)(2,1)} %bitcast.23), channel_id=1, source_target_pairs={{0,4},{1,5},{2,6},{3,7},{4,0},{5,1},{6,2},{7,3},{8,12},{9,13},{10,... | collective-permute-start | bytes 393224 | tf_op jit(solution)/shard_map/ppermute | solution.py:323
  8.5 0.9 %copy-done.1 = bf16[1,512,256]{2,1,0:T(8,128)(2,1)S(1)} copy-done((bf16[1,512,256]{2,1,0:T(8,128)(2,1)S(1)}, bf16[1,512,256]{2,1,0:T(8,128)(2,1)}, u32[]{:S(2)}) %copy-start.1) | copy-done | bytes 262168
  9.4 0.0 collective-permute-done.1.refs_2_
  9.4 0.5 collective-permute-start.10
  10.0 0.0 collective-permute-start.11
  10.0 0.0 collective-permute-done.2.refs_3_
  10.0 3.9 %collective-permute-start.12 = (bf16[4,32,256]{2,1,0:T(8,128)(2,1)S(1)}, bf16[4,32,256]{2,1,0:T(8,128)(2,1)S(1)}, u32[]{:S(2)}, u32[]{:S(2)}) collective-permute-start(bf16[4,32,256]{2,1,0:T(8,128)(2,1)S(1)} %get-tuple-element.36), channel_id=1, source_target_pairs={{0,6},{1,7},{2,4},{3,5},{4,2},{5,3},{6,0},{7,1},{8,14},{9,15},{10,... | collective-permute-start | bytes 196616 | tf_op jit(solution)/shard_map/ppermute | solution.py:323
  13.9 1.1 %copy-done = bf16[1,512,640]{2,1,0:T(8,128)(2,1)S(1)} copy-done((bf16[1,512,640]{2,1,0:T(8,128)(2,1)S(1)}, bf16[1,512,640]{2,1,0:T(8,128)(2,1)}, u32[]{:S(2)}) %copy-start) | copy-done | bytes 655384
  15.0 0.7 copy-done.3
  15.6 0.7 copy-done.5
  16.3 0.7 copy-done.6
  17.0 0.8 weight_rows.1.refs_1_.refs_2_
  17.7 0.3 copy-done.7
  18.0 0.0 copy-done.8
  18.1 1.5 %stats_own.1.refs_2_ = f32[10,8,256]{2,1,0:T(8,128)S(1)} custom-call(bf16[512,640]{1,0:T(8,128)(2,1)S(1)} %bitcast.11, bf16[512,640]{1,0:T(8,128)(2,1)S(1)} %weight_rows.1.refs_1_.refs_2_, bf16[256,256]{1,0:T(8,128)(2,1)S(1)} %bitcast.24, bf16[512,256]{1,0:T(8,128)(2,1)S(1)} %bitcast.9), custom_call_target="tpu_custom_call" | custom-call | flops 2013265920 | bytes 1703936 | tf_op jit(solution)/shard_map/stats_own/pallas_call | solution.py:33
  19.6 0.0 collective-permute-done.10.refs_1_
  19.6 1.6 %collective-permute-start.6 = (bf16[256,256]{1,0:T(8,128)(2,1)S(1)}, bf16[256,256]{1,0:T(8,128)(2,1)S(1)}, u32[]{:S(2)}, u32[]{:S(2)}) collective-permute-start(bf16[256,256]{1,0:T(8,128)(2,1)S(1)} %bitcast.25), channel_id=1, source_target_pairs={{0,1},{1,0},{2,3},{3,2},{4,5},{5,4},{6,7},{7,6},{8,9},{9,8},{10,11... | collective-permute-start | bytes 393224 | tf_op jit(solution)/shard_map/ppermute | solution.py:323
  21.2 0.6 collective-permute-start.13
  21.8 1.5 %collective-permute-start.7 = (bf16[256,256]{1,0:T(8,128)(2,1)S(1)}, bf16[256,256]{1,0:T(8,128)(2,1)S(1)}, u32[]{:S(2)}, u32[]{:S(2)}) collective-permute-start(bf16[256,256]{1,0:T(8,128)(2,1)S(1)} %collective-permute-done.3.refs_3_.refs_4_), channel_id=1, source_target_pairs={{0,1},{1,0},{2,3},{3,2},{4,5},{5,4},{6,7},{7,6},{8,9},{9,8},{10,11... | collective-permute-start | bytes 393224 | tf_op jit(solution)/shard_map/ppermute | solution.py:323
  23.3 0.0 collective-permute-start.5
  23.3 1.5 %collective-permute-start.8 = (bf16[256,256]{1,0:T(8,128)(2,1)S(1)}, bf16[256,256]{1,0:T(8,128)(2,1)S(1)}, u32[]{:S(2)}, u32[]{:S(2)}) collective-permute-start(bf16[256,256]{1,0:T(8,128)(2,1)S(1)} %collective-permute-done.4.refs_4_), channel_id=1, source_target_pairs={{0,1},{1,0},{2,3},{3,2},{4,5},{5,4},{6,7},{7,6},{8,9},{9,8},{10,11... | collective-permute-start | bytes 393224 | tf_op jit(solution)/shard_map/ppermute | solution.py:323
  24.8 1.9 %stats_prompt.3.refs_2_ = f32[10,8,256]{2,1,0:T(8,128)S(1)} custom-call(bf16[512,640]{1,0:T(8,128)(2,1)S(1)} %bitcast.12, bf16[512,640]{1,0:T(8,128)(2,1)S(1)} %weight_rows.1.refs_1_.refs_2_, f32[10,8,256]{2,1,0:T(8,128)S(1)} %stats_own.1.refs_2_, bf16[256,256]{1,0:T(8,128)(2,1)S(1)} %collective-permute-done.3.refs_3_.refs_4_, ...), custom_call_target="tpu_custom_call" | custom-call | flops 2684354560 | bytes 1654784 | tf_op jit(solution)/shard_map/stats_prompt/pallas_call | solution.py:33
  26.6 1.6 %collective-permute-done.5.refs_3_.refs_5_ = bf16[256,256]{1,0:T(8,128)(2,1)S(1)} collective-permute-done((bf16[256,256]{1,0:T(8,128)(2,1)S(1)}, bf16[256,256]{1,0:T(8,128)(2,1)S(1)}, u32[]{:S(2)}, u32[]{:S(2)}) %collective-permute-start.5) | collective-permute-done | bytes 131104 | tf_op jit(solution)/shard_map/ppermute | solution.py:323
  28.2 0.5 collective-permute-start.9
  28.8 1.9 %stats_prompt.4.refs_2_ = f32[10,8,256]{2,1,0:T(8,128)S(1)} custom-call(bf16[512,640]{1,0:T(8,128)(2,1)S(1)} %bitcast.13, bf16[512,640]{1,0:T(8,128)(2,1)S(1)} %weight_rows.1.refs_1_.refs_2_, f32[10,8,256]{2,1,0:T(8,128)S(1)} %stats_prompt.3.refs_2_, bf16[256,256]{1,0:T(8,128)(2,1)S(1)} %collective-permute-done.5.refs_3_.refs_5_, ...), custom_call_target="tpu_custom_call" | custom-call | flops 2684354560 | bytes 1654784 | tf_op jit(solution)/shard_map/stats_prompt/pallas_call | solution.py:33
  30.7 1.0 %collective-permute-done.13.other_ref = bf16[4,4,32,256]{3,2,1,0:T(8,128)(2,1)S(1)} collective-permute-done((bf16[4,4,32,256]{3,2,1,0:T(8,128)(2,1)S(1)}, bf16[4,4,32,256]{3,2,1,0:T(8,128)(2,1)S(1)}, u32[]{:S(2)}, u32[]{:S(2)}) %collective-permute-start.13) | collective-permute-done | bytes 262176 | tf_op jit(solution)/shard_map/ppermute | solution.py:323
  31.7 0.7 pairs_route.1
  32.4 0.1 collective-permute-start.14
  32.5 1.7 %collective-permute-start.15 = (bf16[4,32,256]{2,1,0:T(8,128)(2,1)S(1)}, bf16[4,32,256]{2,1,0:T(8,128)(2,1)S(1)}, u32[]{:S(2)}, u32[]{:S(2)}) collective-permute-start(bf16[4,32,256]{2,1,0:T(8,128)(2,1)S(1)} %get-tuple-element.39), channel_id=1, source_target_pairs={{0,4},{1,5},{2,6},{3,7},{4,0},{5,1},{6,2},{7,3},{8,12},{9,13},{10,... | collective-permute-start | bytes 196616 | tf_op jit(solution)/shard_map/ppermute | solution.py:323
  34.2 2.0 %collective-permute-done.8.refs_4_ = bf16[256,256]{1,0:T(8,128)(2,1)S(1)} collective-permute-done((bf16[256,256]{1,0:T(8,128)(2,1)S(1)}, bf16[256,256]{1,0:T(8,128)(2,1)S(1)}, u32[]{:S(2)}, u32[]{:S(2)}) %collective-permute-start.8) | collective-permute-done | bytes 131104 | tf_op jit(solution)/shard_map/ppermute | solution.py:323
  36.3 1.0 %collective-permute-start.16 = (bf16[4,32,256]{2,1,0:T(8,128)(2,1)S(1)}, bf16[4,32,256]{2,1,0:T(8,128)(2,1)S(1)}, u32[]{:S(2)}, u32[]{:S(2)}) collective-permute-start(bf16[4,32,256]{2,1,0:T(8,128)(2,1)S(1)} %get-tuple-element.40), channel_id=1, source_target_pairs={{0,6},{1,7},{2,4},{3,5},{4,2},{5,3},{6,0},{7,1},{8,14},{9,15},{10,... | collective-permute-start | bytes 196616 | tf_op jit(solution)/shard_map/ppermute | solution.py:323
  37.3 1.8 %stats_prompt.5.refs_3_ = f32[10,8,256]{2,1,0:T(8,128)S(1)} custom-call(bf16[512,640]{1,0:T(8,128)(2,1)S(1)} %bitcast.14, bf16[512,640]{1,0:T(8,128)(2,1)S(1)} %weight_rows.1.refs_1_.refs_2_, f32[10,8,256]{2,1,0:T(8,128)S(1)} %stats_prompt.4.refs_2_, bf16[256,256]{1,0:T(8,128)(2,1)S(1)} %collective-permute-done.7.refs_3_.refs_5_, ...), custom_call_target="tpu_custom_call" | custom-call | flops 2684354560 | bytes 1654784 | tf_op jit(solution)/shard_map/stats_prompt/pallas_call | solution.py:33
  39.1 0.6 collective-permute-done.15.refs_7_
  39.7 2.7 %collective-permute-done.16.refs_8_ = bf16[4,32,256]{2,1,0:T(8,128)(2,1)S(1)} collective-permute-done((bf16[4,32,256]{2,1,0:T(8,128)(2,1)S(1)}, bf16[4,32,256]{2,1,0:T(8,128)(2,1)S(1)}, u32[]{:S(2)}, u32[]{:S(2)}) %collective-permute-start.16) | collective-permute-done | bytes 65568 | tf_op jit(solution)/shard_map/ppermute | solution.py:323
  42.4 2.1 %stats_last.1 = (f32[10,8,256]{2,1,0:T(8,128)S(1)}, bf16[512,256]{1,0:T(8,128)(2,1)S(1)}) custom-call(s32[1,32]{1,0:T(1,128)S(1)} %copy-done.3, bf16[512,640]{1,0:T(8,128)(2,1)S(1)} %bitcast.15, bf16[512,640]{1,0:T(8,128)(2,1)S(1)} %weight_rows.1.refs_1_.refs_2_, f32[10,8,256]{2,1,0:T(8,128)S(1)} %stats_prompt.5.refs_3_, ...), custom_call_target="tpu_custom_call" | custom-call | flops 2013265920 | bytes 1785984 | tf_op jit(solution)/shard_map/stats_last/pallas_call | solution.py:33
  44.5 2.0 %grads_partner.1 = (f32[512,640]{1,0:T(8,128)S(1)}, bf16[4,32,256]{2,1,0:T(8,128)(2,1)S(1)}, bf16[4,32,256]{2,1,0:T(8,128)(2,1)S(1)}, bf16[4,32,256]{2,1,0:T(8,128)(2,1)S(1)}, bf16[4,32,256]{2,1,0:T(8,128)(2,1)S(1)}) custom-call(s32[1,32]{1,0:T(1,128)S(1)} %copy-done.3, bf16[512,640]{1,0:T(8,128)(2,1)S(1)} %bitcast.16, ...), custom_call_target="tpu_custom_call" | custom-call | flops 1677721600 | bytes 1654912 | tf_op jit(solution)/shard_map/grads_partner/pallas_call | solution.py:33
  46.5 0.1 collective-permute-start.18
  46.6 1.5 %collective-permute-start.19 = (bf16[4,32,256]{2,1,0:T(8,128)(2,1)S(1)}, bf16[4,32,256]{2,1,0:T(8,128)(2,1)S(1)}, u32[]{:S(2)}, u32[]{:S(2)}) collective-permute-start(bf16[4,32,256]{2,1,0:T(8,128)(2,1)S(1)} %get-tuple-element.53), channel_id=1, source_target_pairs={{0,4},{1,5},{2,6},{3,7},{4,0},{5,1},{6,2},{7,3},{8,12},{9,13},{10,... | collective-permute-start | bytes 196616 | tf_op jit(solution)/shard_map/ppermute | solution.py:323
  48.1 2.9 %collective-permute-start.20 = (bf16[4,32,256]{2,1,0:T(8,128)(2,1)S(1)}, bf16[4,32,256]{2,1,0:T(8,128)(2,1)S(1)}, u32[]{:S(2)}, u32[]{:S(2)}) collective-permute-start(bf16[4,32,256]{2,1,0:T(8,128)(2,1)S(1)} %get-tuple-element.54), channel_id=1, source_target_pairs={{0,6},{1,7},{2,4},{3,5},{4,2},{5,3},{6,0},{7,1},{8,14},{9,15},{10,... | collective-permute-start | bytes 196616 | tf_op jit(solution)/shard_map/ppermute | solution.py:323
  51.0 4.0 %grads_across.2 = (f32[512,640]{1,0:T(8,128)S(1)}, bf16[512,256]{1,0:T(8,128)(2,1)S(1)}) custom-call(bf16[512,640]{1,0:T(8,128)(2,1)S(1)} %bitcast.17, bf16[512,640]{1,0:T(8,128)(2,1)S(1)} %weight_rows.1.refs_1_.refs_2_, f32[10,8,256]{2,1,0:T(8,128)S(1)} %get-tuple-element.41.refs_3_.refs_2_, f32[512,640]{1,0:T(8,128)S(1)} %get-tuple-element.43.refs_3_, ...), custom_call_target="tpu_custom_call" | custom-call | flops 6710886400 | bytes 2965504 | tf_op jit(solution)/shard_map/grads_across/pallas_call | solution.py:33
  55.0 1.6 %collective-permute-start.17 = (bf16[512,256]{1,0:T(8,128)(2,1)S(1)}, bf16[512,256]{1,0:T(8,128)(2,1)S(1)}, u32[]{:S(2)}, u32[]{:S(2)}) collective-permute-start(bf16[512,256]{1,0:T(8,128)(2,1)S(1)} %get-tuple-element.46), channel_id=1, source_target_pairs={{0,1},{1,0},{2,3},{3,2},{4,5},{5,4},{6,7},{7,6},{8,9},{9,8},{10,11... | collective-permute-start | bytes 786440 | tf_op jit(solution)/shard_map/ppermute | solution.py:323
  56.5 3.8 %grads_across.3 = (f32[512,640]{1,0:T(8,128)S(1)}, bf16[512,256]{1,0:T(8,128)(2,1)S(1)}) custom-call(bf16[512,640]{1,0:T(8,128)(2,1)S(1)} %bitcast.18, bf16[512,640]{1,0:T(8,128)(2,1)S(1)} %weight_rows.1.refs_1_.refs_2_, f32[10,8,256]{2,1,0:T(8,128)S(1)} %get-tuple-element.41.refs_3_.refs_2_, f32[512,640]{1,0:T(8,128)S(1)} %get-tuple-element.44.refs_3_, ...), custom_call_target="tpu_custom_call" | custom-call | flops 6710886400 | bytes 2965504 | tf_op jit(solution)/shard_map/grads_across/pallas_call | solution.py:33
  60.3 0.6 collective-permute-start.25
  61.0 1.6 %collective-permute-start.21 = (bf16[4,4,32,256]{3,2,1,0:T(8,128)(2,1)S(1)}, bf16[4,4,32,256]{3,2,1,0:T(8,128)(2,1)S(1)}, u32[]{:S(2)}, u32[]{:S(2)}) collective-permute-start(bf16[4,4,32,256]{3,2,1,0:T(8,128)(2,1)S(1)} %terms_stack.1.mine_ref), channel_id=1, source_target_pairs={{0,1},{1,0},{2,3},{3,2},{4,5},{5,4},{6,7},{7,6},{8,9},{9,8},{10,11... | collective-permute-start | bytes 786440 | tf_op jit(solution)/shard_map/ppermute | solution.py:323
  62.5 1.7 %collective-permute-done.17.refs_6_ = bf16[512,256]{1,0:T(8,128)(2,1)S(1)} collective-permute-done((bf16[512,256]{1,0:T(8,128)(2,1)S(1)}, bf16[512,256]{1,0:T(8,128)(2,1)S(1)}, u32[]{:S(2)}, u32[]{:S(2)}) %collective-permute-start.17) | collective-permute-done | bytes 262176 | tf_op jit(solution)/shard_map/ppermute | solution.py:323
  64.2 3.8 %grads_near.1 = (f32[512,640]{1,0:T(8,128)S(1)}, bf16[512,256]{1,0:T(8,128)(2,1)S(1)}) custom-call(bf16[512,640]{1,0:T(8,128)(2,1)S(1)} %bitcast.19, bf16[512,640]{1,0:T(8,128)(2,1)S(1)} %weight_rows.1.refs_1_.refs_2_, f32[10,8,256]{2,1,0:T(8,128)S(1)} %get-tuple-element.41.refs_3_.refs_2_, f32[512,640]{1,0:T(8,128)S(1)} %get-tuple-element.45.refs_3_, ...), custom_call_target="tpu_custom_call" | custom-call | flops 6710886400 | bytes 3227648 | tf_op jit(solution)/shard_map/grads_near/pallas_call | solution.py:33
  68.0 0.1 collective-permute-start.26
  68.1 4.6 %grads_own.1 = (f32[512,640]{1,0:T(8,128)S(1)}, f32[256,256]{1,0:T(8,128)S(1)}, f32[512,256]{1,0:T(8,128)S(1)}) custom-call(bf16[512,640]{1,0:T(8,128)(2,1)S(1)} %bitcast.20, bf16[512,640]{1,0:T(8,128)(2,1)S(1)} %weight_rows.1.refs_1_.refs_2_, f32[10,8,256]{2,1,0:T(8,128)S(1)} %get-tuple-element.41.refs_3_.refs_2_, ...), custom_call_target="tpu_custom_call" | custom-call | flops 5033164800 | bytes 3096576 | tf_op jit(solution)/shard_map/grads_own/pallas_call | solution.py:33
  72.7 0.0 copy-start.4
  72.7 4.0 %grads_rest.1 = (bf16[512,640]{1,0:T(8,128)(2,1)}, f32[256,256]{1,0:T(8,128)S(1)}) custom-call(bf16[512,640]{1,0:T(8,128)(2,1)S(1)} %bitcast.21, bf16[512,640]{1,0:T(8,128)(2,1)S(1)} %weight_rows.1.refs_1_.refs_2_, f32[10,8,256]{2,1,0:T(8,128)S(1)} %get-tuple-element.41.refs_3_.refs_2_, f32[512,640]{1,0:T(8,128)S(1)} %get-tuple-element.48.refs_3_, ...), custom_call_target="tpu_custom_call" | custom-call | flops 3355443200 | bytes 2834432 | tf_op jit(solution)/shard_map/grads_rest/pallas_call | solution.py:33
  76.7 0.2 collective-permute-done.26.refs_3_
  77.0 1.4 %collective-permute-start.27 = (bf16[256,256]{1,0:T(8,128)(2,1)S(1)}, bf16[256,256]{1,0:T(8,128)(2,1)S(1)}, u32[]{:S(2)}, u32[]{:S(2)}) collective-permute-start(bf16[256,256]{1,0:T(8,128)(2,1)S(1)} %sum_far.1), channel_id=1, source_target_pairs={{0,4},{1,5},{2,6},{3,7},{4,0},{5,1},{6,2},{7,3},{8,12},{9,13},{10,... | collective-permute-start | bytes 393224 | tf_op jit(solution)/shard_map/ppermute | solution.py:323
  78.4 0.7 terms_route.1
  79.1 0.6 collective-permute-start.22
  79.7 2.9 %collective-permute-start.23 = (bf16[4,32,256]{2,1,0:T(8,128)(2,1)S(1)}, bf16[4,32,256]{2,1,0:T(8,128)(2,1)S(1)}, u32[]{:S(2)}, u32[]{:S(2)}) collective-permute-start(bf16[4,32,256]{2,1,0:T(8,128)(2,1)S(1)} %get-tuple-element.57), channel_id=1, source_target_pairs={{0,4},{1,5},{2,6},{3,7},{4,0},{5,1},{6,2},{7,3},{8,12},{9,13},{10,... | collective-permute-start | bytes 196616 | tf_op jit(solution)/shard_map/ppermute | solution.py:323
  82.6 1.0 %collective-permute-start.24 = (bf16[4,32,256]{2,1,0:T(8,128)(2,1)S(1)}, bf16[4,32,256]{2,1,0:T(8,128)(2,1)S(1)}, u32[]{:S(2)}, u32[]{:S(2)}) collective-permute-start(bf16[4,32,256]{2,1,0:T(8,128)(2,1)S(1)} %get-tuple-element.58), channel_id=1, source_target_pairs={{0,6},{1,7},{2,4},{3,5},{4,2},{5,3},{6,0},{7,1},{8,14},{9,15},{10,... | collective-permute-start | bytes 196616 | tf_op jit(solution)/shard_map/ppermute | solution.py:323
  83.6 1.4 %collective-permute-done.23.refs_2_ = bf16[4,32,256]{2,1,0:T(8,128)(2,1)S(1)} collective-permute-done((bf16[4,32,256]{2,1,0:T(8,128)(2,1)S(1)}, bf16[4,32,256]{2,1,0:T(8,128)(2,1)S(1)}, u32[]{:S(2)}, u32[]{:S(2)}) %collective-permute-start.23) | collective-permute-done | bytes 65568 | tf_op jit(solution)/shard_map/ppermute | solution.py:323
  85.0 3.6 %collective-permute-done.24.refs_3_ = bf16[4,32,256]{2,1,0:T(8,128)(2,1)S(1)} collective-permute-done((bf16[4,32,256]{2,1,0:T(8,128)(2,1)S(1)}, bf16[4,32,256]{2,1,0:T(8,128)(2,1)S(1)}, u32[]{:S(2)}, u32[]{:S(2)}) %collective-permute-start.24) | collective-permute-done | bytes 65568 | tf_op jit(solution)/shard_map/ppermute | solution.py:323
  88.6 1.3 %sum_stream.1 = bf16[512,256]{1,0:T(8,128)(2,1)} custom-call(s32[1,32]{1,0:T(1,128)S(1)} %copy-done.4, f32[512,256]{1,0:T(8,128)S(1)} %get-tuple-element.50.own_ref, bf16[4,32,256]{2,1,0:T(8,128)(2,1)S(1)} %get-tuple-element.55.refs_0_, bf16[4,32,256]{2,1,0:T(8,128)(2,1)S(1)} %collective-permute-done.22.refs_1_, ...), custom_call_target="tpu_custom_call" | custom-call | bytes 786560 | tf_op jit(solution)/shard_map/sum_stream/pallas_call | solution.py:33
  90.0 0.7 sum_prompt.1
  (31 shorter events, 0.2 us)
Async XLA Ops:
  0.6 8.8 %collective-permute-start.1 = (s32[1,16]{1,0:T(1,128)}, s32[1,16]{1,0:T(1,128)S(1)}, u32[]{:S(2)}, u32[]{:S(2)}) collective-permute-start(s32[1,16]{1,0:T(1,128)} %refs_0_.3), channel_id=1, source_target_pairs={{0,16},{8,24},{16,0},{24,8},{1,17},{9,25},{17,1},{25,9},{2,18},{10... | collective-permute-start | bytes 200 | tf_op jit(solution)/shard_map/ppermute | solution.py:323
  3.7 6.3 %collective-permute-start = (s32[1,16]{1,0:T(1,128)}, s32[1,16]{1,0:T(1,128)S(1)}, u32[]{:S(2)}, u32[]{:S(2)}) collective-permute-start(s32[1,16]{1,0:T(1,128)} %refs_0_.3), channel_id=1, source_target_pairs={{0,8},{8,0},{16,24},{24,16},{1,9},{9,1},{17,25},{25,17},{2,10},{10... | collective-permute-start | bytes 200 | tf_op jit(solution)/shard_map/ppermute | solution.py:323
  3.7 6.3 %collective-permute-start.2 = (s32[1,16]{1,0:T(1,128)}, s32[1,16]{1,0:T(1,128)S(1)}, u32[]{:S(2)}, u32[]{:S(2)}) collective-permute-start(s32[1,16]{1,0:T(1,128)} %refs_0_.3), channel_id=1, source_target_pairs={{0,24},{8,16},{16,8},{24,0},{1,25},{9,17},{17,9},{25,1},{2,26},{10... | collective-permute-start | bytes 200 | tf_op jit(solution)/shard_map/ppermute | solution.py:323
  3.9 19.4 %collective-permute-start.4 = (bf16[256,256]{1,0:T(8,128)(2,1)}, bf16[256,256]{1,0:T(8,128)(2,1)S(1)}, u32[]{:S(2)}, u32[]{:S(2)}) collective-permute-start(bf16[256,256]{1,0:T(8,128)(2,1)} %bitcast.22), channel_id=1, source_target_pairs={{0,2},{1,3},{2,0},{3,1},{4,6},{5,7},{6,4},{7,5},{8,10},{9,11},{10,... | collective-permute-start | bytes 393224 | tf_op jit(solution)/shard_map/ppermute | solution.py:323
  5.9 15.9 %collective-permute-start.3 = (bf16[256,256]{1,0:T(8,128)(2,1)}, bf16[256,256]{1,0:T(8,128)(2,1)S(1)}, u32[]{:S(2)}, u32[]{:S(2)}) collective-permute-start(bf16[256,256]{1,0:T(8,128)(2,1)} %bitcast.23), channel_id=1, source_target_pairs={{0,4},{1,5},{2,6},{3,7},{4,0},{5,1},{6,2},{7,3},{8,12},{9,13},{10,... | collective-permute-start | bytes 393224 | tf_op jit(solution)/shard_map/ppermute | solution.py:323
  8.5 0.9 %copy-start.1 = (bf16[1,512,256]{2,1,0:T(8,128)(2,1)S(1)}, bf16[1,512,256]{2,1,0:T(8,128)(2,1)}, u32[]{:S(2)}) copy-start(bf16[1,512,256]{2,1,0:T(8,128)(2,1)} %param.8) | copy-start | bytes 786436
  9.4 8.3 %copy-start.2 = (bf16[1,512,256]{2,1,0:T(8,128)(2,1)S(1)}, bf16[1,512,256]{2,1,0:T(8,128)(2,1)}, u32[]{:S(2)}) copy-start(bf16[1,512,256]{2,1,0:T(8,128)(2,1)} %param.8) | copy-start | bytes 786436
  9.4 10.1 %collective-permute-start.10 = (bf16[4,32,256]{2,1,0:T(8,128)(2,1)S(1)}, bf16[4,32,256]{2,1,0:T(8,128)(2,1)S(1)}, u32[]{:S(2)}, u32[]{:S(2)}) collective-permute-start(bf16[4,32,256]{2,1,0:T(8,128)(2,1)S(1)} %get-tuple-element.34), channel_id=1, source_target_pairs={{0,2},{1,3},{2,0},{3,1},{4,6},{5,7},{6,4},{7,5},{8,10},{9,11},{10,... | collective-permute-start | bytes 196616 | tf_op jit(solution)/shard_map/ppermute | solution.py:323
  10.0 11.2 %collective-permute-start.11 = (bf16[4,32,256]{2,1,0:T(8,128)(2,1)S(1)}, bf16[4,32,256]{2,1,0:T(8,128)(2,1)S(1)}, u32[]{:S(2)}, u32[]{:S(2)}) collective-permute-start(bf16[4,32,256]{2,1,0:T(8,128)(2,1)S(1)} %get-tuple-element.35), channel_id=1, source_target_pairs={{0,4},{1,5},{2,6},{3,7},{4,0},{5,1},{6,2},{7,3},{8,12},{9,13},{10,... | collective-permute-start | bytes 196616 | tf_op jit(solution)/shard_map/ppermute | solution.py:323
  10.0 11.2 %collective-permute-start.12 = (bf16[4,32,256]{2,1,0:T(8,128)(2,1)S(1)}, bf16[4,32,256]{2,1,0:T(8,128)(2,1)S(1)}, u32[]{:S(2)}, u32[]{:S(2)}) collective-permute-start(bf16[4,32,256]{2,1,0:T(8,128)(2,1)S(1)} %get-tuple-element.36), channel_id=1, source_target_pairs={{0,6},{1,7},{2,4},{3,5},{4,2},{5,3},{6,0},{7,1},{8,14},{9,15},{10,... | collective-permute-start | bytes 196616 | tf_op jit(solution)/shard_map/ppermute | solution.py:323
  13.9 1.1 %copy-start = (bf16[1,512,640]{2,1,0:T(8,128)(2,1)S(1)}, bf16[1,512,640]{2,1,0:T(8,128)(2,1)}, u32[]{:S(2)}) copy-start(bf16[1,512,640]{2,1,0:T(8,128)(2,1)} %param.10) | copy-start | bytes 1966084
  15.0 0.7 copy-start.3
  15.6 0.7 copy-start.5
  16.3 0.7 copy-start.6
  17.0 1.1 %copy-start.7 = (bf16[1,512,640]{2,1,0:T(8,128)(2,1)S(1)}, bf16[1,512,640]{2,1,0:T(8,128)(2,1)}, u32[]{:S(2)}) copy-start(bf16[1,512,640]{2,1,0:T(8,128)(2,1)} %param.7) | copy-start | bytes 1966084
  17.0 1.1 %copy-start.8 = (bf16[1,256,256]{2,1,0:T(8,128)(2,1)S(1)}, bf16[1,256,256]{2,1,0:T(8,128)(2,1)}, u32[]{:S(2)}) copy-start(bf16[1,256,256]{2,1,0:T(8,128)(2,1)} %param.9) | copy-start | bytes 393220
  19.6 9.2 %collective-permute-start.6 = (bf16[256,256]{1,0:T(8,128)(2,1)S(1)}, bf16[256,256]{1,0:T(8,128)(2,1)S(1)}, u32[]{:S(2)}, u32[]{:S(2)}) collective-permute-start(bf16[256,256]{1,0:T(8,128)(2,1)S(1)} %bitcast.25), channel_id=1, source_target_pairs={{0,1},{1,0},{2,3},{3,2},{4,5},{5,4},{6,7},{7,6},{8,9},{9,8},{10,11... | collective-permute-start | bytes 393224 | tf_op jit(solution)/shard_map/ppermute | solution.py:323
  21.2 10.5 %collective-permute-start.13 = (bf16[4,4,32,256]{3,2,1,0:T(8,128)(2,1)S(1)}, bf16[4,4,32,256]{3,2,1,0:T(8,128)(2,1)S(1)}, u32[]{:S(2)}, u32[]{:S(2)}) collective-permute-start(bf16[4,4,32,256]{3,2,1,0:T(8,128)(2,1)S(1)} %pairs_stack.1.mine_ref), channel_id=1, source_target_pairs={{0,1},{1,0},{2,3},{3,2},{4,5},{5,4},{6,7},{7,6},{8,9},{9,8},{10,11... | collective-permute-start | bytes 786440 | tf_op jit(solution)/shard_map/ppermute | solution.py:323
  21.8 15.5 %collective-permute-start.7 = (bf16[256,256]{1,0:T(8,128)(2,1)S(1)}, bf16[256,256]{1,0:T(8,128)(2,1)S(1)}, u32[]{:S(2)}, u32[]{:S(2)}) collective-permute-start(bf16[256,256]{1,0:T(8,128)(2,1)S(1)} %collective-permute-done.3.refs_3_.refs_4_), channel_id=1, source_target_pairs={{0,1},{1,0},{2,3},{3,2},{4,5},{5,4},{6,7},{7,6},{8,9},{9,8},{10,11... | collective-permute-start | bytes 393224 | tf_op jit(solution)/shard_map/ppermute | solution.py:323
  23.3 5.0 %collective-permute-start.5 = (bf16[256,256]{1,0:T(8,128)(2,1)S(1)}, bf16[256,256]{1,0:T(8,128)(2,1)S(1)}, u32[]{:S(2)}, u32[]{:S(2)}) collective-permute-start(bf16[256,256]{1,0:T(8,128)(2,1)S(1)} %collective-permute-done.3.refs_3_.refs_4_), channel_id=1, source_target_pairs={{0,2},{1,3},{2,0},{3,1},{4,6},{5,7},{6,4},{7,5},{8,10},{9,11},{10,... | collective-permute-start | bytes 393224 | tf_op jit(solution)/shard_map/ppermute | solution.py:323
  23.3 13.0 %collective-permute-start.8 = (bf16[256,256]{1,0:T(8,128)(2,1)S(1)}, bf16[256,256]{1,0:T(8,128)(2,1)S(1)}, u32[]{:S(2)}, u32[]{:S(2)}) collective-permute-start(bf16[256,256]{1,0:T(8,128)(2,1)S(1)} %collective-permute-done.4.refs_4_), channel_id=1, source_target_pairs={{0,1},{1,0},{2,3},{3,2},{4,5},{5,4},{6,7},{7,6},{8,9},{9,8},{10,11... | collective-permute-start | bytes 393224 | tf_op jit(solution)/shard_map/ppermute | solution.py:323
  28.2 10.9 %collective-permute-start.9 = (bf16[256,256]{1,0:T(8,128)(2,1)S(1)}, bf16[256,256]{1,0:T(8,128)(2,1)S(1)}, u32[]{:S(2)}, u32[]{:S(2)}) collective-permute-start(bf16[256,256]{1,0:T(8,128)(2,1)S(1)} %collective-permute-done.5.refs_3_.refs_5_), channel_id=1, source_target_pairs={{0,1},{1,0},{2,3},{3,2},{4,5},{5,4},{6,7},{7,6},{8,9},{9,8},{10,11... | collective-permute-start | bytes 393224 | tf_op jit(solution)/shard_map/ppermute | solution.py:323
  32.4 6.7 %collective-permute-start.14 = (bf16[4,32,256]{2,1,0:T(8,128)(2,1)S(1)}, bf16[4,32,256]{2,1,0:T(8,128)(2,1)S(1)}, u32[]{:S(2)}, u32[]{:S(2)}) collective-permute-start(bf16[4,32,256]{2,1,0:T(8,128)(2,1)S(1)} %get-tuple-element.38), channel_id=1, source_target_pairs={{0,2},{1,3},{2,0},{3,1},{4,6},{5,7},{6,4},{7,5},{8,10},{9,11},{10,... | collective-permute-start | bytes 196616 | tf_op jit(solution)/shard_map/ppermute | solution.py:323
  32.5 7.2 %collective-permute-start.15 = (bf16[4,32,256]{2,1,0:T(8,128)(2,1)S(1)}, bf16[4,32,256]{2,1,0:T(8,128)(2,1)S(1)}, u32[]{:S(2)}, u32[]{:S(2)}) collective-permute-start(bf16[4,32,256]{2,1,0:T(8,128)(2,1)S(1)} %get-tuple-element.39), channel_id=1, source_target_pairs={{0,4},{1,5},{2,6},{3,7},{4,0},{5,1},{6,2},{7,3},{8,12},{9,13},{10,... | collective-permute-start | bytes 196616 | tf_op jit(solution)/shard_map/ppermute | solution.py:323
  36.3 6.1 %collective-permute-start.16 = (bf16[4,32,256]{2,1,0:T(8,128)(2,1)S(1)}, bf16[4,32,256]{2,1,0:T(8,128)(2,1)S(1)}, u32[]{:S(2)}, u32[]{:S(2)}) collective-permute-start(bf16[4,32,256]{2,1,0:T(8,128)(2,1)S(1)} %get-tuple-element.40), channel_id=1, source_target_pairs={{0,6},{1,7},{2,4},{3,5},{4,2},{5,3},{6,0},{7,1},{8,14},{9,15},{10,... | collective-permute-start | bytes 196616 | tf_op jit(solution)/shard_map/ppermute | solution.py:323
  46.5 14.4 %collective-permute-start.18 = (bf16[4,32,256]{2,1,0:T(8,128)(2,1)S(1)}, bf16[4,32,256]{2,1,0:T(8,128)(2,1)S(1)}, u32[]{:S(2)}, u32[]{:S(2)}) collective-permute-start(bf16[4,32,256]{2,1,0:T(8,128)(2,1)S(1)} %get-tuple-element.52), channel_id=1, source_target_pairs={{0,2},{1,3},{2,0},{3,1},{4,6},{5,7},{6,4},{7,5},{8,10},{9,11},{10,... | collective-permute-start | bytes 196616 | tf_op jit(solution)/shard_map/ppermute | solution.py:323
  46.6 14.3 %collective-permute-start.19 = (bf16[4,32,256]{2,1,0:T(8,128)(2,1)S(1)}, bf16[4,32,256]{2,1,0:T(8,128)(2,1)S(1)}, u32[]{:S(2)}, u32[]{:S(2)}) collective-permute-start(bf16[4,32,256]{2,1,0:T(8,128)(2,1)S(1)} %get-tuple-element.53), channel_id=1, source_target_pairs={{0,4},{1,5},{2,6},{3,7},{4,0},{5,1},{6,2},{7,3},{8,12},{9,13},{10,... | collective-permute-start | bytes 196616 | tf_op jit(solution)/shard_map/ppermute | solution.py:323
  48.1 12.8 %collective-permute-start.20 = (bf16[4,32,256]{2,1,0:T(8,128)(2,1)S(1)}, bf16[4,32,256]{2,1,0:T(8,128)(2,1)S(1)}, u32[]{:S(2)}, u32[]{:S(2)}) collective-permute-start(bf16[4,32,256]{2,1,0:T(8,128)(2,1)S(1)} %get-tuple-element.54), channel_id=1, source_target_pairs={{0,6},{1,7},{2,4},{3,5},{4,2},{5,3},{6,0},{7,1},{8,14},{9,15},{10,... | collective-permute-start | bytes 196616 | tf_op jit(solution)/shard_map/ppermute | solution.py:323
  55.0 9.2 %collective-permute-start.17 = (bf16[512,256]{1,0:T(8,128)(2,1)S(1)}, bf16[512,256]{1,0:T(8,128)(2,1)S(1)}, u32[]{:S(2)}, u32[]{:S(2)}) collective-permute-start(bf16[512,256]{1,0:T(8,128)(2,1)S(1)} %get-tuple-element.46), channel_id=1, source_target_pairs={{0,1},{1,0},{2,3},{3,2},{4,5},{5,4},{6,7},{7,6},{8,9},{9,8},{10,11... | collective-permute-start | bytes 786440 | tf_op jit(solution)/shard_map/ppermute | solution.py:323
  60.3 16.4 %collective-permute-start.25 = (bf16[512,256]{1,0:T(8,128)(2,1)S(1)}, bf16[512,256]{1,0:T(8,128)(2,1)S(1)}, u32[]{:S(2)}, u32[]{:S(2)}) collective-permute-start(bf16[512,256]{1,0:T(8,128)(2,1)S(1)} %get-tuple-element.61), channel_id=1, source_target_pairs={{0,1},{1,0},{2,3},{3,2},{4,5},{5,4},{6,7},{7,6},{8,9},{9,8},{10,11... | collective-permute-start | bytes 786440 | tf_op jit(solution)/shard_map/ppermute | solution.py:323
  61.0 17.4 %collective-permute-start.21 = (bf16[4,4,32,256]{3,2,1,0:T(8,128)(2,1)S(1)}, bf16[4,4,32,256]{3,2,1,0:T(8,128)(2,1)S(1)}, u32[]{:S(2)}, u32[]{:S(2)}) collective-permute-start(bf16[4,4,32,256]{3,2,1,0:T(8,128)(2,1)S(1)} %terms_stack.1.mine_ref), channel_id=1, source_target_pairs={{0,1},{1,0},{2,3},{3,2},{4,5},{5,4},{6,7},{7,6},{8,9},{9,8},{10,11... | collective-permute-start | bytes 786440 | tf_op jit(solution)/shard_map/ppermute | solution.py:323
  68.0 8.9 %collective-permute-start.26 = (bf16[512,256]{1,0:T(8,128)(2,1)S(1)}, bf16[512,256]{1,0:T(8,128)(2,1)S(1)}, u32[]{:S(2)}, u32[]{:S(2)}) collective-permute-start(bf16[512,256]{1,0:T(8,128)(2,1)S(1)} %get-tuple-element.62), channel_id=1, source_target_pairs={{0,2},{1,3},{2,0},{3,1},{4,6},{5,7},{6,4},{7,5},{8,10},{9,11},{10,... | collective-permute-start | bytes 786440 | tf_op jit(solution)/shard_map/ppermute | solution.py:323
  72.7 5.7 %copy-start.4 = (s32[1,32]{1,0:T(1,128)S(1)}, s32[1,32]{1,0:T(1,128)}, u32[]{:S(2)}) copy-start(s32[1,32]{1,0:T(1,128)} %plan_ref.7) | copy-start | bytes 388
  77.0 13.0 %collective-permute-start.27 = (bf16[256,256]{1,0:T(8,128)(2,1)S(1)}, bf16[256,256]{1,0:T(8,128)(2,1)S(1)}, u32[]{:S(2)}, u32[]{:S(2)}) collective-permute-start(bf16[256,256]{1,0:T(8,128)(2,1)S(1)} %sum_far.1), channel_id=1, source_target_pairs={{0,4},{1,5},{2,6},{3,7},{4,0},{5,1},{6,2},{7,3},{8,12},{9,13},{10,... | collective-permute-start | bytes 393224 | tf_op jit(solution)/shard_map/ppermute | solution.py:323
  79.1 4.5 %collective-permute-start.22 = (bf16[4,32,256]{2,1,0:T(8,128)(2,1)S(1)}, bf16[4,32,256]{2,1,0:T(8,128)(2,1)S(1)}, u32[]{:S(2)}, u32[]{:S(2)}) collective-permute-start(bf16[4,32,256]{2,1,0:T(8,128)(2,1)S(1)} %get-tuple-element.56), channel_id=1, source_target_pairs={{0,2},{1,3},{2,0},{3,1},{4,6},{5,7},{6,4},{7,5},{8,10},{9,11},{10,... | collective-permute-start | bytes 196616 | tf_op jit(solution)/shard_map/ppermute | solution.py:323
  79.7 5.3 %collective-permute-start.23 = (bf16[4,32,256]{2,1,0:T(8,128)(2,1)S(1)}, bf16[4,32,256]{2,1,0:T(8,128)(2,1)S(1)}, u32[]{:S(2)}, u32[]{:S(2)}) collective-permute-start(bf16[4,32,256]{2,1,0:T(8,128)(2,1)S(1)} %get-tuple-element.57), channel_id=1, source_target_pairs={{0,4},{1,5},{2,6},{3,7},{4,0},{5,1},{6,2},{7,3},{8,12},{9,13},{10,... | collective-permute-start | bytes 196616 | tf_op jit(solution)/shard_map/ppermute | solution.py:323
  82.6 6.1 %collective-permute-start.24 = (bf16[4,32,256]{2,1,0:T(8,128)(2,1)S(1)}, bf16[4,32,256]{2,1,0:T(8,128)(2,1)S(1)}, u32[]{:S(2)}, u32[]{:S(2)}) collective-permute-start(bf16[4,32,256]{2,1,0:T(8,128)(2,1)S(1)} %get-tuple-element.58), channel_id=1, source_target_pairs={{0,6},{1,7},{2,4},{3,5},{4,2},{5,3},{6,0},{7,1},{8,14},{9,15},{10,... | collective-permute-start | bytes 196616 | tf_op jit(solution)/shard_map/ppermute | solution.py:323

commit v3 on v2

v3 whole, which is shorter than its diff:
```python
from functools import partial

import jax
import jax.numpy as jnp
from jax import lax
from jax.experimental import pallas as pl
from jax.experimental.pallas import tpu as pltpu
from jax.sharding import PartitionSpec as P

RESP = 16
BLK = 128
NB = 2
LOSS_SCALE = 32.0
BIG_NEGATIVE = -1e30
COVER = 7 * 10**9
LOG2E = 1.4426950408889634

F32 = jnp.float32
BF16 = jnp.bfloat16
NT = (((1,), (1,)), ((), ()))
TN = (((0,), (0,)), ((), ()))
NN = (((1,), (0,)), ((), ()))
TILE = 2 * BLK
VMEM = pl.BlockSpec(memory_space=pltpu.VMEM)
SMEM = pl.BlockSpec(memory_space=pltpu.SMEM)
ANY = pl.BlockSpec(memory_space=pl.ANY)


def dot(a, b, dims):
    return lax.dot_general(a, b, dims, preferred_element_type=F32)


def call(kernel, name, out_shape, specs, args, scratch=(), after=(), beside=False):
    specs, args = [*specs, *[ANY] * len(after)], [*args, *after]
    return pl.pallas_call(
        kernel,
        name=name,
        out_shape=out_shape,
        in_specs=specs,
        out_specs=jax.tree.map(lambda _: VMEM, out_shape),
        scratch_shapes=list(scratch),
        compiler_params=pltpu.CompilerParams(vmem_limit_bytes=24 * 2**20),
        cost_estimate=pl.CostEstimate(flops=COVER * beside, bytes_accessed=0, transcendentals=0),
    )(*args)


def write_pieces(pairs_ref, out_refs):
    line = lax.div(lax.axis_index("seq"), 2)
    rows = BLK // len(out_refs)
    for k, out_ref in enumerate(out_refs):
        first = lax.bitwise_xor(line, k) * rows
        for s in range(out_ref.shape[0]):
            place = pl.ds(pl.multiple_of(s * BLK + first, rows), rows)
            out_ref[s] = pairs_ref[place].astype(BF16)


def split_kernel(kv_ref, *out_refs):
    write_pieces(kv_ref, out_refs)


def stack_kernel(count, *refs):
    for k in range(count):
        refs[-1][k] = refs[k][...]


def pass_kernel(x_ref, after_ref, out_ref):
    out_ref[...] = x_ref[...]


def route_kernel(count, plan_ref, mine_ref, other_ref, *refs):
    outs, held, inverse = refs[len(refs) - 2 - count : -2], refs[-2], refs[-1]
    me = lax.axis_index("seq")
    line, side = lax.div(me, 2), lax.rem(me, 2)
    held[side] = mine_ref[...]
    held[1 - side] = other_ref[...]
    local = mine_ref.shape[1]
    for j in range(plan_ref.shape[1]):
        inverse[plan_ref[0, j]] = j
    for k, out_ref in enumerate(outs):
        device = lax.bitwise_xor(line, k) * 2 + side
        for s in range(local):
            partner = inverse[lax.bitwise_xor(plan_ref[0, device * local + s], 1)]
            owner = lax.div(partner, local)
            place = lax.bitwise_xor(lax.div(owner, 2), line)
            out_ref[s] = held[lax.rem(owner, 2), place, lax.rem(partner, local)]


def join_pieces(pieces, out_ref):
    line = lax.div(lax.axis_index("seq"), 2)
    rows = BLK // len(pieces)
    for k, ref in enumerate(pieces):
        first = lax.bitwise_xor(line, k) * rows
        for s in range(ref.shape[0]):
            out_ref[pl.ds(pl.multiple_of(s * BLK + first, rows), rows)] = ref[s]


def weight_kernel(groups, plan_ref, rewards_ref, lengths_ref, grad_ref, prompt_ref, out_ref, prompt_out):
    prompt_out[...] = prompt_ref[...]
    me = lax.axis_index("seq")
    local = grad_ref.shape[0] // BLK
    reward_sum = rewards_ref[0, 0]
    for r in range(1, RESP):
        reward_sum = reward_sum + rewards_ref[0, r]
    mean = reward_sum * (1.0 / RESP)
    row = lax.broadcasted_iota(jnp.int32, (BLK, 1), 0)
    for s in range(local):
        block = plan_ref[0, me * local + s]
        response = lax.div(block, NB)
        first = lax.rem(block, NB) * BLK
        scaled = (rewards_ref[0, response] - mean) * (LOSS_SCALE * groups * RESP * NB * BLK)
        weight = jnp.where(row + first < lengths_ref[0, response], scaled, 0.0)
        rows = slice(s * BLK, (s + 1) * BLK)
        out_ref[rows] = (grad_ref[rows].astype(F32) * weight).astype(BF16)


def head_tiles(q_ref):
    halves = q_ref.shape[0] // TILE
    return [
        (h * halves + r, r, slice(r * TILE, (r + 1) * TILE), slice(h * BLK, (h + 1) * BLK))
        for h in range(q_ref.shape[1] // BLK)
        for r in range(halves)
    ]


KEYS = slice(0, BLK)
VALUES = slice(BLK, 2 * BLK)


def block_rows(ref, j):
    rows = slice(j * BLK, (j + 1) * BLK)
    heads = ref.shape[1] // BLK
    return jnp.concatenate([ref[rows, h * BLK : (h + 1) * BLK] for h in range(heads)], axis=0)


def block_seen(plan_ref, j, local, heads):
    if plan_ref is None:
        key = lax.broadcasted_iota(jnp.int32, (BLK, BLK), 0)
        row = lax.broadcasted_iota(jnp.int32, (BLK, BLK), 1)
        return jnp.concatenate([key <= row] * heads, axis=1)
    me = lax.axis_index("seq")
    odd = lax.rem(plan_ref[0, me * local + j], NB)
    return jnp.full((BLK, heads * BLK), odd, jnp.int32) > 0


def merged(scale, first, second):
    peak = jnp.maximum(first[0], second[0])
    a, b = jnp.exp2((first[0] - peak) * scale), jnp.exp2((second[0] - peak) * scale)
    return peak, first[1] * a + second[1] * b, first[2] * a + second[2] * b


def score_stats(scale, s, dp):
    peak = jnp.max(s, axis=0, keepdims=True)
    e = jnp.exp2(s * scale - peak * scale)
    return peak, jnp.sum(e, axis=0, keepdims=True), jnp.sum(e * dp, axis=0, keepdims=True)


def stats_kernel(scale, shards, own, parts, carried, ordered, *refs):
    refs = list(refs)
    plan_ref = refs.pop(0) if parts else None
    q_ref, w_ref = refs.pop(0), refs.pop(0)
    before = refs.pop(0) if carried else None
    kv = [refs.pop(0) for _ in range(shards)]
    own_ref = refs.pop(0) if own else None
    pieces = [refs.pop(0) for _ in range(parts)]
    refs = refs[ordered:]
    out_ref = refs.pop(0)
    heads, local = q_ref.shape[1] // BLK, q_ref.shape[0] // BLK
    block_stats = None
    if parts:
        own_ref = refs.pop(0)
        join_pieces(pieces, own_ref)
    if own_ref is not None:
        block_stats = []
        for j in range(local):
            pairs = own_ref[j * BLK : (j + 1) * BLK]
            s = dot(pairs[:, KEYS], block_rows(q_ref, j), NT)
            dp = dot(pairs[:, VALUES], block_rows(w_ref, j), NT)
            s = jnp.where(block_seen(plan_ref, j, local, heads), s, BIG_NEGATIVE)
            block_stats.append(score_stats(scale, s, dp))
    for t, r, rows, cols in head_tiles(q_ref):
        q, w = q_ref[rows, cols], w_ref[rows, cols]
        state = None
        if carried:
            state = tuple(before[t, i : i + 1] for i in range(3))
        if block_stats is not None:
            pair = block_stats[2 * r : 2 * r + 2]
            more = tuple(jnp.concatenate([x[i][:, cols] for x in pair], axis=1) for i in range(3))
            state = more if state is None else merged(scale, state, more)
        for ref in kv:
            s, dp = dot(ref[:, KEYS], q, NT), dot(ref[:, VALUES], w, NT)
            if state is None:
                state = score_stats(scale, s, dp)
                continue
            m, l, d = state
            peak = jnp.maximum(m, jnp.max(s, axis=0, keepdims=True))
            shrink = jnp.exp2((m - peak) * scale)
            e = jnp.exp2(s * scale - peak * scale)
            l = l * shrink + jnp.sum(e, axis=0, keepdims=True)
            d = d * shrink + jnp.sum(e * dp, axis=0, keepdims=True)
            state = peak, l, d
        for i in range(3):
            out_ref[t, i : i + 1] = state[i]


def grad_kernel(scale, shards, own, partner, carried, ordered, *refs):
    refs = list(refs)
    plan_ref = refs.pop(0) if partner else None
    q_ref, w_ref, stats_ref = refs.pop(0), refs.pop(0), refs.pop(0)
    before = refs.pop(0) if carried else None
    kv = [refs.pop(0) for _ in range(shards)]
    blocks_ref = refs.pop(0) if own or partner else None
    refs = refs[ordered:]
    dq_ref = refs.pop(0)
    kv_out = refs.pop(0) if shards else None
    kv_sum = refs.pop() if shards else None
    if partner:
        blocks_out, blocks_sum = refs[:partner], refs[partner]
    elif own:
        blocks_sum = refs[0]
    heads, local = q_ref.shape[1] // BLK, q_ref.shape[0] // BLK
    halves = q_ref.shape[0] // TILE
    back = scale / LOG2E

    def factors(rows):
        inverse = 1.0 / rows[1]
        return rows[0] * scale, inverse, rows[2] * inverse

    def grads(s, dp, rows):
        peak, inverse, delta = rows
        p = jnp.exp2(s * scale - peak) * inverse
        return p.astype(BF16), (p * (dp - delta)).astype(BF16)

    def add_queries(dq, rows, cols):
        if carried:
            dq = dq + before[rows, cols]
        dq_ref[rows, cols] = dq

    if blocks_ref is not None:
        for j in range(local):
            place = slice(j * BLK, (j + 1) * BLK)
            lanes = slice((j % 2) * BLK, (j % 2 + 1) * BLK)
            rows = [
                jnp.concatenate(
                    [stats_ref[h * halves + j // 2, i : i + 1, lanes] for h in range(heads)], axis=1
                )
                for i in range(3)
            ]
            q, w = block_rows(q_ref, j), block_rows(w_ref, j)
            keys = blocks_ref[place, KEYS]
            s = jnp.where(block_seen(plan_ref, j, local, heads), dot(keys, q, NT), BIG_NEGATIVE)
            p, ds = grads(s, dot(blocks_ref[place, VALUES], w, NT), factors(rows))
            blocks_sum[place, KEYS] = dot(ds, q, NN) * back
            blocks_sum[place, VALUES] = dot(p, w, NN)
            dq = dot(ds, keys, TN)
            for h in range(heads):
                cols = slice(h * BLK, (h + 1) * BLK)
                add_queries(dq[cols], place, cols)
        if partner:
            write_pieces(blocks_sum, blocks_out)
    if not shards:
        return
    keys = jnp.concatenate([ref[:, KEYS] for ref in kv], axis=0)
    values = jnp.concatenate([ref[:, VALUES] for ref in kv], axis=0)
    for t, r, rows, cols in head_tiles(q_ref):
        q, w = q_ref[rows, cols], w_ref[rows, cols]
        state = factors([stats_ref[t, i : i + 1] for i in range(3)])
        p, ds = grads(dot(keys, q, NT), dot(values, w, NT), state)
        dk, dv = dot(ds, q, NN), dot(p, w, NN)
        if t == 0:
            kv_sum[:, KEYS] = dk
            kv_sum[:, VALUES] = dv
        else:
            kv_sum[:, KEYS] += dk
            kv_sum[:, VALUES] += dv
        add_queries(dot(ds, keys, TN), rows, cols)
    for side, factor in ((KEYS, back), (VALUES, 1.0)):
        kv_out[:, side] = (kv_sum[:, side] * factor).astype(kv_out.dtype)


def join_kernel(count, plan_ref, *refs):
    pieces, out_ref = refs[:count], refs[-1]
    me = lax.axis_index("seq")
    join_pieces(pieces, out_ref)
    local = out_ref.shape[0] // BLK
    for s in range(local):
        rows = slice(s * BLK, (s + 1) * BLK)
        odd = lax.rem(plan_ref[0, me * local + s], NB)
        odd_rows = jnp.full((BLK, 2 * BLK), odd, jnp.int32) > 0
        out_ref[rows] = jnp.where(odd_rows, 0.0, out_ref[rows].astype(F32)).astype(BF16)


def finish_kernel(groups, back, *refs):
    total = jnp.int32(0)
    for ref in refs[:groups]:
        for r in range(RESP):
            total = total + ref[0, r]
    share = 1.0 / jnp.full((1, BLK), total.astype(F32))
    dq_ref, own_ref, back_ref, prompt_ref, dq_out, stream_out, prompt_out = refs[groups:]
    for h in range(dq_ref.shape[1] // BLK):
        cols = slice(h * BLK, (h + 1) * BLK)
        dq_out[:, cols] = (dq_ref[:, cols] * (share * back)).astype(BF16)
    for cols in (KEYS, VALUES):
        stream = own_ref[:, cols] + back_ref[:, cols].astype(F32)
        stream_out[:, cols] = (stream * share).astype(BF16)
        prompt_out[:, cols] = (prompt_ref[:, cols] * share).astype(BF16)


def pick_kernel(per, parts, picked, ordered, *refs):
    out_ref, refs = refs[-1], refs[: len(refs) - 1 - ordered]
    where = []
    for ref in refs[:parts]:
        where += [(ref, i) for i in range(ref.shape[0] // per)]
    for n, i in enumerate(picked):
        ref, at = where[i]
        total = ref[at * per : (at + 1) * per].astype(F32)
        for other in refs[parts:]:
            total = total + other[i * per : (i + 1) * per].astype(F32)
        out_ref[n * per : (n + 1) * per] = total.astype(out_ref.dtype)


def local(query, resp_kv, prompt_kv, grad_out, rewards, lengths, block_order):
    groups = lax.axis_size("grp")
    count = lax.axis_size("seq")
    q, resp, prompt, grad = query[0], resp_kv[0], prompt_kv[0], grad_out[0]
    rows, width = resp.shape
    blocks = rows // BLK
    heads = q.shape[1] // BLK
    line = count // 2
    scale = LOG2E * BLK**-0.5
    piece = jax.ShapeDtypeStruct((blocks, BLK // line, width), BF16)
    stack = jax.ShapeDtypeStruct((line, *piece.shape), BF16)

    def swap(x, axis, k):
        size = lax.axis_size(axis)
        return lax.ppermute(x, axis, [(i, i ^ k) for i in range(size)])

    def along(sent):
        return [sent[0]] + [swap(sent[k], "seq", 2 * k) for k in range(1, line)]

    def gather_line(name, sent, after=()):
        body = partial(stack_kernel, line)
        return call(body, name, stack, [VMEM] * line, along(sent), after=after)

    def deliver(name, mine, after=()):
        other = swap(mine, "seq", 1)
        return call(
            partial(route_kernel, line),
            name + "_route",
            [piece] * line,
            [SMEM, VMEM, VMEM],
            [block_order, mine, other],
            [pltpu.VMEM((2, *stack.shape), BF16), pltpu.SMEM((block_order.shape[1],), jnp.int32)],
            after=after,
        )

    pieces = call(split_kernel, "pairs_split", [piece] * line, [VMEM], [resp])
    weighted, prompt_on = call(
        partial(weight_kernel, groups),
        "weight_rows",
        [jax.ShapeDtypeStruct(grad.shape, BF16), jax.ShapeDtypeStruct(prompt.shape, BF16)],
        [SMEM, SMEM, SMEM, VMEM, VMEM],
        [block_order, rewards, lengths, grad, prompt],
    )
    mine = gather_line("pairs_stack", pieces, after=[weighted])
    stats_shape = jax.ShapeDtypeStruct((heads * rows // TILE, 8, TILE), F32)

    def stats(name, before, kv, own=None, parts=(), after=(), beside=False):
        args = [block_order] if parts else []
        specs = [SMEM] * len(args)
        args += [q, weighted] + ([before] if before is not None else []) + list(kv)
        args += ([own] if own is not None else []) + list(parts)
        specs += [VMEM] * (len(args) - len(specs))
        out = [stats_shape]
        if parts:
            out.append(jax.ShapeDtypeStruct(resp.shape, BF16))
        body = partial(
            stats_kernel,
            scale,
            len(kv),
            own is not None,
            len(parts),
            before is not None,
            len(after),
        )
        return call(body, name, out, specs, args, after=after, beside=beside)

    (state,) = stats("stats_own", None, [prompt_on], own=resp, after=[mine])
    routed = deliver("pairs", mine, after=[state])
    arrived = along(routed)

    def held_back(x, after):
        same = jax.ShapeDtypeStruct(x.shape, x.dtype)
        return call(pass_kernel, "pass_on", same, [VMEM], [x], after=[after])

    column = {0: prompt_on}
    bit = count // 2
    while bit > 1:
        column.update({k ^ bit: swap(x, "seq", bit) for k, x in column.items()})
        if bit == count // 2 or bit == 2:
            column[bit] = held_back(column[bit], state)
        bit //= 2
    early = [k for k in column if not k & 2 or k == 2]
    late = [k for k in column if k not in early]
    across = {k: swap(column[k], "seq", 1) for k in early}
    coming = [x for k, x in column.items() if k] + [across[k] for k in early]
    (state,) = stats("stats_prompt", state, coming[:2], after=[routed[0]])
    across.update({k: swap(held_back(column[k], state), "seq", 1) for k in late})
    coming = coming[2:]
    while len(coming) > 2:
        (state,) = stats("stats_prompt", state, coming[:2])
        coming = coming[2:]
    state, partner = stats("stats_partner", state, coming, parts=arrived, beside=True)
    (state,) = stats("stats_last", state, [across[k] for k in late])

    def grads(name, before, kv, own=None, part=None, kind=BF16, after=(), beside=False):
        args = [block_order] if part is not None else []
        specs = [SMEM] * len(args)
        args += [q, weighted, state] + ([before] if before is not None else [])
        args += list(kv) + [x for x in (own, part) if x is not None]
        specs += [VMEM] * (len(args) - len(specs))
        keys = sum(x.shape[0] for x in kv)
        out = [jax.ShapeDtypeStruct(q.shape, F32)]
        out += [jax.ShapeDtypeStruct((keys, width), kind)] if kv else []
        scratch = [pltpu.VMEM((keys, width), F32)] if kv else []
        if own is not None:
            out.append(jax.ShapeDtypeStruct(resp.shape, F32))
        if part is not None:
            out += [piece] * line
            scratch.append(pltpu.VMEM(resp.shape, F32))
        body = partial(
            grad_kernel,
            scale,
            len(kv),
            own is not None,
            line if part is not None else 0,
            before is not None,
            len(after),
        )
        return call(body, name, out, specs, args, scratch, after=after, beside=beside)

    per = prompt.shape[0]

    def pick(name, parts, extra, picked, kind, after=(), beside=False):
        args = [*parts, *extra]
        return call(
            partial(pick_kernel, per, len(parts), tuple(picked), len(after)),
            name,
            jax.ShapeDtypeStruct((per * len(picked), width), kind),
            [VMEM] * len(args),
            args,
            after=after,
            beside=beside,
        )

    near = [k for k in column if k & 2]
    rest = [k for k in column if not k & 2]
    dq, *terms = grads("grads_partner", None, [], part=partner)
    dq, far_near = grads("grads_across", dq, [across[k] for k in near])
    mine = gather_line("terms_stack", terms, after=[far_near])
    far_near = swap(far_near, "seq", 1)
    dq, sums = grads("grads_near", dq, [column[k] for k in near], kind=F32, after=[mine], beside=True)
    dq, far_rest = grads("grads_across", dq, [across[k] for k in rest])
    sums = pick("sum_near", [sums], [far_near], range(len(near)), BF16, after=[far_rest])
    far_rest = swap(far_rest, "seq", 1)
    dq, sent = grads("grads_rest", dq, [column[k] for k in rest], kind=F32, after=[sums])
    sums = swap(sums, "seq", 2)
    routed = deliver("terms", mine, after=[sent])
    returned = along(routed)
    sums_on = call(
        pass_kernel,
        "pass_sums",
        jax.ShapeDtypeStruct(sums.shape, BF16),
        [VMEM],
        [sums],
        after=[routed[0]],
        beside=True,
    )
    held, parts, extra, order = rest, [sent], [far_rest, sums_on], []
    bit = 4
    while bit < count:
        keep = [i for i, k in enumerate(held) if not k & bit]
        send = [i for i, k in enumerate(held) if k & bit]
        leaving = pick("sum_far", parts, extra, send, BF16, after=order)
        kept = pick("sum_kept", parts, extra, keep, F32)
        held, parts, extra, order = [held[i] for i in keep], [kept], [swap(leaving, "seq", bit)], []
        if bit == 4:
            dq, own_terms = grads("grads_own", dq, [], own=resp, after=[leaving], beside=False)
            lengths_on = call(
                pass_kernel,
                "pass_lengths",
                jax.ShapeDtypeStruct(lengths.shape, jnp.int32),
                [VMEM],
                [lengths],
                after=[own_terms],
            )
            joined = call(
                partial(join_kernel, line),
                "join_terms",
                jax.ShapeDtypeStruct(resp.shape, BF16),
                [SMEM] + [VMEM] * line,
                [block_order, *returned],
                after=[own_terms],
            )
        bit *= 2
    lengths_all = [lengths] + [swap(lengths_on, "grp", k) for k in range(1, groups)]
    prompt_sum = pick("sum_prompt", parts, extra, [0], F32, after=[joined], beside=True)
    grad_query, grad_stream, grad_prompt = call(
        partial(finish_kernel, groups, scale / LOG2E),
        "over_count",
        [jax.ShapeDtypeStruct(x.shape, BF16) for x in (q, resp, prompt)],
        [SMEM] * groups + [VMEM] * 4,
        [*lengths_all, dq, own_terms, joined, prompt_sum],
    )
    return grad_query[None], grad_stream[None], grad_prompt[None]


def solution(mesh):
    in_specs = (
        P("grp", "seq", None),
        P("grp", "seq", None),
        P("grp", "seq", None),
        P("grp", "seq", None),
        P("grp", None),
        P("grp", None),
        P("grp", None),
    )
    out_specs = (P("grp", "seq", None), P("grp", "seq", None), P("grp", "seq", None))
    return jax.shard_map(local, mesh=mesh, in_specs=in_specs, out_specs=out_specs, check_vma=False)
```

time: 90.9 us -> 81.2 us (0.89)
  waiting for transfers between devices: 14.8 us -> 10.6 us
  Pallas kernels: 35.9 us -> 32.7 us
  starting transfers between devices: 34.8 us -> 31.6 us
    ppermute x28, waiting for transfers between devices: 14.8 us -> 10.6 us  [swap(): return lax.ppermute(x, axis, [(i, i ^ k) for i in range(size)])]
    pallas_call x21 -> x28, Pallas kernels: 35.9 us -> 32.7 us  [call(): pl.pallas_call(kernel, name=name, out_shape=out_shape, in_specs=specs, ou...]
    ppermute x28, starting transfers between devices: 34.8 us -> 31.6 us  [swap(): return lax.ppermute(x, axis, [(i, i ^ k) for i in range(size)])]
    unnamed x18 -> x20, local copies, waits for them, and re-layouts: 4.32 us -> 4.98 us
  transfers between devices with their start and end apart: 28 -> 28, of which waited for: 9 -> 8; matrix products, arithmetic and copies ran while one was open for 0% -> 0% of each run, Pallas kernels for 34% -> 35%
where the time goes in v3:
time: 81.2 us; the launch traced here: 80.9 us
  Pallas kernels  32.7 us (40%)
  starting transfers between devices  31.6 us (39%)
  waiting for transfers between devices  10.6 us (13%)
  local copies, waits for them, and re-layouts  4.98 us (6%)
  between operations  0.97 us (1%)
    pallas_call x28, Pallas kernels, call(): pl.pallas_call(kernel, name=name, out_shape=out_shape, in_specs=specs, ou...  32.7 us
    ppermute x28, starting transfers between devices, swap(): return lax.ppermute(x, axis, [(i, i ^ k) for i in range(size)])  31.6 us
    ppermute x28, waiting for transfers between devices, swap(): return lax.ppermute(x, axis, [(i, i ^ k) for i in range(size)])  10.6 us
    unnamed x20, local copies, waits for them, and re-layouts  4.98 us
  transfers between devices with their start and end apart: 28, of which 8 were waited for; matrix products, arithmetic and copies ran while one was open for 0% of the time, Pallas kernels for 35%

profile of v3, /device:TPU:0, one launch (start us, length us, event | category | flops | bytes accessed | tf_op | source)
XLA Modules:
  0.0 80.9 jit_solution(6771754624978667266)
XLA Ops:
  0.6 1.0 %copy-done.1 = bf16[1,512,256]{2,1,0:T(8,128)(2,1)S(1)} copy-done((bf16[1,512,256]{2,1,0:T(8,128)(2,1)S(1)}, bf16[1,512,256]{2,1,0:T(8,128)(2,1)}, u32[]{:S(2)}) %copy-start.1) | copy-done | bytes 262168
  1.7 3.1 %collective-permute-start = (bf16[4,32,256]{2,1,0:T(8,128)(2,1)S(1)}, bf16[4,32,256]{2,1,0:T(8,128)(2,1)S(1)}, u32[]{:S(2)}, u32[]{:S(2)}) collective-permute-start(bf16[4,32,256]{2,1,0:T(8,128)(2,1)S(1)} %get-tuple-element.40), channel_id=1, source_target_pairs={{0,2},{1,3},{2,0},{3,1},{4,6},{5,7},{6,4},{7,5},{8,10},{9,11},{10,... | collective-permute-start | bytes 196616 | tf_op jit(solution)/shard_map/ppermute | solution.py:335
  4.8 2.6 %collective-permute-start.1 = (bf16[4,32,256]{2,1,0:T(8,128)(2,1)S(1)}, bf16[4,32,256]{2,1,0:T(8,128)(2,1)S(1)}, u32[]{:S(2)}, u32[]{:S(2)}) collective-permute-start(bf16[4,32,256]{2,1,0:T(8,128)(2,1)S(1)} %get-tuple-element.41), channel_id=1, source_target_pairs={{0,4},{1,5},{2,6},{3,7},{4,0},{5,1},{6,2},{7,3},{8,12},{9,13},{10,... | collective-permute-start | bytes 196616 | tf_op jit(solution)/shard_map/ppermute | solution.py:335
  7.4 0.0 collective-permute-start.2
  7.4 1.1 %copy-done.3 = bf16[1,512,640]{2,1,0:T(8,128)(2,1)S(1)} copy-done((bf16[1,512,640]{2,1,0:T(8,128)(2,1)S(1)}, bf16[1,512,640]{2,1,0:T(8,128)(2,1)}, u32[]{:S(2)}) %copy-start.3) | copy-done | bytes 655384
  8.5 0.9 %copy-done.4 = bf16[1,256,256]{2,1,0:T(8,128)(2,1)S(1)} copy-done((bf16[1,256,256]{2,1,0:T(8,128)(2,1)S(1)}, bf16[1,256,256]{2,1,0:T(8,128)(2,1)}, u32[]{:S(2)}) %copy-start.4) | copy-done | bytes 131096
  9.4 0.7 copy-done.5
  10.0 0.7 copy-done.7
  10.7 0.7 copy-done.9
  11.3 0.7 weight_rows.1
  12.1 0.0 collective-permute-done.1.refs_2_
  12.1 1.4 %collective-permute-done.2.refs_3_ = bf16[4,32,256]{2,1,0:T(8,128)(2,1)S(1)} collective-permute-done((bf16[4,32,256]{2,1,0:T(8,128)(2,1)S(1)}, bf16[4,32,256]{2,1,0:T(8,128)(2,1)S(1)}, u32[]{:S(2)}, u32[]{:S(2)}) %collective-permute-start.2) | collective-permute-done | bytes 65568 | tf_op jit(solution)/shard_map/ppermute | solution.py:335
  13.5 1.6 %collective-permute-start.5 = (bf16[4,4,32,256]{3,2,1,0:T(8,128)(2,1)S(1)}, bf16[4,4,32,256]{3,2,1,0:T(8,128)(2,1)S(1)}, u32[]{:S(2)}, u32[]{:S(2)}) collective-permute-start(bf16[4,4,32,256]{3,2,1,0:T(8,128)(2,1)S(1)} %pairs_stack.1.refs_4_.mine_ref), channel_id=1, source_target_pairs={{0,1},{1,0},{2,3},{3,2},{4,5},{5,4},{6,7},{7,6},{8,9},{9,8},{10,11... | collective-permute-start | bytes 786440 | tf_op jit(solution)/shard_map/ppermute | solution.py:335
  15.0 1.6 %collective-permute-start.3 = (bf16[256,256]{1,0:T(8,128)(2,1)S(1)}, bf16[256,256]{1,0:T(8,128)(2,1)S(1)}, u32[]{:S(2)}, u32[]{:S(2)}) collective-permute-start(bf16[256,256]{1,0:T(8,128)(2,1)S(1)} %get-tuple-element.38.refs_2_.refs_4_), channel_id=1, source_target_pairs={{0,4},{1,5},{2,6},{3,7},{4,0},{5,1},{6,2},{7,3},{8,12},{9,13},{10,... | collective-permute-start | bytes 393224 | tf_op jit(solution)/shard_map/ppermute | solution.py:335
  16.6 1.5 %collective-permute-start.4 = (bf16[256,256]{1,0:T(8,128)(2,1)S(1)}, bf16[256,256]{1,0:T(8,128)(2,1)S(1)}, u32[]{:S(2)}, u32[]{:S(2)}) collective-permute-start(bf16[256,256]{1,0:T(8,128)(2,1)S(1)} %get-tuple-element.38.refs_2_.refs_4_), channel_id=1, source_target_pairs={{0,2},{1,3},{2,0},{3,1},{4,6},{5,7},{6,4},{7,5},{8,10},{9,11},{10,... | collective-permute-start | bytes 393224 | tf_op jit(solution)/shard_map/ppermute | solution.py:335
  18.0 0.5 collective-permute-start.7
  18.6 1.5 %stats_own.1.after_ref.refs_0_.refs_2_ = f32[10,8,256]{2,1,0:T(8,128)S(1)} custom-call(bf16[512,640]{1,0:T(8,128)(2,1)S(1)} %bitcast.7, bf16[512,640]{1,0:T(8,128)(2,1)S(1)} %get-tuple-element.37.refs_4_.refs_1_.refs_2_, bf16[256,256]{1,0:T(8,128)(2,1)S(1)} %get-tuple-element.38.refs_2_.refs_4_, bf16[512,256]{1,0:T(8,128)(2,1)S(1)} %bitcast.19, ...), custom_call_target="tpu_custom_call" | custom-call | tf_op jit(solution)/shard_map/stats_own/pallas_call | solution.py:35
  20.1 2.1 %collective-permute-done.3.x_ref = bf16[256,256]{1,0:T(8,128)(2,1)S(1)} collective-permute-done((bf16[256,256]{1,0:T(8,128)(2,1)S(1)}, bf16[256,256]{1,0:T(8,128)(2,1)S(1)}, u32[]{:S(2)}, u32[]{:S(2)}) %collective-permute-start.3) | collective-permute-done | bytes 131104 | tf_op jit(solution)/shard_map/ppermute | solution.py:335
  22.2 0.1 collective-permute-start.6
  22.3 0.7 collective-permute-done.4.x_ref
  23.0 0.6 collective-permute-start.9
  23.6 1.5 %collective-permute-start.8 = (bf16[256,256]{1,0:T(8,128)(2,1)S(1)}, bf16[256,256]{1,0:T(8,128)(2,1)S(1)}, u32[]{:S(2)}, u32[]{:S(2)}) collective-permute-start(bf16[256,256]{1,0:T(8,128)(2,1)S(1)} %pass_on.3.refs_3_.refs_5_), channel_id=1, source_target_pairs={{0,1},{1,0},{2,3},{3,2},{4,5},{5,4},{6,7},{7,6},{8,9},{9,8},{10,11... | collective-permute-start | bytes 393224 | tf_op jit(solution)/shard_map/ppermute | solution.py:335
  25.1 0.7 pairs_route.1
  25.8 1.5 %collective-permute-start.10 = (bf16[4,32,256]{2,1,0:T(8,128)(2,1)S(1)}, bf16[4,32,256]{2,1,0:T(8,128)(2,1)S(1)}, u32[]{:S(2)}, u32[]{:S(2)}) collective-permute-start(bf16[4,32,256]{2,1,0:T(8,128)(2,1)S(1)} %get-tuple-element.44), channel_id=1, source_target_pairs={{0,2},{1,3},{2,0},{3,1},{4,6},{5,7},{6,4},{7,5},{8,10},{9,11},{10,... | collective-permute-start | bytes 196616 | tf_op jit(solution)/shard_map/ppermute | solution.py:335
  27.3 1.3 %collective-permute-start.11 = (bf16[4,32,256]{2,1,0:T(8,128)(2,1)S(1)}, bf16[4,32,256]{2,1,0:T(8,128)(2,1)S(1)}, u32[]{:S(2)}, u32[]{:S(2)}) collective-permute-start(bf16[4,32,256]{2,1,0:T(8,128)(2,1)S(1)} %get-tuple-element.45), channel_id=1, source_target_pairs={{0,4},{1,5},{2,6},{3,7},{4,0},{5,1},{6,2},{7,3},{8,12},{9,13},{10,... | collective-permute-start | bytes 196616 | tf_op jit(solution)/shard_map/ppermute | solution.py:335
  28.6 1.7 %collective-permute-start.12 = (bf16[4,32,256]{2,1,0:T(8,128)(2,1)S(1)}, bf16[4,32,256]{2,1,0:T(8,128)(2,1)S(1)}, u32[]{:S(2)}, u32[]{:S(2)}) collective-permute-start(bf16[4,32,256]{2,1,0:T(8,128)(2,1)S(1)} %get-tuple-element.46), channel_id=1, source_target_pairs={{0,6},{1,7},{2,4},{3,5},{4,2},{5,3},{6,0},{7,1},{8,14},{9,15},{10,... | collective-permute-start | bytes 196616 | tf_op jit(solution)/shard_map/ppermute | solution.py:335
  30.3 1.8 %stats_prompt.2.refs_2_.after_ref = f32[10,8,256]{2,1,0:T(8,128)S(1)} custom-call(bf16[512,640]{1,0:T(8,128)(2,1)S(1)} %bitcast.8, bf16[512,640]{1,0:T(8,128)(2,1)S(1)} %get-tuple-element.37.refs_4_.refs_1_.refs_2_, f32[10,8,256]{2,1,0:T(8,128)S(1)} %stats_own.1.after_ref.refs_0_.refs_2_, bf16[256,256]{1,0:T(8,128)(2,1)S(1)} %pass_on.3.refs_3_.refs_5_, ...), custom_call_target="tpu_custom_call" | custom-call | tf_op jit(solution)/shard_map/stats_prompt/pallas_call | solution.py:35
  32.1 0.0 copy-start.6
  32.1 1.8 %stats_prompt.3.refs_3_ = f32[10,8,256]{2,1,0:T(8,128)S(1)} custom-call(bf16[512,640]{1,0:T(8,128)(2,1)S(1)} %bitcast.9, bf16[512,640]{1,0:T(8,128)(2,1)S(1)} %get-tuple-element.37.refs_4_.refs_1_.refs_2_, f32[10,8,256]{2,1,0:T(8,128)S(1)} %stats_prompt.2.refs_2_.after_ref, bf16[256,256]{1,0:T(8,128)(2,1)S(1)} %collective-permute-done.6.refs_3_.x_ref.refs_5_, ...), custom_call_target="tpu_custom_call" | custom-call | tf_op jit(solution)/shard_map/stats_prompt/pallas_call | solution.py:35
  33.9 0.0 collective-permute-done.9.refs_5_.refs_4_
  34.0 0.6 collective-permute-start.13
  34.6 0.0 collective-permute-done.8.refs_4_.refs_5_
  34.6 0.0 collective-permute-done.10.refs_7_
  34.6 0.2 collective-permute-done.12.refs_9_
  34.8 2.9 %stats_partner.1 = (f32[10,8,256]{2,1,0:T(8,128)S(1)}, bf16[512,256]{1,0:T(8,128)(2,1)S(1)}) custom-call(s32[1,32]{1,0:T(1,128)S(1)} %copy-done.6, bf16[512,640]{1,0:T(8,128)(2,1)S(1)} %bitcast.10, bf16[512,640]{1,0:T(8,128)(2,1)S(1)} %get-tuple-element.37.refs_4_.refs_1_.refs_2_, f32[10,8,256]{2,1,0:T(8,128)S(1)} %stats_prompt.3.refs_3_, ...), custom_call_target="tpu_custom_call" | custom-call | flops 7000000000 | tf_op jit(solution)/shard_map/stats_partner/pallas_call | solution.py:35
  37.7 1.3 %collective-permute-done.13.refs_3_.refs_5_ = bf16[256,256]{1,0:T(8,128)(2,1)S(1)} collective-permute-done((bf16[256,256]{1,0:T(8,128)(2,1)S(1)}, bf16[256,256]{1,0:T(8,128)(2,1)S(1)}, u32[]{:S(2)}, u32[]{:S(2)}) %collective-permute-start.13) | collective-permute-done | bytes 131104 | tf_op jit(solution)/shard_map/ppermute | solution.py:335
  39.0 1.0 %stats_last.1.refs_3_.refs_2_ = f32[10,8,256]{2,1,0:T(8,128)S(1)} custom-call(bf16[512,640]{1,0:T(8,128)(2,1)S(1)} %bitcast.11, bf16[512,640]{1,0:T(8,128)(2,1)S(1)} %get-tuple-element.37.refs_4_.refs_1_.refs_2_, f32[10,8,256]{2,1,0:T(8,128)S(1)} %get-tuple-element.47.refs_2_, bf16[256,256]{1,0:T(8,128)(2,1)S(1)} %collective-permute-done.13.refs_3_.refs_5_), custom_call_target="tpu_custom_call" | custom-call | tf_op jit(solution)/shard_map/stats_last/pallas_call | solution.py:35
  40.0 2.0 %grads_partner.1 = (f32[512,640]{1,0:T(8,128)S(1)}, bf16[4,32,256]{2,1,0:T(8,128)(2,1)S(1)}, bf16[4,32,256]{2,1,0:T(8,128)(2,1)S(1)}, bf16[4,32,256]{2,1,0:T(8,128)(2,1)S(1)}, bf16[4,32,256]{2,1,0:T(8,128)(2,1)S(1)}) custom-call(s32[1,32]{1,0:T(1,128)S(1)} %copy-done.6, bf16[512,640]{1,0:T(8,128)(2,1)S(1)} %bitcast.12, ...), custom_call_target="tpu_custom_call" | custom-call | tf_op jit(solution)/shard_map/grads_partner/pallas_call | solution.py:35
  42.0 0.6 collective-permute-start.14
  42.6 2.2 %collective-permute-start.15 = (bf16[4,32,256]{2,1,0:T(8,128)(2,1)S(1)}, bf16[4,32,256]{2,1,0:T(8,128)(2,1)S(1)}, u32[]{:S(2)}, u32[]{:S(2)}) collective-permute-start(bf16[4,32,256]{2,1,0:T(8,128)(2,1)S(1)} %get-tuple-element.53), channel_id=1, source_target_pairs={{0,4},{1,5},{2,6},{3,7},{4,0},{5,1},{6,2},{7,3},{8,12},{9,13},{10,... | collective-permute-start | bytes 196616 | tf_op jit(solution)/shard_map/ppermute | solution.py:335
  44.8 1.7 %collective-permute-start.16 = (bf16[4,32,256]{2,1,0:T(8,128)(2,1)S(1)}, bf16[4,32,256]{2,1,0:T(8,128)(2,1)S(1)}, u32[]{:S(2)}, u32[]{:S(2)}) collective-permute-start(bf16[4,32,256]{2,1,0:T(8,128)(2,1)S(1)} %get-tuple-element.54), channel_id=1, source_target_pairs={{0,6},{1,7},{2,4},{3,5},{4,2},{5,3},{6,0},{7,1},{8,14},{9,15},{10,... | collective-permute-start | bytes 196616 | tf_op jit(solution)/shard_map/ppermute | solution.py:335
  46.5 4.0 %grads_across.2 = (f32[512,640]{1,0:T(8,128)S(1)}, bf16[512,256]{1,0:T(8,128)(2,1)S(1)}) custom-call(bf16[512,640]{1,0:T(8,128)(2,1)S(1)} %bitcast.13, bf16[512,640]{1,0:T(8,128)(2,1)S(1)} %get-tuple-element.37.refs_4_.refs_1_.refs_2_, f32[10,8,256]{2,1,0:T(8,128)S(1)} %stats_last.1.refs_3_.refs_2_, f32[512,640]{1,0:T(8,128)S(1)} %get-tuple-element.49.refs_3_, ...), custom_call_target="tpu_custom_call" | custom-call | tf_op jit(solution)/shard_map/grads_across/pallas_call | solution.py:35
  50.5 0.6 collective-permute-start.17
  51.1 1.6 %collective-permute-start.20 = (bf16[4,4,32,256]{3,2,1,0:T(8,128)(2,1)S(1)}, bf16[4,4,32,256]{3,2,1,0:T(8,128)(2,1)S(1)}, u32[]{:S(2)}, u32[]{:S(2)}) collective-permute-start(bf16[4,4,32,256]{3,2,1,0:T(8,128)(2,1)S(1)} %terms_stack.1.refs_6_.mine_ref), channel_id=1, source_target_pairs={{0,1},{1,0},{2,3},{3,2},{4,5},{5,4},{6,7},{7,6},{8,9},{9,8},{10,11... | collective-permute-start | bytes 786440 | tf_op jit(solution)/shard_map/ppermute | solution.py:335
  52.7 3.8 %grads_near.1 = (f32[512,640]{1,0:T(8,128)S(1)}, f32[512,256]{1,0:T(8,128)S(1)}) custom-call(bf16[512,640]{1,0:T(8,128)(2,1)S(1)} %bitcast.14, bf16[512,640]{1,0:T(8,128)(2,1)S(1)} %get-tuple-element.37.refs_4_.refs_1_.refs_2_, f32[10,8,256]{2,1,0:T(8,128)S(1)} %stats_last.1.refs_3_.refs_2_, f32[512,640]{1,0:T(8,128)S(1)} %get-tuple-element.50.refs_3_, ...), custom_call_target="tpu_custom_call" | custom-call | flops 7000000000 | tf_op jit(solution)/shard_map/grads_near/pallas_call | solution.py:35
  56.5 3.8 %grads_across.3 = (f32[512,640]{1,0:T(8,128)S(1)}, bf16[512,256]{1,0:T(8,128)(2,1)S(1)}) custom-call(bf16[512,640]{1,0:T(8,128)(2,1)S(1)} %bitcast.15, bf16[512,640]{1,0:T(8,128)(2,1)S(1)} %get-tuple-element.37.refs_4_.refs_1_.refs_2_, f32[10,8,256]{2,1,0:T(8,128)S(1)} %stats_last.1.refs_3_.refs_2_, f32[512,640]{1,0:T(8,128)S(1)} %get-tuple-element.56.refs_3_, ...), custom_call_target="tpu_custom_call" | custom-call | tf_op jit(solution)/shard_map/grads_across/pallas_call | solution.py:35
  60.3 0.1 collective-permute-start.19
  60.4 0.6 collective-permute-start.18
  61.0 4.0 %grads_rest.1 = (f32[512,640]{1,0:T(8,128)S(1)}, f32[512,256]{1,0:T(8,128)S(1)}) custom-call(bf16[512,640]{1,0:T(8,128)(2,1)S(1)} %bitcast.16, bf16[512,640]{1,0:T(8,128)(2,1)S(1)} %get-tuple-element.37.refs_4_.refs_1_.refs_2_, f32[10,8,256]{2,1,0:T(8,128)S(1)} %stats_last.1.refs_3_.refs_2_, f32[512,640]{1,0:T(8,128)S(1)} %get-tuple-element.57.refs_3_, ...), custom_call_target="tpu_custom_call" | custom-call | tf_op jit(solution)/shard_map/grads_rest/pallas_call | solution.py:35
  65.0 0.7 terms_route.1
  65.7 3.6 %collective-permute-done.19.x_ref = bf16[512,256]{1,0:T(8,128)(2,1)S(1)} collective-permute-done((bf16[512,256]{1,0:T(8,128)(2,1)S(1)}, bf16[512,256]{1,0:T(8,128)(2,1)S(1)}, u32[]{:S(2)}, u32[]{:S(2)}) %collective-permute-start.19) | collective-permute-done | bytes 262176 | tf_op jit(solution)/shard_map/ppermute | solution.py:335
  69.4 0.2 collective-permute-start.27
  69.6 2.1 %collective-permute-start.24 = (bf16[4,32,256]{2,1,0:T(8,128)(2,1)S(1)}, bf16[4,32,256]{2,1,0:T(8,128)(2,1)S(1)}, u32[]{:S(2)}, u32[]{:S(2)}) collective-permute-start(bf16[4,32,256]{2,1,0:T(8,128)(2,1)S(1)} %get-tuple-element.65), channel_id=1, source_target_pairs={{0,2},{1,3},{2,0},{3,1},{4,6},{5,7},{6,4},{7,5},{8,10},{9,11},{10,... | collective-permute-start | bytes 196616 | tf_op jit(solution)/shard_map/ppermute | solution.py:335
  71.6 0.8 collective-permute-start.25
  72.4 1.6 %collective-permute-start.26 = (bf16[4,32,256]{2,1,0:T(8,128)(2,1)S(1)}, bf16[4,32,256]{2,1,0:T(8,128)(2,1)S(1)}, u32[]{:S(2)}, u32[]{:S(2)}) collective-permute-start(bf16[4,32,256]{2,1,0:T(8,128)(2,1)S(1)} %get-tuple-element.67), channel_id=1, source_target_pairs={{0,6},{1,7},{2,4},{3,5},{4,2},{5,3},{6,0},{7,1},{8,14},{9,15},{10,... | collective-permute-start | bytes 196616 | tf_op jit(solution)/shard_map/ppermute | solution.py:335
  74.0 1.5 %grads_own.1 = (f32[512,640]{1,0:T(8,128)S(1)}, f32[512,256]{1,0:T(8,128)S(1)}) custom-call(bf16[512,640]{1,0:T(8,128)(2,1)S(1)} %bitcast.17, bf16[512,640]{1,0:T(8,128)(2,1)S(1)} %get-tuple-element.37.refs_4_.refs_1_.refs_2_, f32[10,8,256]{2,1,0:T(8,128)S(1)} %stats_last.1.refs_3_.refs_2_, f32[512,640]{1,0:T(8,128)S(1)} %get-tuple-element.60.refs_3_, ...), custom_call_target="tpu_custom_call" | custom-call | tf_op jit(solution)/shard_map/grads_own/pallas_call | solution.py:35
  75.5 0.1 collective-permute-start.23
  75.7 1.6 %collective-permute-start.22 = (s32[1,16]{1,0:T(1,128)S(1)}, s32[1,16]{1,0:T(1,128)S(1)}, u32[]{:S(2)}, u32[]{:S(2)}) collective-permute-start(s32[1,16]{1,0:T(1,128)S(1)} %pass_lengths.1), channel_id=1, source_target_pairs={{0,16},{8,24},{16,0},{24,8},{1,17},{9,25},{17,1},{25,9},{2,18},{10... | collective-permute-start | bytes 200 | tf_op jit(solution)/shard_map/ppermute | solution.py:335
  77.3 0.2 collective-permute-done.25.refs_2_
  77.5 0.1 collective-permute-start.21
  77.6 1.0 %collective-permute-done.26.refs_3_ = bf16[4,32,256]{2,1,0:T(8,128)(2,1)S(1)} collective-permute-done((bf16[4,32,256]{2,1,0:T(8,128)(2,1)S(1)}, bf16[4,32,256]{2,1,0:T(8,128)(2,1)S(1)}, u32[]{:S(2)}, u32[]{:S(2)}) %collective-permute-start.26) | collective-permute-done | bytes 65568 | tf_op jit(solution)/shard_map/ppermute | solution.py:335
  78.6 0.6 join_terms.1.refs_2_.refs_6_
  79.2 0.0 collective-permute-done.22.refs_2_
  79.3 1.6 %over_count.1 = (bf16[512,640]{1,0:T(8,128)(2,1)}, bf16[512,256]{1,0:T(8,128)(2,1)}, bf16[256,256]{1,0:T(8,128)(2,1)}) custom-call(s32[1,16]{1,0:T(1,128)S(1)} %copy-done.8, s32[1,16]{1,0:T(1,128)S(1)} %collective-permute-done.21.refs_1_, s32[1,16]{1,0:T(1,128)S(1)} %collective-permute-done.22.refs_2_, s32[1,16]{1,0:T(1,128)S(1)} %collective-permute-done.23.refs_3_, ...), custom_call_target="tpu_custom_call" | custom-call | tf_op jit(solution)/shard_map/over_count/pallas_call | solution.py:35
  (40 shorter events, 0.3 us)
Async XLA Ops:
  0.6 18.0 %copy-start = (bf16[1,512,640]{2,1,0:T(8,128)(2,1)S(1)}, bf16[1,512,640]{2,1,0:T(8,128)(2,1)}, u32[]{:S(2)}) copy-start(bf16[1,512,640]{2,1,0:T(8,128)(2,1)} %param.7) | copy-start | bytes 1966084
  0.6 1.0 %copy-start.1 = (bf16[1,512,256]{2,1,0:T(8,128)(2,1)S(1)}, bf16[1,512,256]{2,1,0:T(8,128)(2,1)}, u32[]{:S(2)}) copy-start(bf16[1,512,256]{2,1,0:T(8,128)(2,1)} %param.8) | copy-start | bytes 786436
  1.7 16.9 %copy-start.2 = (bf16[1,512,256]{2,1,0:T(8,128)(2,1)S(1)}, bf16[1,512,256]{2,1,0:T(8,128)(2,1)}, u32[]{:S(2)}) copy-start(bf16[1,512,256]{2,1,0:T(8,128)(2,1)} %param.8) | copy-start | bytes 786436
  1.7 10.4 %collective-permute-start = (bf16[4,32,256]{2,1,0:T(8,128)(2,1)S(1)}, bf16[4,32,256]{2,1,0:T(8,128)(2,1)S(1)}, u32[]{:S(2)}, u32[]{:S(2)}) collective-permute-start(bf16[4,32,256]{2,1,0:T(8,128)(2,1)S(1)} %get-tuple-element.40), channel_id=1, source_target_pairs={{0,2},{1,3},{2,0},{3,1},{4,6},{5,7},{6,4},{7,5},{8,10},{9,11},{10,... | collective-permute-start | bytes 196616 | tf_op jit(solution)/shard_map/ppermute | solution.py:335
  4.8 7.3 %collective-permute-start.1 = (bf16[4,32,256]{2,1,0:T(8,128)(2,1)S(1)}, bf16[4,32,256]{2,1,0:T(8,128)(2,1)S(1)}, u32[]{:S(2)}, u32[]{:S(2)}) collective-permute-start(bf16[4,32,256]{2,1,0:T(8,128)(2,1)S(1)} %get-tuple-element.41), channel_id=1, source_target_pairs={{0,4},{1,5},{2,6},{3,7},{4,0},{5,1},{6,2},{7,3},{8,12},{9,13},{10,... | collective-permute-start | bytes 196616 | tf_op jit(solution)/shard_map/ppermute | solution.py:335
  7.4 6.1 %collective-permute-start.2 = (bf16[4,32,256]{2,1,0:T(8,128)(2,1)S(1)}, bf16[4,32,256]{2,1,0:T(8,128)(2,1)S(1)}, u32[]{:S(2)}, u32[]{:S(2)}) collective-permute-start(bf16[4,32,256]{2,1,0:T(8,128)(2,1)S(1)} %get-tuple-element.42), channel_id=1, source_target_pairs={{0,6},{1,7},{2,4},{3,5},{4,2},{5,3},{6,0},{7,1},{8,14},{9,15},{10,... | collective-permute-start | bytes 196616 | tf_op jit(solution)/shard_map/ppermute | solution.py:335
  7.4 1.1 %copy-start.3 = (bf16[1,512,640]{2,1,0:T(8,128)(2,1)S(1)}, bf16[1,512,640]{2,1,0:T(8,128)(2,1)}, u32[]{:S(2)}) copy-start(bf16[1,512,640]{2,1,0:T(8,128)(2,1)} %param.10) | copy-start | bytes 1966084
  8.5 0.9 %copy-start.4 = (bf16[1,256,256]{2,1,0:T(8,128)(2,1)S(1)}, bf16[1,256,256]{2,1,0:T(8,128)(2,1)}, u32[]{:S(2)}) copy-start(bf16[1,256,256]{2,1,0:T(8,128)(2,1)} %param.9) | copy-start | bytes 393220
  9.4 0.7 copy-start.5
  10.0 0.7 copy-start.7
  10.7 0.7 copy-start.9
  13.5 11.6 %collective-permute-start.5 = (bf16[4,4,32,256]{3,2,1,0:T(8,128)(2,1)S(1)}, bf16[4,4,32,256]{3,2,1,0:T(8,128)(2,1)S(1)}, u32[]{:S(2)}, u32[]{:S(2)}) collective-permute-start(bf16[4,4,32,256]{3,2,1,0:T(8,128)(2,1)S(1)} %pairs_stack.1.refs_4_.mine_ref), channel_id=1, source_target_pairs={{0,1},{1,0},{2,3},{3,2},{4,5},{5,4},{6,7},{7,6},{8,9},{9,8},{10,11... | collective-permute-start | bytes 786440 | tf_op jit(solution)/shard_map/ppermute | solution.py:335
  15.0 7.2 %collective-permute-start.3 = (bf16[256,256]{1,0:T(8,128)(2,1)S(1)}, bf16[256,256]{1,0:T(8,128)(2,1)S(1)}, u32[]{:S(2)}, u32[]{:S(2)}) collective-permute-start(bf16[256,256]{1,0:T(8,128)(2,1)S(1)} %get-tuple-element.38.refs_2_.refs_4_), channel_id=1, source_target_pairs={{0,4},{1,5},{2,6},{3,7},{4,0},{5,1},{6,2},{7,3},{8,12},{9,13},{10,... | collective-permute-start | bytes 393224 | tf_op jit(solution)/shard_map/ppermute | solution.py:335
  16.6 6.4 %collective-permute-start.4 = (bf16[256,256]{1,0:T(8,128)(2,1)S(1)}, bf16[256,256]{1,0:T(8,128)(2,1)S(1)}, u32[]{:S(2)}, u32[]{:S(2)}) collective-permute-start(bf16[256,256]{1,0:T(8,128)(2,1)S(1)} %get-tuple-element.38.refs_2_.refs_4_), channel_id=1, source_target_pairs={{0,2},{1,3},{2,0},{3,1},{4,6},{5,7},{6,4},{7,5},{8,10},{9,11},{10,... | collective-permute-start | bytes 393224 | tf_op jit(solution)/shard_map/ppermute | solution.py:335
  18.0 9.3 %collective-permute-start.7 = (bf16[256,256]{1,0:T(8,128)(2,1)S(1)}, bf16[256,256]{1,0:T(8,128)(2,1)S(1)}, u32[]{:S(2)}, u32[]{:S(2)}) collective-permute-start(bf16[256,256]{1,0:T(8,128)(2,1)S(1)} %get-tuple-element.38.refs_2_.refs_4_), channel_id=1, source_target_pairs={{0,1},{1,0},{2,3},{3,2},{4,5},{5,4},{6,7},{7,6},{8,9},{9,8},{10,11... | collective-permute-start | bytes 393224 | tf_op jit(solution)/shard_map/ppermute | solution.py:335
  22.2 6.4 %collective-permute-start.6 = (bf16[256,256]{1,0:T(8,128)(2,1)S(1)}, bf16[256,256]{1,0:T(8,128)(2,1)S(1)}, u32[]{:S(2)}, u32[]{:S(2)}) collective-permute-start(bf16[256,256]{1,0:T(8,128)(2,1)S(1)} %pass_on.3.refs_3_.refs_5_), channel_id=1, source_target_pairs={{0,2},{1,3},{2,0},{3,1},{4,6},{5,7},{6,4},{7,5},{8,10},{9,11},{10,... | collective-permute-start | bytes 393224 | tf_op jit(solution)/shard_map/ppermute | solution.py:335
  23.0 10.9 %collective-permute-start.9 = (bf16[256,256]{1,0:T(8,128)(2,1)S(1)}, bf16[256,256]{1,0:T(8,128)(2,1)S(1)}, u32[]{:S(2)}, u32[]{:S(2)}) collective-permute-start(bf16[256,256]{1,0:T(8,128)(2,1)S(1)} %pass_on.4.refs_4_), channel_id=1, source_target_pairs={{0,1},{1,0},{2,3},{3,2},{4,5},{5,4},{6,7},{7,6},{8,9},{9,8},{10,11... | collective-permute-start | bytes 393224 | tf_op jit(solution)/shard_map/ppermute | solution.py:335
  23.6 11.0 %collective-permute-start.8 = (bf16[256,256]{1,0:T(8,128)(2,1)S(1)}, bf16[256,256]{1,0:T(8,128)(2,1)S(1)}, u32[]{:S(2)}, u32[]{:S(2)}) collective-permute-start(bf16[256,256]{1,0:T(8,128)(2,1)S(1)} %pass_on.3.refs_3_.refs_5_), channel_id=1, source_target_pairs={{0,1},{1,0},{2,3},{3,2},{4,5},{5,4},{6,7},{7,6},{8,9},{9,8},{10,11... | collective-permute-start | bytes 393224 | tf_op jit(solution)/shard_map/ppermute | solution.py:335
  25.8 8.7 %collective-permute-start.10 = (bf16[4,32,256]{2,1,0:T(8,128)(2,1)S(1)}, bf16[4,32,256]{2,1,0:T(8,128)(2,1)S(1)}, u32[]{:S(2)}, u32[]{:S(2)}) collective-permute-start(bf16[4,32,256]{2,1,0:T(8,128)(2,1)S(1)} %get-tuple-element.44), channel_id=1, source_target_pairs={{0,2},{1,3},{2,0},{3,1},{4,6},{5,7},{6,4},{7,5},{8,10},{9,11},{10,... | collective-permute-start | bytes 196616 | tf_op jit(solution)/shard_map/ppermute | solution.py:335
  27.3 7.2 %collective-permute-start.11 = (bf16[4,32,256]{2,1,0:T(8,128)(2,1)S(1)}, bf16[4,32,256]{2,1,0:T(8,128)(2,1)S(1)}, u32[]{:S(2)}, u32[]{:S(2)}) collective-permute-start(bf16[4,32,256]{2,1,0:T(8,128)(2,1)S(1)} %get-tuple-element.45), channel_id=1, source_target_pairs={{0,4},{1,5},{2,6},{3,7},{4,0},{5,1},{6,2},{7,3},{8,12},{9,13},{10,... | collective-permute-start | bytes 196616 | tf_op jit(solution)/shard_map/ppermute | solution.py:335
  28.6 6.2 %collective-permute-start.12 = (bf16[4,32,256]{2,1,0:T(8,128)(2,1)S(1)}, bf16[4,32,256]{2,1,0:T(8,128)(2,1)S(1)}, u32[]{:S(2)}, u32[]{:S(2)}) collective-permute-start(bf16[4,32,256]{2,1,0:T(8,128)(2,1)S(1)} %get-tuple-element.46), channel_id=1, source_target_pairs={{0,6},{1,7},{2,4},{3,5},{4,2},{5,3},{6,0},{7,1},{8,14},{9,15},{10,... | collective-permute-start | bytes 196616 | tf_op jit(solution)/shard_map/ppermute | solution.py:335
  32.1 2.7 %copy-start.6 = (s32[1,32]{1,0:T(1,128)S(1)}, s32[1,32]{1,0:T(1,128)}, u32[]{:S(2)}) copy-start(s32[1,32]{1,0:T(1,128)} %plan_ref.7) | copy-start | bytes 388
  34.0 5.0 %collective-permute-start.13 = (bf16[256,256]{1,0:T(8,128)(2,1)S(1)}, bf16[256,256]{1,0:T(8,128)(2,1)S(1)}, u32[]{:S(2)}, u32[]{:S(2)}) collective-permute-start(bf16[256,256]{1,0:T(8,128)(2,1)S(1)} %pass_on.5), channel_id=1, source_target_pairs={{0,1},{1,0},{2,3},{3,2},{4,5},{5,4},{6,7},{7,6},{8,9},{9,8},{10,11... | collective-permute-start | bytes 393224 | tf_op jit(solution)/shard_map/ppermute | solution.py:335
  42.0 9.0 %collective-permute-start.14 = (bf16[4,32,256]{2,1,0:T(8,128)(2,1)S(1)}, bf16[4,32,256]{2,1,0:T(8,128)(2,1)S(1)}, u32[]{:S(2)}, u32[]{:S(2)}) collective-permute-start(bf16[4,32,256]{2,1,0:T(8,128)(2,1)S(1)} %get-tuple-element.52), channel_id=1, source_target_pairs={{0,2},{1,3},{2,0},{3,1},{4,6},{5,7},{6,4},{7,5},{8,10},{9,11},{10,... | collective-permute-start | bytes 196616 | tf_op jit(solution)/shard_map/ppermute | solution.py:335
  42.6 8.5 %collective-permute-start.15 = (bf16[4,32,256]{2,1,0:T(8,128)(2,1)S(1)}, bf16[4,32,256]{2,1,0:T(8,128)(2,1)S(1)}, u32[]{:S(2)}, u32[]{:S(2)}) collective-permute-start(bf16[4,32,256]{2,1,0:T(8,128)(2,1)S(1)} %get-tuple-element.53), channel_id=1, source_target_pairs={{0,4},{1,5},{2,6},{3,7},{4,0},{5,1},{6,2},{7,3},{8,12},{9,13},{10,... | collective-permute-start | bytes 196616 | tf_op jit(solution)/shard_map/ppermute | solution.py:335
  44.8 6.3 %collective-permute-start.16 = (bf16[4,32,256]{2,1,0:T(8,128)(2,1)S(1)}, bf16[4,32,256]{2,1,0:T(8,128)(2,1)S(1)}, u32[]{:S(2)}, u32[]{:S(2)}) collective-permute-start(bf16[4,32,256]{2,1,0:T(8,128)(2,1)S(1)} %get-tuple-element.54), channel_id=1, source_target_pairs={{0,6},{1,7},{2,4},{3,5},{4,2},{5,3},{6,0},{7,1},{8,14},{9,15},{10,... | collective-permute-start | bytes 196616 | tf_op jit(solution)/shard_map/ppermute | solution.py:335
  50.5 9.8 %collective-permute-start.17 = (bf16[512,256]{1,0:T(8,128)(2,1)S(1)}, bf16[512,256]{1,0:T(8,128)(2,1)S(1)}, u32[]{:S(2)}, u32[]{:S(2)}) collective-permute-start(bf16[512,256]{1,0:T(8,128)(2,1)S(1)} %get-tuple-element.55.refs_4_), channel_id=1, source_target_pairs={{0,1},{1,0},{2,3},{3,2},{4,5},{5,4},{6,7},{7,6},{8,9},{9,8},{10,11... | collective-permute-start | bytes 786440 | tf_op jit(solution)/shard_map/ppermute | solution.py:335
  51.1 13.9 %collective-permute-start.20 = (bf16[4,4,32,256]{3,2,1,0:T(8,128)(2,1)S(1)}, bf16[4,4,32,256]{3,2,1,0:T(8,128)(2,1)S(1)}, u32[]{:S(2)}, u32[]{:S(2)}) collective-permute-start(bf16[4,4,32,256]{3,2,1,0:T(8,128)(2,1)S(1)} %terms_stack.1.refs_6_.mine_ref), channel_id=1, source_target_pairs={{0,1},{1,0},{2,3},{3,2},{4,5},{5,4},{6,7},{7,6},{8,9},{9,8},{10,11... | collective-permute-start | bytes 786440 | tf_op jit(solution)/shard_map/ppermute | solution.py:335
  60.3 9.0 %collective-permute-start.19 = (bf16[512,256]{1,0:T(8,128)(2,1)S(1)}, bf16[512,256]{1,0:T(8,128)(2,1)S(1)}, u32[]{:S(2)}, u32[]{:S(2)}) collective-permute-start(bf16[512,256]{1,0:T(8,128)(2,1)S(1)} %sum_near.1.refs_6_), channel_id=1, source_target_pairs={{0,2},{1,3},{2,0},{3,1},{4,6},{5,7},{6,4},{7,5},{8,10},{9,11},{10,... | collective-permute-start | bytes 786440 | tf_op jit(solution)/shard_map/ppermute | solution.py:335
  60.4 9.0 %collective-permute-start.18 = (bf16[512,256]{1,0:T(8,128)(2,1)S(1)}, bf16[512,256]{1,0:T(8,128)(2,1)S(1)}, u32[]{:S(2)}, u32[]{:S(2)}) collective-permute-start(bf16[512,256]{1,0:T(8,128)(2,1)S(1)} %get-tuple-element.59.refs_2_), channel_id=1, source_target_pairs={{0,1},{1,0},{2,3},{3,2},{4,5},{5,4},{6,7},{7,6},{8,9},{9,8},{10,11... | collective-permute-start | bytes 786440 | tf_op jit(solution)/shard_map/ppermute | solution.py:335
  69.4 9.8 %collective-permute-start.27 = (bf16[256,256]{1,0:T(8,128)(2,1)S(1)}, bf16[256,256]{1,0:T(8,128)(2,1)S(1)}, u32[]{:S(2)}, u32[]{:S(2)}) collective-permute-start(bf16[256,256]{1,0:T(8,128)(2,1)S(1)} %sum_far.1.refs_5_), channel_id=1, source_target_pairs={{0,4},{1,5},{2,6},{3,7},{4,0},{5,1},{6,2},{7,3},{8,12},{9,13},{10,... | collective-permute-start | bytes 393224 | tf_op jit(solution)/shard_map/ppermute | solution.py:335
  69.6 6.1 %collective-permute-start.24 = (bf16[4,32,256]{2,1,0:T(8,128)(2,1)S(1)}, bf16[4,32,256]{2,1,0:T(8,128)(2,1)S(1)}, u32[]{:S(2)}, u32[]{:S(2)}) collective-permute-start(bf16[4,32,256]{2,1,0:T(8,128)(2,1)S(1)} %get-tuple-element.65), channel_id=1, source_target_pairs={{0,2},{1,3},{2,0},{3,1},{4,6},{5,7},{6,4},{7,5},{8,10},{9,11},{10,... | collective-permute-start | bytes 196616 | tf_op jit(solution)/shard_map/ppermute | solution.py:335
  71.6 5.9 %collective-permute-start.25 = (bf16[4,32,256]{2,1,0:T(8,128)(2,1)S(1)}, bf16[4,32,256]{2,1,0:T(8,128)(2,1)S(1)}, u32[]{:S(2)}, u32[]{:S(2)}) collective-permute-start(bf16[4,32,256]{2,1,0:T(8,128)(2,1)S(1)} %get-tuple-element.66), channel_id=1, source_target_pairs={{0,4},{1,5},{2,6},{3,7},{4,0},{5,1},{6,2},{7,3},{8,12},{9,13},{10,... | collective-permute-start | bytes 196616 | tf_op jit(solution)/shard_map/ppermute | solution.py:335
  72.4 6.2 %collective-permute-start.26 = (bf16[4,32,256]{2,1,0:T(8,128)(2,1)S(1)}, bf16[4,32,256]{2,1,0:T(8,128)(2,1)S(1)}, u32[]{:S(2)}, u32[]{:S(2)}) collective-permute-start(bf16[4,32,256]{2,1,0:T(8,128)(2,1)S(1)} %get-tuple-element.67), channel_id=1, source_target_pairs={{0,6},{1,7},{2,4},{3,5},{4,2},{5,3},{6,0},{7,1},{8,14},{9,15},{10,... | collective-permute-start | bytes 196616 | tf_op jit(solution)/shard_map/ppermute | solution.py:335
  74.0 1.5 %copy-start.8 = (s32[1,16]{1,0:T(1,128)S(1)}, s32[1,16]{1,0:T(1,128)}, u32[]{:S(2)}) copy-start(s32[1,16]{1,0:T(1,128)} %refs_0_.5) | copy-start | bytes 196
  75.5 3.7 %collective-permute-start.23 = (s32[1,16]{1,0:T(1,128)S(1)}, s32[1,16]{1,0:T(1,128)S(1)}, u32[]{:S(2)}, u32[]{:S(2)}) collective-permute-start(s32[1,16]{1,0:T(1,128)S(1)} %pass_lengths.1), channel_id=1, source_target_pairs={{0,24},{8,16},{16,8},{24,0},{1,25},{9,17},{17,9},{25,1},{2,26},{10... | collective-permute-start | bytes 200 | tf_op jit(solution)/shard_map/ppermute | solution.py:335
  75.7 3.6 %collective-permute-start.22 = (s32[1,16]{1,0:T(1,128)S(1)}, s32[1,16]{1,0:T(1,128)S(1)}, u32[]{:S(2)}, u32[]{:S(2)}) collective-permute-start(s32[1,16]{1,0:T(1,128)S(1)} %pass_lengths.1), channel_id=1, source_target_pairs={{0,16},{8,24},{16,0},{24,8},{1,17},{9,25},{17,1},{25,9},{2,18},{10... | collective-permute-start | bytes 200 | tf_op jit(solution)/shard_map/ppermute | solution.py:335
  77.5 1.8 %collective-permute-start.21 = (s32[1,16]{1,0:T(1,128)S(1)}, s32[1,16]{1,0:T(1,128)S(1)}, u32[]{:S(2)}, u32[]{:S(2)}) collective-permute-start(s32[1,16]{1,0:T(1,128)S(1)} %pass_lengths.1), channel_id=1, source_target_pairs={{0,8},{8,0},{16,24},{24,16},{1,9},{9,1},{17,25},{25,17},{2,10},{10... | collective-permute-start | bytes 200 | tf_op jit(solution)/shard_map/ppermute | solution.py:335

commit v4 on v3

--- a/solution.py
+++ b/solution.py
@@ -18,7 +18,6 @@
 F32 = jnp.float32
 BF16 = jnp.bfloat16
 NT = (((1,), (1,)), ((), ()))
-TN = (((0,), (0,)), ((), ()))
 NN = (((1,), (0,)), ((), ()))
 TILE = 2 * BLK
 VMEM = pl.BlockSpec(memory_space=pltpu.VMEM)
@@ -65,6 +64,10 @@
 
 def pass_kernel(x_ref, after_ref, out_ref):
     out_ref[...] = x_ref[...]
+
+
+def add_kernel(x_ref, y_ref, after_ref, out_ref):
+    out_ref[...] = x_ref[...] + y_ref[...]
 
 
 def route_kernel(count, plan_ref, mine_ref, other_ref, *refs):
@@ -85,13 +88,14 @@
             out_ref[s] = held[lax.rem(owner, 2), place, lax.rem(partner, local)]
 
 
-def join_pieces(pieces, out_ref):
+def join_pieces(pieces, out_ref, start=0):
     line = lax.div(lax.axis_index("seq"), 2)
     rows = BLK // len(pieces)
     for k, ref in enumerate(pieces):
-        first = lax.bitwise_xor(line, k) * rows
-        for s in range(ref.shape[0]):
-            out_ref[pl.ds(pl.multiple_of(s * BLK + first, rows), rows)] = ref[s]
+        place = lax.bitwise_xor(line, k) * rows
+        for s in range(out_ref.shape[0] // BLK):
+            piece = ref[s] if len(ref.shape) == 3 else ref[start + s * rows : start + (s + 1) * rows]
+            out_ref[pl.ds(pl.multiple_of(s * BLK + place, rows), rows)] = piece
 
 
 def weight_kernel(groups, plan_ref, rewards_ref, lengths_ref, grad_ref, prompt_ref, out_ref, prompt_out):
@@ -232,8 +236,8 @@
 
     def add_queries(dq, rows, cols):
         if carried:
-            dq = dq + before[rows, cols]
-        dq_ref[rows, cols] = dq
+            dq = dq + before[cols, rows]
+        dq_ref[cols, rows] = dq
 
     if blocks_ref is not None:
         for j in range(local):
@@ -251,16 +255,17 @@
             p, ds = grads(s, dot(blocks_ref[place, VALUES], w, NT), factors(rows))
             blocks_sum[place, KEYS] = dot(ds, q, NN) * back
             blocks_sum[place, VALUES] = dot(p, w, NN)
-            dq = dot(ds, keys, TN)
+            dq = dot(keys.T, ds, NN)
             for h in range(heads):
                 cols = slice(h * BLK, (h + 1) * BLK)
-                add_queries(dq[cols], place, cols)
+                add_queries(dq[:, cols], place, cols)
         if partner:
             write_pieces(blocks_sum, blocks_out)
     if not shards:
         return
     keys = jnp.concatenate([ref[:, KEYS] for ref in kv], axis=0)
     values = jnp.concatenate([ref[:, VALUES] for ref in kv], axis=0)
+    turned = keys.T
     for t, r, rows, cols in head_tiles(q_ref):
         q, w = q_ref[rows, cols], w_ref[rows, cols]
         state = factors([stats_ref[t, i : i + 1] for i in range(3)])
@@ -272,41 +277,41 @@
         else:
             kv_sum[:, KEYS] += dk
             kv_sum[:, VALUES] += dv
-        add_queries(dot(ds, keys, TN), rows, cols)
+        add_queries(dot(turned, ds, NN), rows, cols)
     for side, factor in ((KEYS, back), (VALUES, 1.0)):
         kv_out[:, side] = (kv_sum[:, side] * factor).astype(kv_out.dtype)
 
 
-def join_kernel(count, plan_ref, *refs):
-    pieces, out_ref = refs[:count], refs[-1]
+def finish_kernel(back, start, plan_ref, lengths_ref, *refs):
+    total = jnp.int32(0)
+    for r in range(RESP):
+        total = total + lengths_ref[0, r]
+    share = 1.0 / jnp.full((1, BLK), total.astype(F32))
+    (dq_ref, own_ref, prompt_ref), pieces = refs[:3], refs[3:-4]
+    dq_out, stream_out, prompt_out, held = refs[-4:]
+    join_pieces(pieces, held, start)
     me = lax.axis_index("seq")
-    join_pieces(pieces, out_ref)
-    local = out_ref.shape[0] // BLK
-    for s in range(local):
-        rows = slice(s * BLK, (s + 1) * BLK)
-        odd = lax.rem(plan_ref[0, me * local + s], NB)
-        odd_rows = jnp.full((BLK, 2 * BLK), odd, jnp.int32) > 0
-        out_ref[rows] = jnp.where(odd_rows, 0.0, out_ref[rows].astype(F32)).astype(BF16)
-
-
-def finish_kernel(groups, back, *refs):
-    total = jnp.int32(0)
-    for ref in refs[:groups]:
-        for r in range(RESP):
-            total = total + ref[0, r]
-    share = 1.0 / jnp.full((1, BLK), total.astype(F32))
-    dq_ref, own_ref, back_ref, prompt_ref, dq_out, stream_out, prompt_out = refs[groups:]
-    for h in range(dq_ref.shape[1] // BLK):
+    local = own_ref.shape[0] // BLK
+    for h in range(dq_ref.shape[0] // BLK):
         cols = slice(h * BLK, (h + 1) * BLK)
-        dq_out[:, cols] = (dq_ref[:, cols] * (share * back)).astype(BF16)
+        dq_out[:, cols] = (dq_ref[cols, :] * (share[:, :1] * back)).astype(BF16).T
     for cols in (KEYS, VALUES):
-        stream = own_ref[:, cols] + back_ref[:, cols].astype(F32)
-        stream_out[:, cols] = (stream * share).astype(BF16)
+        for s in range(local):
+            rows = slice(s * BLK, (s + 1) * BLK)
+            odd = lax.rem(plan_ref[0, me * local + s], NB)
+            odd_rows = jnp.full((BLK, BLK), odd, jnp.int32) > 0
+            stream = own_ref[rows, cols] + jnp.where(odd_rows, 0.0, held[rows, cols].astype(F32))
+            stream_out[rows, cols] = (stream * share).astype(BF16)
         prompt_out[:, cols] = (prompt_ref[:, cols] * share).astype(BF16)
 
 
-def pick_kernel(per, parts, picked, ordered, *refs):
+def pick_kernel(per, parts, picked, joined, ordered, *refs):
     out_ref, refs = refs[-1], refs[: len(refs) - 1 - ordered]
+    if joined:
+        piece, refs = refs[-1], refs[:-1]
+        first, rows = len(picked) * per, piece.shape[1]
+        for s in range(piece.shape[0]):
+            out_ref[first + s * rows : first + (s + 1) * rows] = piece[s]
     where = []
     for ref in refs[:parts]:
         where += [(ref, i) for i in range(ref.shape[0] // per)]
@@ -401,7 +406,7 @@
         bit //= 2
     early = [k for k in column if not k & 2 or k == 2]
     late = [k for k in column if k not in early]
-    across = {k: swap(column[k], "seq", 1) for k in early}
+    across = {k: swap(column[k] if k else prompt_on, "seq", 1) for k in early}
     coming = [x for k, x in column.items() if k] + [across[k] for k in early]
     (state,) = stats("stats_prompt", state, coming[:2], after=[routed[0]])
     across.update({k: swap(held_back(column[k], state), "seq", 1) for k in late})
@@ -419,7 +424,7 @@
         args += list(kv) + [x for x in (own, part) if x is not None]
         specs += [VMEM] * (len(args) - len(specs))
         keys = sum(x.shape[0] for x in kv)
-        out = [jax.ShapeDtypeStruct(q.shape, F32)]
+        out = [jax.ShapeDtypeStruct(q.shape[::-1], F32)]
         out += [jax.ShapeDtypeStruct((keys, width), kind)] if kv else []
         scratch = [pltpu.VMEM((keys, width), F32)] if kv else []
         if own is not None:
@@ -440,12 +445,13 @@
 
     per = prompt.shape[0]
 
-    def pick(name, parts, extra, picked, kind, after=(), beside=False):
-        args = [*parts, *extra]
+    def pick(name, parts, extra, picked, kind, joined=(), after=(), beside=False):
+        args = [*parts, *extra, *joined]
+        height = per * len(picked) + sum(x.shape[0] * x.shape[1] for x in joined)
         return call(
-            partial(pick_kernel, per, len(parts), tuple(picked), len(after)),
+            partial(pick_kernel, per, len(parts), tuple(picked), len(joined), len(after)),
             name,
-            jax.ShapeDtypeStruct((per * len(picked), width), kind),
+            jax.ShapeDtypeStruct((height, width), kind),
             [VMEM] * len(args),
             args,
             after=after,
@@ -462,10 +468,20 @@
     dq, far_rest = grads("grads_across", dq, [across[k] for k in rest])
     sums = pick("sum_near", [sums], [far_near], range(len(near)), BF16, after=[far_rest])
     far_rest = swap(far_rest, "seq", 1)
+    as_lengths = jax.ShapeDtypeStruct(lengths.shape, jnp.int32)
+
+    def added(x, step, after):
+        args = [x, swap(x, "grp", step)]
+        return call(add_kernel, "add_lengths", as_lengths, [VMEM] * 2, args, after=[after])
+
+    total = call(pass_kernel, "pass_lengths", as_lengths, [VMEM], [lengths], after=[sums])
     dq, sent = grads("grads_rest", dq, [column[k] for k in rest], kind=F32, after=[sums])
     sums = swap(sums, "seq", 2)
+    step = 1
+    if step < groups:
+        total, step = added(total, step, sent), 2
     routed = deliver("terms", mine, after=[sent])
-    returned = along(routed)
+    returned = {k: routed[k] if k == 0 else swap(routed[k], "seq", 2 * k) for k in range(line) if k != 2}
     sums_on = call(
         pass_kernel,
         "pass_sums",
@@ -480,36 +496,25 @@
     while bit < count:
         keep = [i for i, k in enumerate(held) if not k & bit]
         send = [i for i, k in enumerate(held) if k & bit]
-        leaving = pick("sum_far", parts, extra, send, BF16, after=order)
+        joined = [routed[2]] if bit == 4 else []
+        leaving = pick("sum_far", parts, extra, send, BF16, joined=joined, after=order)
         kept = pick("sum_kept", parts, extra, keep, F32)
         held, parts, extra, order = [held[i] for i in keep], [kept], [swap(leaving, "seq", bit)], []
         if bit == 4:
-            dq, own_terms = grads("grads_own", dq, [], own=resp, after=[leaving], beside=False)
-            lengths_on = call(
-                pass_kernel,
-                "pass_lengths",
-                jax.ShapeDtypeStruct(lengths.shape, jnp.int32),
-                [VMEM],
-                [lengths],
-                after=[own_terms],
-            )
-            joined = call(
-                partial(join_kernel, line),
-                "join_terms",
-                jax.ShapeDtypeStruct(resp.shape, BF16),
-                [SMEM] + [VMEM] * line,
-                [block_order, *returned],
-                after=[own_terms],
-            )
+            returned[2], start = extra[0], per * len(send)
+            dq, own_terms = grads("grads_own", dq, [], own=resp, after=[leaving])
         bit *= 2
-    lengths_all = [lengths] + [swap(lengths_on, "grp", k) for k in range(1, groups)]
-    prompt_sum = pick("sum_prompt", parts, extra, [0], F32, after=[joined], beside=True)
+    while step < groups:
+        total = added(total, step, own_terms)
+        step *= 2
+    prompt_sum = pick("sum_prompt", parts, extra, [0], F32, after=[own_terms])
     grad_query, grad_stream, grad_prompt = call(
-        partial(finish_kernel, groups, scale / LOG2E),
+        partial(finish_kernel, scale / LOG2E, start),
         "over_count",
         [jax.ShapeDtypeStruct(x.shape, BF16) for x in (q, resp, prompt)],
-        [SMEM] * groups + [VMEM] * 4,
-        [*lengths_all, dq, own_terms, joined, prompt_sum],
+        [SMEM] * 2 + [VMEM] * (3 + line),
+        [block_order, total, dq, own_terms, prompt_sum, *[returned[k] for k in range(line)]],
+        [pltpu.VMEM(resp.shape, BF16)],
     )
     return grad_query[None], grad_stream[None], grad_prompt[None]
 

time: 81.2 us -> 77.3 us (0.952)
  Pallas kernels: 32.7 us -> 29.9 us
  waiting for transfers between devices: 10.6 us -> 9.62 us
    pallas_call x28 -> x29, Pallas kernels: 32.7 us -> 29.9 us  [call(): pl.pallas_call(kernel, name=name, out_shape=out_shape, in_specs=specs, ou...]
    ppermute x28 -> x26, waiting for transfers between devices: 10.6 us -> 9.62 us  [swap(): return lax.ppermute(x, axis, [(i, i ^ k) for i in range(size)])]
    ppermute x28 -> x26, starting transfers between devices: 31.6 us -> 31.6 us  [swap(): return lax.ppermute(x, axis, [(i, i ^ k) for i in range(size)])]
  transfers between devices with their start and end apart: 28 -> 26, of which waited for: 8 -> 11; matrix products, arithmetic and copies ran while one was open for 0% -> 0% of each run, Pallas kernels for 35% -> 33%
where the time goes in v4:
time: 77.3 us; the launch traced here: 77.1 us
  starting transfers between devices  31.6 us (41%)
  Pallas kernels  29.9 us (39%)
  waiting for transfers between devices  9.62 us (12%)
  local copies, waits for them, and re-layouts  4.98 us (6%)
  between operations  0.91 us (1%)
    ppermute x26, starting transfers between devices, swap(): return lax.ppermute(x, axis, [(i, i ^ k) for i in range(size)])  31.6 us
    pallas_call x29, Pallas kernels, call(): pl.pallas_call(kernel, name=name, out_shape=out_shape, in_specs=specs, ou...  29.9 us
    ppermute x26, waiting for transfers between devices, swap(): return lax.ppermute(x, axis, [(i, i ^ k) for i in range(size)])  9.62 us
    unnamed x20, local copies, waits for them, and re-layouts  4.98 us
  transfers between devices with their start and end apart: 26, of which 11 were waited for; matrix products, arithmetic and copies ran while one was open for 0% of the time, Pallas kernels for 33%

profile of v4, /device:TPU:0, one launch (start us, length us, event | category | flops | bytes accessed | tf_op | source)
XLA Modules:
  0.0 77.1 jit_solution(3553814252284311951)
XLA Ops:
  0.6 1.0 %copy-done.1 = bf16[1,512,256]{2,1,0:T(8,128)(2,1)S(1)} copy-done((bf16[1,512,256]{2,1,0:T(8,128)(2,1)S(1)}, bf16[1,512,256]{2,1,0:T(8,128)(2,1)}, u32[]{:S(2)}) %copy-start.1) | copy-done | bytes 262168
  1.7 3.1 %collective-permute-start = (bf16[4,32,256]{2,1,0:T(8,128)(2,1)S(1)}, bf16[4,32,256]{2,1,0:T(8,128)(2,1)S(1)}, u32[]{:S(2)}, u32[]{:S(2)}) collective-permute-start(bf16[4,32,256]{2,1,0:T(8,128)(2,1)S(1)} %get-tuple-element.40), channel_id=1, source_target_pairs={{0,2},{1,3},{2,0},{3,1},{4,6},{5,7},{6,4},{7,5},{8,10},{9,11},{10,... | collective-permute-start | bytes 196616 | tf_op jit(solution)/shard_map/ppermute | solution.py:340
  4.8 2.6 %collective-permute-start.1 = (bf16[4,32,256]{2,1,0:T(8,128)(2,1)S(1)}, bf16[4,32,256]{2,1,0:T(8,128)(2,1)S(1)}, u32[]{:S(2)}, u32[]{:S(2)}) collective-permute-start(bf16[4,32,256]{2,1,0:T(8,128)(2,1)S(1)} %get-tuple-element.41), channel_id=1, source_target_pairs={{0,4},{1,5},{2,6},{3,7},{4,0},{5,1},{6,2},{7,3},{8,12},{9,13},{10,... | collective-permute-start | bytes 196616 | tf_op jit(solution)/shard_map/ppermute | solution.py:340
  7.4 1.1 %copy-done.3 = bf16[1,512,640]{2,1,0:T(8,128)(2,1)S(1)} copy-done((bf16[1,512,640]{2,1,0:T(8,128)(2,1)S(1)}, bf16[1,512,640]{2,1,0:T(8,128)(2,1)}, u32[]{:S(2)}) %copy-start.3) | copy-done | bytes 655384
  8.5 0.9 %copy-done.4 = bf16[1,256,256]{2,1,0:T(8,128)(2,1)S(1)} copy-done((bf16[1,256,256]{2,1,0:T(8,128)(2,1)S(1)}, bf16[1,256,256]{2,1,0:T(8,128)(2,1)}, u32[]{:S(2)}) %copy-start.4) | copy-done | bytes 131096
  9.4 0.7 copy-done.5
  10.0 0.7 copy-done.7
  10.7 0.7 copy-done.9
  11.3 0.7 weight_rows.1
  12.0 0.0 collective-permute-done.refs_1_
  12.1 1.4 %collective-permute-done.2.refs_3_ = bf16[4,32,256]{2,1,0:T(8,128)(2,1)S(1)} collective-permute-done((bf16[4,32,256]{2,1,0:T(8,128)(2,1)S(1)}, bf16[4,32,256]{2,1,0:T(8,128)(2,1)S(1)}, u32[]{:S(2)}, u32[]{:S(2)}) %collective-permute-start.2) | collective-permute-done | bytes 65568 | tf_op jit(solution)/shard_map/ppermute | solution.py:340
  13.5 1.6 %collective-permute-start.5 = (bf16[4,4,32,256]{3,2,1,0:T(8,128)(2,1)S(1)}, bf16[4,4,32,256]{3,2,1,0:T(8,128)(2,1)S(1)}, u32[]{:S(2)}, u32[]{:S(2)}) collective-permute-start(bf16[4,4,32,256]{3,2,1,0:T(8,128)(2,1)S(1)} %pairs_stack.1.refs_4_.mine_ref), channel_id=1, source_target_pairs={{0,1},{1,0},{2,3},{3,2},{4,5},{5,4},{6,7},{7,6},{8,9},{9,8},{10,11... | collective-permute-start | bytes 786440 | tf_op jit(solution)/shard_map/ppermute | solution.py:340
  15.0 1.6 %collective-permute-start.3 = (bf16[256,256]{1,0:T(8,128)(2,1)S(1)}, bf16[256,256]{1,0:T(8,128)(2,1)S(1)}, u32[]{:S(2)}, u32[]{:S(2)}) collective-permute-start(bf16[256,256]{1,0:T(8,128)(2,1)S(1)} %get-tuple-element.38.refs_2_.refs_4_), channel_id=1, source_target_pairs={{0,4},{1,5},{2,6},{3,7},{4,0},{5,1},{6,2},{7,3},{8,12},{9,13},{10,... | collective-permute-start | bytes 393224 | tf_op jit(solution)/shard_map/ppermute | solution.py:340
  16.6 1.5 %collective-permute-start.4 = (bf16[256,256]{1,0:T(8,128)(2,1)S(1)}, bf16[256,256]{1,0:T(8,128)(2,1)S(1)}, u32[]{:S(2)}, u32[]{:S(2)}) collective-permute-start(bf16[256,256]{1,0:T(8,128)(2,1)S(1)} %get-tuple-element.38.refs_2_.refs_4_), channel_id=1, source_target_pairs={{0,2},{1,3},{2,0},{3,1},{4,6},{5,7},{6,4},{7,5},{8,10},{9,11},{10,... | collective-permute-start | bytes 393224 | tf_op jit(solution)/shard_map/ppermute | solution.py:340
  18.0 0.5 collective-permute-start.7
  18.6 1.5 %stats_own.1.after_ref.refs_0_.refs_2_ = f32[10,8,256]{2,1,0:T(8,128)S(1)} custom-call(bf16[512,640]{1,0:T(8,128)(2,1)S(1)} %bitcast.7, bf16[512,640]{1,0:T(8,128)(2,1)S(1)} %get-tuple-element.37.refs_4_.refs_1_.refs_2_, bf16[256,256]{1,0:T(8,128)(2,1)S(1)} %get-tuple-element.38.refs_2_.refs_4_, bf16[512,256]{1,0:T(8,128)(2,1)S(1)} %bitcast.19, ...), custom_call_target="tpu_custom_call" | custom-call | tf_op jit(solution)/shard_map/stats_own/pallas_call | solution.py:34
  20.1 2.1 %collective-permute-done.3.x_ref = bf16[256,256]{1,0:T(8,128)(2,1)S(1)} collective-permute-done((bf16[256,256]{1,0:T(8,128)(2,1)S(1)}, bf16[256,256]{1,0:T(8,128)(2,1)S(1)}, u32[]{:S(2)}, u32[]{:S(2)}) %collective-permute-start.3) | collective-permute-done | bytes 131104 | tf_op jit(solution)/shard_map/ppermute | solution.py:340
  22.2 0.1 collective-permute-start.6
  22.3 0.6 collective-permute-start.8
  22.9 0.1 collective-permute-done.4.x_ref
  23.0 1.5 %collective-permute-start.9 = (bf16[256,256]{1,0:T(8,128)(2,1)S(1)}, bf16[256,256]{1,0:T(8,128)(2,1)S(1)}, u32[]{:S(2)}, u32[]{:S(2)}) collective-permute-start(bf16[256,256]{1,0:T(8,128)(2,1)S(1)} %pass_on.4.refs_4_), channel_id=1, source_target_pairs={{0,1},{1,0},{2,3},{3,2},{4,5},{5,4},{6,7},{7,6},{8,9},{9,8},{10,11... | collective-permute-start | bytes 393224 | tf_op jit(solution)/shard_map/ppermute | solution.py:340
  24.5 0.7 pairs_route.1
  25.2 2.0 %collective-permute-start.10 = (bf16[4,32,256]{2,1,0:T(8,128)(2,1)S(1)}, bf16[4,32,256]{2,1,0:T(8,128)(2,1)S(1)}, u32[]{:S(2)}, u32[]{:S(2)}) collective-permute-start(bf16[4,32,256]{2,1,0:T(8,128)(2,1)S(1)} %get-tuple-element.44), channel_id=1, source_target_pairs={{0,2},{1,3},{2,0},{3,1},{4,6},{5,7},{6,4},{7,5},{8,10},{9,11},{10,... | collective-permute-start | bytes 196616 | tf_op jit(solution)/shard_map/ppermute | solution.py:340
  27.2 1.4 %collective-permute-start.11 = (bf16[4,32,256]{2,1,0:T(8,128)(2,1)S(1)}, bf16[4,32,256]{2,1,0:T(8,128)(2,1)S(1)}, u32[]{:S(2)}, u32[]{:S(2)}) collective-permute-start(bf16[4,32,256]{2,1,0:T(8,128)(2,1)S(1)} %get-tuple-element.45), channel_id=1, source_target_pairs={{0,4},{1,5},{2,6},{3,7},{4,0},{5,1},{6,2},{7,3},{8,12},{9,13},{10,... | collective-permute-start | bytes 196616 | tf_op jit(solution)/shard_map/ppermute | solution.py:340
  28.6 0.0 collective-permute-done.6.refs_3_.x_ref.refs_5_
  28.6 1.4 %collective-permute-start.12 = (bf16[4,32,256]{2,1,0:T(8,128)(2,1)S(1)}, bf16[4,32,256]{2,1,0:T(8,128)(2,1)S(1)}, u32[]{:S(2)}, u32[]{:S(2)}) collective-permute-start(bf16[4,32,256]{2,1,0:T(8,128)(2,1)S(1)} %get-tuple-element.46), channel_id=1, source_target_pairs={{0,6},{1,7},{2,4},{3,5},{4,2},{5,3},{6,0},{7,1},{8,14},{9,15},{10,... | collective-permute-start | bytes 196616 | tf_op jit(solution)/shard_map/ppermute | solution.py:340
  30.1 1.8 %stats_prompt.2.refs_2_.after_ref = f32[10,8,256]{2,1,0:T(8,128)S(1)} custom-call(bf16[512,640]{1,0:T(8,128)(2,1)S(1)} %bitcast.8, bf16[512,640]{1,0:T(8,128)(2,1)S(1)} %get-tuple-element.37.refs_4_.refs_1_.refs_2_, f32[10,8,256]{2,1,0:T(8,128)S(1)} %stats_own.1.after_ref.refs_0_.refs_2_, bf16[256,256]{1,0:T(8,128)(2,1)S(1)} %pass_on.3.refs_3_.refs_5_, ...), custom_call_target="tpu_custom_call" | custom-call | tf_op jit(solution)/shard_map/stats_prompt/pallas_call | solution.py:34
  31.9 0.0 copy-start.6
  31.9 1.8 %stats_prompt.3.refs_3_ = f32[10,8,256]{2,1,0:T(8,128)S(1)} custom-call(bf16[512,640]{1,0:T(8,128)(2,1)S(1)} %bitcast.9, bf16[512,640]{1,0:T(8,128)(2,1)S(1)} %get-tuple-element.37.refs_4_.refs_1_.refs_2_, f32[10,8,256]{2,1,0:T(8,128)S(1)} %stats_prompt.2.refs_2_.after_ref, bf16[256,256]{1,0:T(8,128)(2,1)S(1)} %collective-permute-done.6.refs_3_.x_ref.refs_5_, ...), custom_call_target="tpu_custom_call" | custom-call | tf_op jit(solution)/shard_map/stats_prompt/pallas_call | solution.py:34
  33.7 0.6 collective-permute-start.13
  34.3 0.5 collective-permute-done.12.refs_9_
  34.8 2.9 %stats_partner.1 = (f32[10,8,256]{2,1,0:T(8,128)S(1)}, bf16[512,256]{1,0:T(8,128)(2,1)S(1)}) custom-call(s32[1,32]{1,0:T(1,128)S(1)} %copy-done.6, bf16[512,640]{1,0:T(8,128)(2,1)S(1)} %bitcast.10, bf16[512,640]{1,0:T(8,128)(2,1)S(1)} %get-tuple-element.37.refs_4_.refs_1_.refs_2_, f32[10,8,256]{2,1,0:T(8,128)S(1)} %stats_prompt.3.refs_3_, ...), custom_call_target="tpu_custom_call" | custom-call | flops 7000000000 | tf_op jit(solution)/shard_map/stats_partner/pallas_call | solution.py:34
  37.7 1.1 %collective-permute-done.13.refs_3_.refs_5_ = bf16[256,256]{1,0:T(8,128)(2,1)S(1)} collective-permute-done((bf16[256,256]{1,0:T(8,128)(2,1)S(1)}, bf16[256,256]{1,0:T(8,128)(2,1)S(1)}, u32[]{:S(2)}, u32[]{:S(2)}) %collective-permute-start.13) | collective-permute-done | bytes 131104 | tf_op jit(solution)/shard_map/ppermute | solution.py:340
  38.8 1.0 %stats_last.1.refs_3_.refs_2_ = f32[10,8,256]{2,1,0:T(8,128)S(1)} custom-call(bf16[512,640]{1,0:T(8,128)(2,1)S(1)} %bitcast.11, bf16[512,640]{1,0:T(8,128)(2,1)S(1)} %get-tuple-element.37.refs_4_.refs_1_.refs_2_, f32[10,8,256]{2,1,0:T(8,128)S(1)} %get-tuple-element.47.refs_2_, bf16[256,256]{1,0:T(8,128)(2,1)S(1)} %collective-permute-done.13.refs_3_.refs_5_), custom_call_target="tpu_custom_call" | custom-call | tf_op jit(solution)/shard_map/stats_last/pallas_call | solution.py:34
  39.8 2.0 %grads_partner.1 = (f32[640,512]{1,0:T(8,128)S(1)}, bf16[4,32,256]{2,1,0:T(8,128)(2,1)S(1)}, bf16[4,32,256]{2,1,0:T(8,128)(2,1)S(1)}, bf16[4,32,256]{2,1,0:T(8,128)(2,1)S(1)}, bf16[4,32,256]{2,1,0:T(8,128)(2,1)S(1)}) custom-call(s32[1,32]{1,0:T(1,128)S(1)} %copy-done.6, bf16[512,640]{1,0:T(8,128)(2,1)S(1)} %bitcast.12, ...), custom_call_target="tpu_custom_call" | custom-call | tf_op jit(solution)/shard_map/grads_partner/pallas_call | solution.py:34
  41.8 0.7 collective-permute-start.14
  42.5 2.3 %collective-permute-start.15 = (bf16[4,32,256]{2,1,0:T(8,128)(2,1)S(1)}, bf16[4,32,256]{2,1,0:T(8,128)(2,1)S(1)}, u32[]{:S(2)}, u32[]{:S(2)}) collective-permute-start(bf16[4,32,256]{2,1,0:T(8,128)(2,1)S(1)} %get-tuple-element.53), channel_id=1, source_target_pairs={{0,4},{1,5},{2,6},{3,7},{4,0},{5,1},{6,2},{7,3},{8,12},{9,13},{10,... | collective-permute-start | bytes 196616 | tf_op jit(solution)/shard_map/ppermute | solution.py:340
  44.8 1.4 %collective-permute-start.16 = (bf16[4,32,256]{2,1,0:T(8,128)(2,1)S(1)}, bf16[4,32,256]{2,1,0:T(8,128)(2,1)S(1)}, u32[]{:S(2)}, u32[]{:S(2)}) collective-permute-start(bf16[4,32,256]{2,1,0:T(8,128)(2,1)S(1)} %get-tuple-element.54), channel_id=1, source_target_pairs={{0,6},{1,7},{2,4},{3,5},{4,2},{5,3},{6,0},{7,1},{8,14},{9,15},{10,... | collective-permute-start | bytes 196616 | tf_op jit(solution)/shard_map/ppermute | solution.py:340
  46.2 3.5 %grads_across.2 = (f32[640,512]{1,0:T(8,128)S(1)}, bf16[512,256]{1,0:T(8,128)(2,1)S(1)}) custom-call(bf16[512,640]{1,0:T(8,128)(2,1)S(1)} %bitcast.13, bf16[512,640]{1,0:T(8,128)(2,1)S(1)} %get-tuple-element.37.refs_4_.refs_1_.refs_2_, f32[10,8,256]{2,1,0:T(8,128)S(1)} %stats_last.1.refs_3_.refs_2_, f32[640,512]{1,0:T(8,128)S(1)} %get-tuple-element.49.refs_3_, ...), custom_call_target="tpu_custom_call" | custom-call | tf_op jit(solution)/shard_map/grads_across/pallas_call | solution.py:34
  49.7 0.6 collective-permute-start.17
  50.3 0.0 collective-permute-done.14.refs_1_
  50.3 0.0 collective-permute-done.15.refs_2_
  50.3 0.5 collective-permute-done.16.refs_3_
  50.9 1.0 %collective-permute-start.22 = (bf16[4,4,32,256]{3,2,1,0:T(8,128)(2,1)S(1)}, bf16[4,4,32,256]{3,2,1,0:T(8,128)(2,1)S(1)}, u32[]{:S(2)}, u32[]{:S(2)}) collective-permute-start(bf16[4,4,32,256]{3,2,1,0:T(8,128)(2,1)S(1)} %terms_stack.1.refs_6_.mine_ref), channel_id=1, source_target_pairs={{0,1},{1,0},{2,3},{3,2},{4,5},{5,4},{6,7},{7,6},{8,9},{9,8},{10,11... | collective-permute-start | bytes 786440 | tf_op jit(solution)/shard_map/ppermute | solution.py:340
  51.9 3.3 %grads_near.1 = (f32[640,512]{1,0:T(8,128)S(1)}, f32[512,256]{1,0:T(8,128)S(1)}) custom-call(bf16[512,640]{1,0:T(8,128)(2,1)S(1)} %bitcast.14, bf16[512,640]{1,0:T(8,128)(2,1)S(1)} %get-tuple-element.37.refs_4_.refs_1_.refs_2_, f32[10,8,256]{2,1,0:T(8,128)S(1)} %stats_last.1.refs_3_.refs_2_, f32[640,512]{1,0:T(8,128)S(1)} %get-tuple-element.50.refs_3_, ...), custom_call_target="tpu_custom_call" | custom-call | flops 7000000000 | tf_op jit(solution)/shard_map/grads_near/pallas_call | solution.py:34
  55.2 3.3 %grads_across.3 = (f32[640,512]{1,0:T(8,128)S(1)}, bf16[512,256]{1,0:T(8,128)(2,1)S(1)}) custom-call(bf16[512,640]{1,0:T(8,128)(2,1)S(1)} %bitcast.15, bf16[512,640]{1,0:T(8,128)(2,1)S(1)} %get-tuple-element.37.refs_4_.refs_1_.refs_2_, f32[10,8,256]{2,1,0:T(8,128)S(1)} %stats_last.1.refs_3_.refs_2_, f32[640,512]{1,0:T(8,128)S(1)} %get-tuple-element.57.refs_3_, ...), custom_call_target="tpu_custom_call" | custom-call | tf_op jit(solution)/shard_map/grads_across/pallas_call | solution.py:34
  58.5 0.0 collective-permute-done.17.refs_1_
  58.5 0.1 collective-permute-start.21
  58.6 1.1 %collective-permute-start.20 = (bf16[512,256]{1,0:T(8,128)(2,1)S(1)}, bf16[512,256]{1,0:T(8,128)(2,1)S(1)}, u32[]{:S(2)}, u32[]{:S(2)}) collective-permute-start(bf16[512,256]{1,0:T(8,128)(2,1)S(1)} %get-tuple-element.58.refs_2_), channel_id=1, source_target_pairs={{0,1},{1,0},{2,3},{3,2},{4,5},{5,4},{6,7},{7,6},{8,9},{9,8},{10,11... | collective-permute-start | bytes 786440 | tf_op jit(solution)/shard_map/ppermute | solution.py:340
  59.7 3.3 %grads_rest.1 = (f32[640,512]{1,0:T(8,128)S(1)}, f32[512,256]{1,0:T(8,128)S(1)}) custom-call(bf16[512,640]{1,0:T(8,128)(2,1)S(1)} %bitcast.16, bf16[512,640]{1,0:T(8,128)(2,1)S(1)} %get-tuple-element.37.refs_4_.refs_1_.refs_2_, f32[10,8,256]{2,1,0:T(8,128)S(1)} %stats_last.1.refs_3_.refs_2_, f32[640,512]{1,0:T(8,128)S(1)} %get-tuple-element.59.refs_3_, ...), custom_call_target="tpu_custom_call" | custom-call | tf_op jit(solution)/shard_map/grads_rest/pallas_call | solution.py:34
  63.0 0.0 collective-permute-done.22.other_ref
  63.0 0.7 terms_route.1
  63.7 1.4 %collective-permute-done.21.x_ref = bf16[512,256]{1,0:T(8,128)(2,1)S(1)} collective-permute-done((bf16[512,256]{1,0:T(8,128)(2,1)S(1)}, bf16[512,256]{1,0:T(8,128)(2,1)S(1)}, u32[]{:S(2)}, u32[]{:S(2)}) %collective-permute-start.21) | collective-permute-done | bytes 262176 | tf_op jit(solution)/shard_map/ppermute | solution.py:340
  65.2 0.0 copy-start.8
  65.2 2.8 %collective-permute-start.23 = (bf16[384,256]{1,0:T(8,128)(2,1)S(1)}, bf16[384,256]{1,0:T(8,128)(2,1)S(1)}, u32[]{:S(2)}, u32[]{:S(2)}) collective-permute-start(bf16[384,256]{1,0:T(8,128)(2,1)S(1)} %sum_far.1.refs_5_), channel_id=1, source_target_pairs={{0,4},{1,5},{2,6},{3,7},{4,0},{5,1},{6,2},{7,3},{8,12},{9,13},{10,... | collective-permute-start | bytes 589832 | tf_op jit(solution)/shard_map/ppermute | solution.py:340
  68.0 1.2 %collective-permute-start.24 = (bf16[4,32,256]{2,1,0:T(8,128)(2,1)S(1)}, bf16[4,32,256]{2,1,0:T(8,128)(2,1)S(1)}, u32[]{:S(2)}, u32[]{:S(2)}) collective-permute-start(bf16[4,32,256]{2,1,0:T(8,128)(2,1)S(1)} %get-tuple-element.66), channel_id=1, source_target_pairs={{0,2},{1,3},{2,0},{3,1},{4,6},{5,7},{6,4},{7,5},{8,10},{9,11},{10,... | collective-permute-start | bytes 196616 | tf_op jit(solution)/shard_map/ppermute | solution.py:340
  69.2 0.5 collective-permute-start.25
  69.7 1.1 %collective-permute-done.18.y_ref = s32[1,16]{1,0:T(1,128)S(1)} collective-permute-done((s32[1,16]{1,0:T(1,128)S(1)}, s32[1,16]{1,0:T(1,128)S(1)}, u32[]{:S(2)}, u32[]{:S(2)}) %collective-permute-start.18) | collective-permute-done | bytes 96 | tf_op jit(solution)/shard_map/ppermute | solution.py:340
  70.8 1.5 %collective-permute-start.19 = (s32[1,16]{1,0:T(1,128)S(1)}, s32[1,16]{1,0:T(1,128)S(1)}, u32[]{:S(2)}, u32[]{:S(2)}) collective-permute-start(s32[1,16]{1,0:T(1,128)S(1)} %add_lengths.2.x_ref), channel_id=1, source_target_pairs={{0,16},{8,24},{16,0},{24,8},{1,17},{9,25},{17,1},{25,9},{2,18},{10... | collective-permute-start | bytes 200 | tf_op jit(solution)/shard_map/ppermute | solution.py:340
  72.3 1.5 %grads_own.1 = (f32[640,512]{1,0:T(8,128)S(1)}, f32[512,256]{1,0:T(8,128)S(1)}) custom-call(bf16[512,640]{1,0:T(8,128)(2,1)S(1)} %bitcast.17, bf16[512,640]{1,0:T(8,128)(2,1)S(1)} %get-tuple-element.37.refs_4_.refs_1_.refs_2_, f32[10,8,256]{2,1,0:T(8,128)S(1)} %stats_last.1.refs_3_.refs_2_, f32[640,512]{1,0:T(8,128)S(1)} %get-tuple-element.61.refs_3_, ...), custom_call_target="tpu_custom_call" | custom-call | tf_op jit(solution)/shard_map/grads_own/pallas_call | solution.py:34
  73.9 0.5 collective-permute-done.19.y_ref
  74.4 0.1 collective-permute-done.23.refs_1_.refs_5_
  74.5 0.8 %collective-permute-done.25.refs_6_ = bf16[4,32,256]{2,1,0:T(8,128)(2,1)S(1)} collective-permute-done((bf16[4,32,256]{2,1,0:T(8,128)(2,1)S(1)}, bf16[4,32,256]{2,1,0:T(8,128)(2,1)S(1)}, u32[]{:S(2)}, u32[]{:S(2)}) %collective-permute-start.25) | collective-permute-done | bytes 65568 | tf_op jit(solution)/shard_map/ppermute | solution.py:340
  75.3 1.8 %over_count.1 = (bf16[512,640]{1,0:T(8,128)(2,1)}, bf16[512,256]{1,0:T(8,128)(2,1)}, bf16[256,256]{1,0:T(8,128)(2,1)}) custom-call(s32[1,32]{1,0:T(1,128)S(1)} %copy-done.6, s32[1,16]{1,0:T(1,128)S(1)} %add_lengths.3.lengths_ref, f32[640,512]{1,0:T(8,128)S(1)} %get-tuple-element.65.refs_0_, f32[512,256]{1,0:T(8,128)S(1)} %get-tuple-element.64.after_ref.refs_2_.refs_1_, ...), custom_call_target="tpu_custom_call" | custom-call | tf_op jit(solution)/shard_map/over_count/pallas_call | solution.py:34
  (37 shorter events, 0.3 us)
Async XLA Ops:
  0.6 18.0 %copy-start = (bf16[1,512,640]{2,1,0:T(8,128)(2,1)S(1)}, bf16[1,512,640]{2,1,0:T(8,128)(2,1)}, u32[]{:S(2)}) copy-start(bf16[1,512,640]{2,1,0:T(8,128)(2,1)} %param.7) | copy-start | bytes 1966084
  0.6 1.0 %copy-start.1 = (bf16[1,512,256]{2,1,0:T(8,128)(2,1)S(1)}, bf16[1,512,256]{2,1,0:T(8,128)(2,1)}, u32[]{:S(2)}) copy-start(bf16[1,512,256]{2,1,0:T(8,128)(2,1)} %param.8) | copy-start | bytes 786436
  1.7 16.9 %copy-start.2 = (bf16[1,512,256]{2,1,0:T(8,128)(2,1)S(1)}, bf16[1,512,256]{2,1,0:T(8,128)(2,1)}, u32[]{:S(2)}) copy-start(bf16[1,512,256]{2,1,0:T(8,128)(2,1)} %param.8) | copy-start | bytes 786436
  1.7 10.4 %collective-permute-start = (bf16[4,32,256]{2,1,0:T(8,128)(2,1)S(1)}, bf16[4,32,256]{2,1,0:T(8,128)(2,1)S(1)}, u32[]{:S(2)}, u32[]{:S(2)}) collective-permute-start(bf16[4,32,256]{2,1,0:T(8,128)(2,1)S(1)} %get-tuple-element.40), channel_id=1, source_target_pairs={{0,2},{1,3},{2,0},{3,1},{4,6},{5,7},{6,4},{7,5},{8,10},{9,11},{10,... | collective-permute-start | bytes 196616 | tf_op jit(solution)/shard_map/ppermute | solution.py:340
  4.8 7.3 %collective-permute-start.1 = (bf16[4,32,256]{2,1,0:T(8,128)(2,1)S(1)}, bf16[4,32,256]{2,1,0:T(8,128)(2,1)S(1)}, u32[]{:S(2)}, u32[]{:S(2)}) collective-permute-start(bf16[4,32,256]{2,1,0:T(8,128)(2,1)S(1)} %get-tuple-element.41), channel_id=1, source_target_pairs={{0,4},{1,5},{2,6},{3,7},{4,0},{5,1},{6,2},{7,3},{8,12},{9,13},{10,... | collective-permute-start | bytes 196616 | tf_op jit(solution)/shard_map/ppermute | solution.py:340
  7.4 6.1 %collective-permute-start.2 = (bf16[4,32,256]{2,1,0:T(8,128)(2,1)S(1)}, bf16[4,32,256]{2,1,0:T(8,128)(2,1)S(1)}, u32[]{:S(2)}, u32[]{:S(2)}) collective-permute-start(bf16[4,32,256]{2,1,0:T(8,128)(2,1)S(1)} %get-tuple-element.42), channel_id=1, source_target_pairs={{0,6},{1,7},{2,4},{3,5},{4,2},{5,3},{6,0},{7,1},{8,14},{9,15},{10,... | collective-permute-start | bytes 196616 | tf_op jit(solution)/shard_map/ppermute | solution.py:340
  7.4 1.1 %copy-start.3 = (bf16[1,512,640]{2,1,0:T(8,128)(2,1)S(1)}, bf16[1,512,640]{2,1,0:T(8,128)(2,1)}, u32[]{:S(2)}) copy-start(bf16[1,512,640]{2,1,0:T(8,128)(2,1)} %param.10) | copy-start | bytes 1966084
  8.5 0.9 %copy-start.4 = (bf16[1,256,256]{2,1,0:T(8,128)(2,1)S(1)}, bf16[1,256,256]{2,1,0:T(8,128)(2,1)}, u32[]{:S(2)}) copy-start(bf16[1,256,256]{2,1,0:T(8,128)(2,1)} %param.9) | copy-start | bytes 393220
  9.4 0.7 copy-start.5
  10.0 0.7 copy-start.7
  10.7 0.7 copy-start.9
  13.5 11.0 %collective-permute-start.5 = (bf16[4,4,32,256]{3,2,1,0:T(8,128)(2,1)S(1)}, bf16[4,4,32,256]{3,2,1,0:T(8,128)(2,1)S(1)}, u32[]{:S(2)}, u32[]{:S(2)}) collective-permute-start(bf16[4,4,32,256]{3,2,1,0:T(8,128)(2,1)S(1)} %pairs_stack.1.refs_4_.mine_ref), channel_id=1, source_target_pairs={{0,1},{1,0},{2,3},{3,2},{4,5},{5,4},{6,7},{7,6},{8,9},{9,8},{10,11... | collective-permute-start | bytes 786440 | tf_op jit(solution)/shard_map/ppermute | solution.py:340
  15.0 7.2 %collective-permute-start.3 = (bf16[256,256]{1,0:T(8,128)(2,1)S(1)}, bf16[256,256]{1,0:T(8,128)(2,1)S(1)}, u32[]{:S(2)}, u32[]{:S(2)}) collective-permute-start(bf16[256,256]{1,0:T(8,128)(2,1)S(1)} %get-tuple-element.38.refs_2_.refs_4_), channel_id=1, source_target_pairs={{0,4},{1,5},{2,6},{3,7},{4,0},{5,1},{6,2},{7,3},{8,12},{9,13},{10,... | collective-permute-start | bytes 393224 | tf_op jit(solution)/shard_map/ppermute | solution.py:340
  16.6 6.4 %collective-permute-start.4 = (bf16[256,256]{1,0:T(8,128)(2,1)S(1)}, bf16[256,256]{1,0:T(8,128)(2,1)S(1)}, u32[]{:S(2)}, u32[]{:S(2)}) collective-permute-start(bf16[256,256]{1,0:T(8,128)(2,1)S(1)} %get-tuple-element.38.refs_2_.refs_4_), channel_id=1, source_target_pairs={{0,2},{1,3},{2,0},{3,1},{4,6},{5,7},{6,4},{7,5},{8,10},{9,11},{10,... | collective-permute-start | bytes 393224 | tf_op jit(solution)/shard_map/ppermute | solution.py:340
  18.0 9.2 %collective-permute-start.7 = (bf16[256,256]{1,0:T(8,128)(2,1)S(1)}, bf16[256,256]{1,0:T(8,128)(2,1)S(1)}, u32[]{:S(2)}, u32[]{:S(2)}) collective-permute-start(bf16[256,256]{1,0:T(8,128)(2,1)S(1)} %get-tuple-element.38.refs_2_.refs_4_), channel_id=1, source_target_pairs={{0,1},{1,0},{2,3},{3,2},{4,5},{5,4},{6,7},{7,6},{8,9},{9,8},{10,11... | collective-permute-start | bytes 393224 | tf_op jit(solution)/shard_map/ppermute | solution.py:340
  22.2 6.4 %collective-permute-start.6 = (bf16[256,256]{1,0:T(8,128)(2,1)S(1)}, bf16[256,256]{1,0:T(8,128)(2,1)S(1)}, u32[]{:S(2)}, u32[]{:S(2)}) collective-permute-start(bf16[256,256]{1,0:T(8,128)(2,1)S(1)} %pass_on.3.refs_3_.refs_5_), channel_id=1, source_target_pairs={{0,2},{1,3},{2,0},{3,1},{4,6},{5,7},{6,4},{7,5},{8,10},{9,11},{10,... | collective-permute-start | bytes 393224 | tf_op jit(solution)/shard_map/ppermute | solution.py:340
  22.3 11.4 %collective-permute-start.8 = (bf16[256,256]{1,0:T(8,128)(2,1)S(1)}, bf16[256,256]{1,0:T(8,128)(2,1)S(1)}, u32[]{:S(2)}, u32[]{:S(2)}) collective-permute-start(bf16[256,256]{1,0:T(8,128)(2,1)S(1)} %pass_on.3.refs_3_.refs_5_), channel_id=1, source_target_pairs={{0,1},{1,0},{2,3},{3,2},{4,5},{5,4},{6,7},{7,6},{8,9},{9,8},{10,11... | collective-permute-start | bytes 393224 | tf_op jit(solution)/shard_map/ppermute | solution.py:340
  23.0 11.3 %collective-permute-start.9 = (bf16[256,256]{1,0:T(8,128)(2,1)S(1)}, bf16[256,256]{1,0:T(8,128)(2,1)S(1)}, u32[]{:S(2)}, u32[]{:S(2)}) collective-permute-start(bf16[256,256]{1,0:T(8,128)(2,1)S(1)} %pass_on.4.refs_4_), channel_id=1, source_target_pairs={{0,1},{1,0},{2,3},{3,2},{4,5},{5,4},{6,7},{7,6},{8,9},{9,8},{10,11... | collective-permute-start | bytes 393224 | tf_op jit(solution)/shard_map/ppermute | solution.py:340
  25.2 9.1 %collective-permute-start.10 = (bf16[4,32,256]{2,1,0:T(8,128)(2,1)S(1)}, bf16[4,32,256]{2,1,0:T(8,128)(2,1)S(1)}, u32[]{:S(2)}, u32[]{:S(2)}) collective-permute-start(bf16[4,32,256]{2,1,0:T(8,128)(2,1)S(1)} %get-tuple-element.44), channel_id=1, source_target_pairs={{0,2},{1,3},{2,0},{3,1},{4,6},{5,7},{6,4},{7,5},{8,10},{9,11},{10,... | collective-permute-start | bytes 196616 | tf_op jit(solution)/shard_map/ppermute | solution.py:340
  27.2 7.1 %collective-permute-start.11 = (bf16[4,32,256]{2,1,0:T(8,128)(2,1)S(1)}, bf16[4,32,256]{2,1,0:T(8,128)(2,1)S(1)}, u32[]{:S(2)}, u32[]{:S(2)}) collective-permute-start(bf16[4,32,256]{2,1,0:T(8,128)(2,1)S(1)} %get-tuple-element.45), channel_id=1, source_target_pairs={{0,4},{1,5},{2,6},{3,7},{4,0},{5,1},{6,2},{7,3},{8,12},{9,13},{10,... | collective-permute-start | bytes 196616 | tf_op jit(solution)/shard_map/ppermute | solution.py:340
  28.6 6.2 %collective-permute-start.12 = (bf16[4,32,256]{2,1,0:T(8,128)(2,1)S(1)}, bf16[4,32,256]{2,1,0:T(8,128)(2,1)S(1)}, u32[]{:S(2)}, u32[]{:S(2)}) collective-permute-start(bf16[4,32,256]{2,1,0:T(8,128)(2,1)S(1)} %get-tuple-element.46), channel_id=1, source_target_pairs={{0,6},{1,7},{2,4},{3,5},{4,2},{5,3},{6,0},{7,1},{8,14},{9,15},{10,... | collective-permute-start | bytes 196616 | tf_op jit(solution)/shard_map/ppermute | solution.py:340
  31.9 2.9 %copy-start.6 = (s32[1,32]{1,0:T(1,128)S(1)}, s32[1,32]{1,0:T(1,128)}, u32[]{:S(2)}) copy-start(s32[1,32]{1,0:T(1,128)} %plan_ref.7) | copy-start | bytes 388
  33.7 5.0 %collective-permute-start.13 = (bf16[256,256]{1,0:T(8,128)(2,1)S(1)}, bf16[256,256]{1,0:T(8,128)(2,1)S(1)}, u32[]{:S(2)}, u32[]{:S(2)}) collective-permute-start(bf16[256,256]{1,0:T(8,128)(2,1)S(1)} %pass_on.5), channel_id=1, source_target_pairs={{0,1},{1,0},{2,3},{3,2},{4,5},{5,4},{6,7},{7,6},{8,9},{9,8},{10,11... | collective-permute-start | bytes 393224 | tf_op jit(solution)/shard_map/ppermute | solution.py:340
  41.8 8.5 %collective-permute-start.14 = (bf16[4,32,256]{2,1,0:T(8,128)(2,1)S(1)}, bf16[4,32,256]{2,1,0:T(8,128)(2,1)S(1)}, u32[]{:S(2)}, u32[]{:S(2)}) collective-permute-start(bf16[4,32,256]{2,1,0:T(8,128)(2,1)S(1)} %get-tuple-element.52), channel_id=1, source_target_pairs={{0,2},{1,3},{2,0},{3,1},{4,6},{5,7},{6,4},{7,5},{8,10},{9,11},{10,... | collective-permute-start | bytes 196616 | tf_op jit(solution)/shard_map/ppermute | solution.py:340
  42.5 7.8 %collective-permute-start.15 = (bf16[4,32,256]{2,1,0:T(8,128)(2,1)S(1)}, bf16[4,32,256]{2,1,0:T(8,128)(2,1)S(1)}, u32[]{:S(2)}, u32[]{:S(2)}) collective-permute-start(bf16[4,32,256]{2,1,0:T(8,128)(2,1)S(1)} %get-tuple-element.53), channel_id=1, source_target_pairs={{0,4},{1,5},{2,6},{3,7},{4,0},{5,1},{6,2},{7,3},{8,12},{9,13},{10,... | collective-permute-start | bytes 196616 | tf_op jit(solution)/shard_map/ppermute | solution.py:340
  44.8 6.1 %collective-permute-start.16 = (bf16[4,32,256]{2,1,0:T(8,128)(2,1)S(1)}, bf16[4,32,256]{2,1,0:T(8,128)(2,1)S(1)}, u32[]{:S(2)}, u32[]{:S(2)}) collective-permute-start(bf16[4,32,256]{2,1,0:T(8,128)(2,1)S(1)} %get-tuple-element.54), channel_id=1, source_target_pairs={{0,6},{1,7},{2,4},{3,5},{4,2},{5,3},{6,0},{7,1},{8,14},{9,15},{10,... | collective-permute-start | bytes 196616 | tf_op jit(solution)/shard_map/ppermute | solution.py:340
  49.7 8.7 %collective-permute-start.17 = (bf16[512,256]{1,0:T(8,128)(2,1)S(1)}, bf16[512,256]{1,0:T(8,128)(2,1)S(1)}, u32[]{:S(2)}, u32[]{:S(2)}) collective-permute-start(bf16[512,256]{1,0:T(8,128)(2,1)S(1)} %get-tuple-element.55.refs_4_), channel_id=1, source_target_pairs={{0,1},{1,0},{2,3},{3,2},{4,5},{5,4},{6,7},{7,6},{8,9},{9,8},{10,11... | collective-permute-start | bytes 786440 | tf_op jit(solution)/shard_map/ppermute | solution.py:340
  50.9 12.1 %collective-permute-start.22 = (bf16[4,4,32,256]{3,2,1,0:T(8,128)(2,1)S(1)}, bf16[4,4,32,256]{3,2,1,0:T(8,128)(2,1)S(1)}, u32[]{:S(2)}, u32[]{:S(2)}) collective-permute-start(bf16[4,4,32,256]{3,2,1,0:T(8,128)(2,1)S(1)} %terms_stack.1.refs_6_.mine_ref), channel_id=1, source_target_pairs={{0,1},{1,0},{2,3},{3,2},{4,5},{5,4},{6,7},{7,6},{8,9},{9,8},{10,11... | collective-permute-start | bytes 786440 | tf_op jit(solution)/shard_map/ppermute | solution.py:340
  58.5 6.6 %collective-permute-start.21 = (bf16[512,256]{1,0:T(8,128)(2,1)S(1)}, bf16[512,256]{1,0:T(8,128)(2,1)S(1)}, u32[]{:S(2)}, u32[]{:S(2)}) collective-permute-start(bf16[512,256]{1,0:T(8,128)(2,1)S(1)} %sum_near.1.after_ref.refs_6_), channel_id=1, source_target_pairs={{0,2},{1,3},{2,0},{3,1},{4,6},{5,7},{6,4},{7,5},{8,10},{9,11},{10,... | collective-permute-start | bytes 786440 | tf_op jit(solution)/shard_map/ppermute | solution.py:340
  58.6 6.6 %collective-permute-start.20 = (bf16[512,256]{1,0:T(8,128)(2,1)S(1)}, bf16[512,256]{1,0:T(8,128)(2,1)S(1)}, u32[]{:S(2)}, u32[]{:S(2)}) collective-permute-start(bf16[512,256]{1,0:T(8,128)(2,1)S(1)} %get-tuple-element.58.refs_2_), channel_id=1, source_target_pairs={{0,1},{1,0},{2,3},{3,2},{4,5},{5,4},{6,7},{7,6},{8,9},{9,8},{10,11... | collective-permute-start | bytes 786440 | tf_op jit(solution)/shard_map/ppermute | solution.py:340
  65.2 4.5 %copy-start.8 = (s32[1,16]{1,0:T(1,128)S(1)}, s32[1,16]{1,0:T(1,128)}, u32[]{:S(2)}) copy-start(s32[1,16]{1,0:T(1,128)} %x_ref.1) | copy-start | bytes 196
  65.2 9.2 %collective-permute-start.23 = (bf16[384,256]{1,0:T(8,128)(2,1)S(1)}, bf16[384,256]{1,0:T(8,128)(2,1)S(1)}, u32[]{:S(2)}, u32[]{:S(2)}) collective-permute-start(bf16[384,256]{1,0:T(8,128)(2,1)S(1)} %sum_far.1.refs_5_), channel_id=1, source_target_pairs={{0,4},{1,5},{2,6},{3,7},{4,0},{5,1},{6,2},{7,3},{8,12},{9,13},{10,... | collective-permute-start | bytes 589832 | tf_op jit(solution)/shard_map/ppermute | solution.py:340
  68.0 6.5 %collective-permute-start.24 = (bf16[4,32,256]{2,1,0:T(8,128)(2,1)S(1)}, bf16[4,32,256]{2,1,0:T(8,128)(2,1)S(1)}, u32[]{:S(2)}, u32[]{:S(2)}) collective-permute-start(bf16[4,32,256]{2,1,0:T(8,128)(2,1)S(1)} %get-tuple-element.66), channel_id=1, source_target_pairs={{0,2},{1,3},{2,0},{3,1},{4,6},{5,7},{6,4},{7,5},{8,10},{9,11},{10,... | collective-permute-start | bytes 196616 | tf_op jit(solution)/shard_map/ppermute | solution.py:340
  69.2 6.2 %collective-permute-start.25 = (bf16[4,32,256]{2,1,0:T(8,128)(2,1)S(1)}, bf16[4,32,256]{2,1,0:T(8,128)(2,1)S(1)}, u32[]{:S(2)}, u32[]{:S(2)}) collective-permute-start(bf16[4,32,256]{2,1,0:T(8,128)(2,1)S(1)} %get-tuple-element.67), channel_id=1, source_target_pairs={{0,6},{1,7},{2,4},{3,5},{4,2},{5,3},{6,0},{7,1},{8,14},{9,15},{10,... | collective-permute-start | bytes 196616 | tf_op jit(solution)/shard_map/ppermute | solution.py:340
  69.7 1.1 %collective-permute-start.18 = (s32[1,16]{1,0:T(1,128)S(1)}, s32[1,16]{1,0:T(1,128)S(1)}, u32[]{:S(2)}, u32[]{:S(2)}) collective-permute-start(s32[1,16]{1,0:T(1,128)S(1)} %pass_lengths.1.x_ref), channel_id=1, source_target_pairs={{0,8},{8,0},{16,24},{24,16},{1,9},{9,1},{17,25},{25,17},{2,10},{10... | collective-permute-start | bytes 200 | tf_op jit(solution)/shard_map/ppermute | solution.py:340
  70.8 3.5 %collective-permute-start.19 = (s32[1,16]{1,0:T(1,128)S(1)}, s32[1,16]{1,0:T(1,128)S(1)}, u32[]{:S(2)}, u32[]{:S(2)}) collective-permute-start(s32[1,16]{1,0:T(1,128)S(1)} %add_lengths.2.x_ref), channel_id=1, source_target_pairs={{0,16},{8,24},{16,0},{24,8},{1,17},{9,25},{17,1},{25,9},{2,18},{10... | collective-permute-start | bytes 200 | tf_op jit(solution)/shard_map/ppermute | solution.py:340

commit v5 on v4

--- a/solution.py
+++ b/solution.py
@@ -29,14 +29,14 @@
     return lax.dot_general(a, b, dims, preferred_element_type=F32)
 
 
-def call(kernel, name, out_shape, specs, args, scratch=(), after=(), beside=False):
+def call(kernel, name, out_shape, specs, args, scratch=(), after=(), beside=False, out_spec=VMEM):
     specs, args = [*specs, *[ANY] * len(after)], [*args, *after]
     return pl.pallas_call(
         kernel,
         name=name,
         out_shape=out_shape,
         in_specs=specs,
-        out_specs=jax.tree.map(lambda _: VMEM, out_shape),
+        out_specs=jax.tree.map(lambda _: out_spec, out_shape),
         scratch_shapes=list(scratch),
         compiler_params=pltpu.CompilerParams(vmem_limit_bytes=24 * 2**20),
         cost_estimate=pl.CostEstimate(flops=COVER * beside, bytes_accessed=0, transcendentals=0),
@@ -282,19 +282,27 @@
         kv_out[:, side] = (kv_sum[:, side] * factor).astype(kv_out.dtype)
 
 
+def turn_kernel(x_ref, after_ref, out_ref):
+    for h in range(x_ref.shape[0] // BLK):
+        cols = slice(h * BLK, (h + 1) * BLK)
+        out_ref[:, cols] = x_ref[cols, :].T
+
+
 def finish_kernel(back, start, plan_ref, lengths_ref, *refs):
     total = jnp.int32(0)
     for r in range(RESP):
         total = total + lengths_ref[0, r]
     share = 1.0 / jnp.full((1, BLK), total.astype(F32))
-    (dq_ref, own_ref, prompt_ref), pieces = refs[:3], refs[3:-4]
-    dq_out, stream_out, prompt_out, held = refs[-4:]
+    (dq_ref, own_ref, prompt_ref), pieces = refs[:3], refs[3:-8]
+    outs = refs[-8:-5]
+    held, dq_out, stream_out, prompt_out, sems = refs[-5:]
+    leaving = [dq_out, stream_out, prompt_out]
+    copies = [pltpu.make_async_copy(a, b, sems.at[i]) for i, (a, b) in enumerate(zip(leaving, outs))]
     join_pieces(pieces, held, start)
     me = lax.axis_index("seq")
     local = own_ref.shape[0] // BLK
-    for h in range(dq_ref.shape[0] // BLK):
-        cols = slice(h * BLK, (h + 1) * BLK)
-        dq_out[:, cols] = (dq_ref[cols, :] * (share[:, :1] * back)).astype(BF16).T
+    dq_out[...] = (dq_ref[...] * (share[:, :1] * back)).astype(BF16)
+    copies[0].start()
     for cols in (KEYS, VALUES):
         for s in range(local):
             rows = slice(s * BLK, (s + 1) * BLK)
@@ -303,6 +311,10 @@
             stream = own_ref[rows, cols] + jnp.where(odd_rows, 0.0, held[rows, cols].astype(F32))
             stream_out[rows, cols] = (stream * share).astype(BF16)
         prompt_out[:, cols] = (prompt_ref[:, cols] * share).astype(BF16)
+    for copy in copies[1:]:
+        copy.start()
+    for copy in copies:
+        copy.wait()
 
 
 def pick_kernel(per, parts, picked, joined, ordered, *refs):
@@ -482,13 +494,14 @@
         total, step = added(total, step, sent), 2
     routed = deliver("terms", mine, after=[sent])
     returned = {k: routed[k] if k == 0 else swap(routed[k], "seq", 2 * k) for k in range(line) if k != 2}
+    dq, own_terms = grads("grads_own", dq, [], own=resp, after=[routed[0]])
     sums_on = call(
         pass_kernel,
         "pass_sums",
         jax.ShapeDtypeStruct(sums.shape, BF16),
         [VMEM],
         [sums],
-        after=[routed[0]],
+        after=[own_terms],
         beside=True,
     )
     held, parts, extra, order = rest, [sent], [far_rest, sums_on], []
@@ -502,10 +515,11 @@
         held, parts, extra, order = [held[i] for i in keep], [kept], [swap(leaving, "seq", bit)], []
         if bit == 4:
             returned[2], start = extra[0], per * len(send)
-            dq, own_terms = grads("grads_own", dq, [], own=resp, after=[leaving])
+            shape = jax.ShapeDtypeStruct(q.shape, F32)
+            turned = call(turn_kernel, "turn_queries", shape, [VMEM], [dq], after=[leaving])
         bit *= 2
     while step < groups:
-        total = added(total, step, own_terms)
+        total = added(total, step, turned)
         step *= 2
     prompt_sum = pick("sum_prompt", parts, extra, [0], F32, after=[own_terms])
     grad_query, grad_stream, grad_prompt = call(
@@ -513,8 +527,12 @@
         "over_count",
         [jax.ShapeDtypeStruct(x.shape, BF16) for x in (q, resp, prompt)],
         [SMEM] * 2 + [VMEM] * (3 + line),
-        [block_order, total, dq, own_terms, prompt_sum, *[returned[k] for k in range(line)]],
-        [pltpu.VMEM(resp.shape, BF16)],
+        [block_order, total, turned, own_terms, prompt_sum, *[returned[k] for k in range(line)]],
+        [
+            *[pltpu.VMEM(x.shape, BF16) for x in (resp, q, resp, prompt)],
+            pltpu.SemaphoreType.DMA((3,)),
+        ],
+        out_spec=ANY,
     )
     return grad_query[None], grad_stream[None], grad_prompt[None]
 

time: 77.3 us -> 77.4 us (level)
    pallas_call x29 -> x30, Pallas kernels: 29.9 us -> 30.3 us  [call(): pl.pallas_call(kernel, name=name, out_shape=out_shape, in_specs=specs, ou...]
  transfers between devices with their start and end apart: 26 -> 26, of which waited for: 11 -> 9; matrix products, arithmetic and copies ran while one was open for 0% -> 0% of each run, Pallas kernels for 33% -> 33%
where the time goes in v5:
time: 77.4 us; the launch traced here: 77.2 us
  starting transfers between devices  31.6 us (41%)
  Pallas kernels  30.3 us (39%)
  waiting for transfers between devices  9.22 us (12%)
  local copies, waits for them, and re-layouts  4.98 us (6%)
  between operations  1.09 us (1%)
    ppermute x26, starting transfers between devices, swap(): return lax.ppermute(x, axis, [(i, i ^ k) for i in range(size)])  31.6 us
    pallas_call x30, Pallas kernels, call(): pl.pallas_call(kernel, name=name, out_shape=out_shape, in_specs=specs, ou...  30.3 us
    ppermute x26, waiting for transfers between devices, swap(): return lax.ppermute(x, axis, [(i, i ^ k) for i in range(size)])  9.22 us
    unnamed x20, local copies, waits for them, and re-layouts  4.98 us
  transfers between devices with their start and end apart: 26, of which 9 were waited for; matrix products, arithmetic and copies ran while one was open for 0% of the time, Pallas kernels for 33%

profile of v5, /device:TPU:0, one launch (start us, length us, event | category | flops | bytes accessed | tf_op | source)
XLA Modules:
  0.0 77.2 jit_solution(16013711589637784402)
XLA Ops:
  0.6 1.0 %copy-done.1 = bf16[1,512,256]{2,1,0:T(8,128)(2,1)S(1)} copy-done((bf16[1,512,256]{2,1,0:T(8,128)(2,1)S(1)}, bf16[1,512,256]{2,1,0:T(8,128)(2,1)}, u32[]{:S(2)}) %copy-start.1) | copy-done | bytes 262168
  1.7 3.1 %collective-permute-start = (bf16[4,32,256]{2,1,0:T(8,128)(2,1)S(1)}, bf16[4,32,256]{2,1,0:T(8,128)(2,1)S(1)}, u32[]{:S(2)}, u32[]{:S(2)}) collective-permute-start(bf16[4,32,256]{2,1,0:T(8,128)(2,1)S(1)} %get-tuple-element.40), channel_id=1, source_target_pairs={{0,2},{1,3},{2,0},{3,1},{4,6},{5,7},{6,4},{7,5},{8,10},{9,11},{10,... | collective-permute-start | bytes 196616 | tf_op jit(solution)/shard_map/ppermute | solution.py:352
  4.8 2.6 %collective-permute-start.1 = (bf16[4,32,256]{2,1,0:T(8,128)(2,1)S(1)}, bf16[4,32,256]{2,1,0:T(8,128)(2,1)S(1)}, u32[]{:S(2)}, u32[]{:S(2)}) collective-permute-start(bf16[4,32,256]{2,1,0:T(8,128)(2,1)S(1)} %get-tuple-element.41), channel_id=1, source_target_pairs={{0,4},{1,5},{2,6},{3,7},{4,0},{5,1},{6,2},{7,3},{8,12},{9,13},{10,... | collective-permute-start | bytes 196616 | tf_op jit(solution)/shard_map/ppermute | solution.py:352
  7.4 0.0 collective-permute-start.2
  7.4 1.1 %copy-done.3 = bf16[1,512,640]{2,1,0:T(8,128)(2,1)S(1)} copy-done((bf16[1,512,640]{2,1,0:T(8,128)(2,1)S(1)}, bf16[1,512,640]{2,1,0:T(8,128)(2,1)}, u32[]{:S(2)}) %copy-start.3) | copy-done | bytes 655384
  8.5 0.9 %copy-done.4 = bf16[1,256,256]{2,1,0:T(8,128)(2,1)S(1)} copy-done((bf16[1,256,256]{2,1,0:T(8,128)(2,1)S(1)}, bf16[1,256,256]{2,1,0:T(8,128)(2,1)}, u32[]{:S(2)}) %copy-start.4) | copy-done | bytes 131096
  9.4 0.7 copy-done.5
  10.0 0.7 copy-done.7
  10.7 0.7 copy-done.9
  11.3 0.7 weight_rows.1
  12.0 0.0 collective-permute-done.refs_1_
  12.1 1.4 %collective-permute-done.2.refs_3_ = bf16[4,32,256]{2,1,0:T(8,128)(2,1)S(1)} collective-permute-done((bf16[4,32,256]{2,1,0:T(8,128)(2,1)S(1)}, bf16[4,32,256]{2,1,0:T(8,128)(2,1)S(1)}, u32[]{:S(2)}, u32[]{:S(2)}) %collective-permute-start.2) | collective-permute-done | bytes 65568 | tf_op jit(solution)/shard_map/ppermute | solution.py:352
  13.5 1.6 %collective-permute-start.5 = (bf16[4,4,32,256]{3,2,1,0:T(8,128)(2,1)S(1)}, bf16[4,4,32,256]{3,2,1,0:T(8,128)(2,1)S(1)}, u32[]{:S(2)}, u32[]{:S(2)}) collective-permute-start(bf16[4,4,32,256]{3,2,1,0:T(8,128)(2,1)S(1)} %pairs_stack.1.refs_4_.mine_ref), channel_id=1, source_target_pairs={{0,1},{1,0},{2,3},{3,2},{4,5},{5,4},{6,7},{7,6},{8,9},{9,8},{10,11... | collective-permute-start | bytes 786440 | tf_op jit(solution)/shard_map/ppermute | solution.py:352
  15.0 1.6 %collective-permute-start.3 = (bf16[256,256]{1,0:T(8,128)(2,1)S(1)}, bf16[256,256]{1,0:T(8,128)(2,1)S(1)}, u32[]{:S(2)}, u32[]{:S(2)}) collective-permute-start(bf16[256,256]{1,0:T(8,128)(2,1)S(1)} %get-tuple-element.38.refs_2_.refs_4_), channel_id=1, source_target_pairs={{0,4},{1,5},{2,6},{3,7},{4,0},{5,1},{6,2},{7,3},{8,12},{9,13},{10,... | collective-permute-start | bytes 393224 | tf_op jit(solution)/shard_map/ppermute | solution.py:352
  16.6 1.5 %collective-permute-start.4 = (bf16[256,256]{1,0:T(8,128)(2,1)S(1)}, bf16[256,256]{1,0:T(8,128)(2,1)S(1)}, u32[]{:S(2)}, u32[]{:S(2)}) collective-permute-start(bf16[256,256]{1,0:T(8,128)(2,1)S(1)} %get-tuple-element.38.refs_2_.refs_4_), channel_id=1, source_target_pairs={{0,2},{1,3},{2,0},{3,1},{4,6},{5,7},{6,4},{7,5},{8,10},{9,11},{10,... | collective-permute-start | bytes 393224 | tf_op jit(solution)/shard_map/ppermute | solution.py:352
  18.0 0.5 collective-permute-start.7
  18.6 1.5 %stats_own.1.after_ref.refs_0_.refs_2_ = f32[10,8,256]{2,1,0:T(8,128)S(1)} custom-call(bf16[512,640]{1,0:T(8,128)(2,1)S(1)} %bitcast.7, bf16[512,640]{1,0:T(8,128)(2,1)S(1)} %get-tuple-element.37.refs_4_.refs_1_.refs_2_, bf16[256,256]{1,0:T(8,128)(2,1)S(1)} %get-tuple-element.38.refs_2_.refs_4_, bf16[512,256]{1,0:T(8,128)(2,1)S(1)} %bitcast.19, ...), custom_call_target="tpu_custom_call" | custom-call | tf_op jit(solution)/shard_map/stats_own/pallas_call | solution.py:34
  20.1 2.1 %collective-permute-done.3.x_ref = bf16[256,256]{1,0:T(8,128)(2,1)S(1)} collective-permute-done((bf16[256,256]{1,0:T(8,128)(2,1)S(1)}, bf16[256,256]{1,0:T(8,128)(2,1)S(1)}, u32[]{:S(2)}, u32[]{:S(2)}) %collective-permute-start.3) | collective-permute-done | bytes 131104 | tf_op jit(solution)/shard_map/ppermute | solution.py:352
  22.2 0.1 collective-permute-start.6
  22.3 0.6 collective-permute-start.8
  22.9 0.1 collective-permute-done.4.x_ref
  23.0 1.5 %collective-permute-start.9 = (bf16[256,256]{1,0:T(8,128)(2,1)S(1)}, bf16[256,256]{1,0:T(8,128)(2,1)S(1)}, u32[]{:S(2)}, u32[]{:S(2)}) collective-permute-start(bf16[256,256]{1,0:T(8,128)(2,1)S(1)} %pass_on.4.refs_4_), channel_id=1, source_target_pairs={{0,1},{1,0},{2,3},{3,2},{4,5},{5,4},{6,7},{7,6},{8,9},{9,8},{10,11... | collective-permute-start | bytes 393224 | tf_op jit(solution)/shard_map/ppermute | solution.py:352
  24.5 0.7 pairs_route.1
  25.2 2.0 %collective-permute-start.10 = (bf16[4,32,256]{2,1,0:T(8,128)(2,1)S(1)}, bf16[4,32,256]{2,1,0:T(8,128)(2,1)S(1)}, u32[]{:S(2)}, u32[]{:S(2)}) collective-permute-start(bf16[4,32,256]{2,1,0:T(8,128)(2,1)S(1)} %get-tuple-element.44), channel_id=1, source_target_pairs={{0,2},{1,3},{2,0},{3,1},{4,6},{5,7},{6,4},{7,5},{8,10},{9,11},{10,... | collective-permute-start | bytes 196616 | tf_op jit(solution)/shard_map/ppermute | solution.py:352
  27.2 1.4 %collective-permute-start.11 = (bf16[4,32,256]{2,1,0:T(8,128)(2,1)S(1)}, bf16[4,32,256]{2,1,0:T(8,128)(2,1)S(1)}, u32[]{:S(2)}, u32[]{:S(2)}) collective-permute-start(bf16[4,32,256]{2,1,0:T(8,128)(2,1)S(1)} %get-tuple-element.45), channel_id=1, source_target_pairs={{0,4},{1,5},{2,6},{3,7},{4,0},{5,1},{6,2},{7,3},{8,12},{9,13},{10,... | collective-permute-start | bytes 196616 | tf_op jit(solution)/shard_map/ppermute | solution.py:352
  28.6 0.0 collective-permute-done.6.refs_3_.x_ref.refs_5_
  28.6 1.4 %collective-permute-start.12 = (bf16[4,32,256]{2,1,0:T(8,128)(2,1)S(1)}, bf16[4,32,256]{2,1,0:T(8,128)(2,1)S(1)}, u32[]{:S(2)}, u32[]{:S(2)}) collective-permute-start(bf16[4,32,256]{2,1,0:T(8,128)(2,1)S(1)} %get-tuple-element.46), channel_id=1, source_target_pairs={{0,6},{1,7},{2,4},{3,5},{4,2},{5,3},{6,0},{7,1},{8,14},{9,15},{10,... | collective-permute-start | bytes 196616 | tf_op jit(solution)/shard_map/ppermute | solution.py:352
  30.1 1.8 %stats_prompt.2.refs_2_.after_ref = f32[10,8,256]{2,1,0:T(8,128)S(1)} custom-call(bf16[512,640]{1,0:T(8,128)(2,1)S(1)} %bitcast.8, bf16[512,640]{1,0:T(8,128)(2,1)S(1)} %get-tuple-element.37.refs_4_.refs_1_.refs_2_, f32[10,8,256]{2,1,0:T(8,128)S(1)} %stats_own.1.after_ref.refs_0_.refs_2_, bf16[256,256]{1,0:T(8,128)(2,1)S(1)} %pass_on.3.refs_3_.refs_5_, ...), custom_call_target="tpu_custom_call" | custom-call | tf_op jit(solution)/shard_map/stats_prompt/pallas_call | solution.py:34
  31.9 0.0 copy-start.6
  31.9 1.8 %stats_prompt.3.refs_3_ = f32[10,8,256]{2,1,0:T(8,128)S(1)} custom-call(bf16[512,640]{1,0:T(8,128)(2,1)S(1)} %bitcast.9, bf16[512,640]{1,0:T(8,128)(2,1)S(1)} %get-tuple-element.37.refs_4_.refs_1_.refs_2_, f32[10,8,256]{2,1,0:T(8,128)S(1)} %stats_prompt.2.refs_2_.after_ref, bf16[256,256]{1,0:T(8,128)(2,1)S(1)} %collective-permute-done.6.refs_3_.x_ref.refs_5_, ...), custom_call_target="tpu_custom_call" | custom-call | tf_op jit(solution)/shard_map/stats_prompt/pallas_call | solution.py:34
  33.7 0.6 collective-permute-start.13
  34.3 0.4 collective-permute-done.12.refs_9_
  34.8 2.9 %stats_partner.1 = (f32[10,8,256]{2,1,0:T(8,128)S(1)}, bf16[512,256]{1,0:T(8,128)(2,1)S(1)}) custom-call(s32[1,32]{1,0:T(1,128)S(1)} %copy-done.6, bf16[512,640]{1,0:T(8,128)(2,1)S(1)} %bitcast.10, bf16[512,640]{1,0:T(8,128)(2,1)S(1)} %get-tuple-element.37.refs_4_.refs_1_.refs_2_, f32[10,8,256]{2,1,0:T(8,128)S(1)} %stats_prompt.3.refs_3_, ...), custom_call_target="tpu_custom_call" | custom-call | flops 7000000000 | tf_op jit(solution)/shard_map/stats_partner/pallas_call | solution.py:34
  37.7 1.1 %collective-permute-done.13.refs_3_.refs_5_ = bf16[256,256]{1,0:T(8,128)(2,1)S(1)} collective-permute-done((bf16[256,256]{1,0:T(8,128)(2,1)S(1)}, bf16[256,256]{1,0:T(8,128)(2,1)S(1)}, u32[]{:S(2)}, u32[]{:S(2)}) %collective-permute-start.13) | collective-permute-done | bytes 131104 | tf_op jit(solution)/shard_map/ppermute | solution.py:352
  38.8 1.0 %stats_last.1.refs_3_.refs_2_ = f32[10,8,256]{2,1,0:T(8,128)S(1)} custom-call(bf16[512,640]{1,0:T(8,128)(2,1)S(1)} %bitcast.11, bf16[512,640]{1,0:T(8,128)(2,1)S(1)} %get-tuple-element.37.refs_4_.refs_1_.refs_2_, f32[10,8,256]{2,1,0:T(8,128)S(1)} %get-tuple-element.47.refs_2_, bf16[256,256]{1,0:T(8,128)(2,1)S(1)} %collective-permute-done.13.refs_3_.refs_5_), custom_call_target="tpu_custom_call" | custom-call | tf_op jit(solution)/shard_map/stats_last/pallas_call | solution.py:34
  39.8 2.0 %grads_partner.1 = (f32[640,512]{1,0:T(8,128)S(1)}, bf16[4,32,256]{2,1,0:T(8,128)(2,1)S(1)}, bf16[4,32,256]{2,1,0:T(8,128)(2,1)S(1)}, bf16[4,32,256]{2,1,0:T(8,128)(2,1)S(1)}, bf16[4,32,256]{2,1,0:T(8,128)(2,1)S(1)}) custom-call(s32[1,32]{1,0:T(1,128)S(1)} %copy-done.6, bf16[512,640]{1,0:T(8,128)(2,1)S(1)} %bitcast.12, ...), custom_call_target="tpu_custom_call" | custom-call | tf_op jit(solution)/shard_map/grads_partner/pallas_call | solution.py:34
  41.8 0.7 collective-permute-start.14
  42.5 2.3 %collective-permute-start.15 = (bf16[4,32,256]{2,1,0:T(8,128)(2,1)S(1)}, bf16[4,32,256]{2,1,0:T(8,128)(2,1)S(1)}, u32[]{:S(2)}, u32[]{:S(2)}) collective-permute-start(bf16[4,32,256]{2,1,0:T(8,128)(2,1)S(1)} %get-tuple-element.53), channel_id=1, source_target_pairs={{0,4},{1,5},{2,6},{3,7},{4,0},{5,1},{6,2},{7,3},{8,12},{9,13},{10,... | collective-permute-start | bytes 196616 | tf_op jit(solution)/shard_map/ppermute | solution.py:352
  44.8 1.4 %collective-permute-start.16 = (bf16[4,32,256]{2,1,0:T(8,128)(2,1)S(1)}, bf16[4,32,256]{2,1,0:T(8,128)(2,1)S(1)}, u32[]{:S(2)}, u32[]{:S(2)}) collective-permute-start(bf16[4,32,256]{2,1,0:T(8,128)(2,1)S(1)} %get-tuple-element.54), channel_id=1, source_target_pairs={{0,6},{1,7},{2,4},{3,5},{4,2},{5,3},{6,0},{7,1},{8,14},{9,15},{10,... | collective-permute-start | bytes 196616 | tf_op jit(solution)/shard_map/ppermute | solution.py:352
  46.2 3.5 %grads_across.2 = (f32[640,512]{1,0:T(8,128)S(1)}, bf16[512,256]{1,0:T(8,128)(2,1)S(1)}) custom-call(bf16[512,640]{1,0:T(8,128)(2,1)S(1)} %bitcast.13, bf16[512,640]{1,0:T(8,128)(2,1)S(1)} %get-tuple-element.37.refs_4_.refs_1_.refs_2_, f32[10,8,256]{2,1,0:T(8,128)S(1)} %stats_last.1.refs_3_.refs_2_, f32[640,512]{1,0:T(8,128)S(1)} %get-tuple-element.49.refs_3_, ...), custom_call_target="tpu_custom_call" | custom-call | tf_op jit(solution)/shard_map/grads_across/pallas_call | solution.py:34
  49.7 0.6 collective-permute-start.17
  50.3 0.5 collective-permute-done.16.refs_3_
  50.9 1.0 %collective-permute-start.20 = (bf16[4,4,32,256]{3,2,1,0:T(8,128)(2,1)S(1)}, bf16[4,4,32,256]{3,2,1,0:T(8,128)(2,1)S(1)}, u32[]{:S(2)}, u32[]{:S(2)}) collective-permute-start(bf16[4,4,32,256]{3,2,1,0:T(8,128)(2,1)S(1)} %terms_stack.1.refs_6_.mine_ref), channel_id=1, source_target_pairs={{0,1},{1,0},{2,3},{3,2},{4,5},{5,4},{6,7},{7,6},{8,9},{9,8},{10,11... | collective-permute-start | bytes 786440 | tf_op jit(solution)/shard_map/ppermute | solution.py:352
  51.9 3.3 %grads_near.1 = (f32[640,512]{1,0:T(8,128)S(1)}, f32[512,256]{1,0:T(8,128)S(1)}) custom-call(bf16[512,640]{1,0:T(8,128)(2,1)S(1)} %bitcast.14, bf16[512,640]{1,0:T(8,128)(2,1)S(1)} %get-tuple-element.37.refs_4_.refs_1_.refs_2_, f32[10,8,256]{2,1,0:T(8,128)S(1)} %stats_last.1.refs_3_.refs_2_, f32[640,512]{1,0:T(8,128)S(1)} %get-tuple-element.50.refs_3_, ...), custom_call_target="tpu_custom_call" | custom-call | flops 7000000000 | tf_op jit(solution)/shard_map/grads_near/pallas_call | solution.py:34
  55.2 3.3 %grads_across.3 = (f32[640,512]{1,0:T(8,128)S(1)}, bf16[512,256]{1,0:T(8,128)(2,1)S(1)}) custom-call(bf16[512,640]{1,0:T(8,128)(2,1)S(1)} %bitcast.15, bf16[512,640]{1,0:T(8,128)(2,1)S(1)} %get-tuple-element.37.refs_4_.refs_1_.refs_2_, f32[10,8,256]{2,1,0:T(8,128)S(1)} %stats_last.1.refs_3_.refs_2_, f32[640,512]{1,0:T(8,128)S(1)} %get-tuple-element.57.refs_3_, ...), custom_call_target="tpu_custom_call" | custom-call | tf_op jit(solution)/shard_map/grads_across/pallas_call | solution.py:34
  58.5 0.1 collective-permute-start.22
  58.6 1.1 %collective-permute-start.21 = (bf16[512,256]{1,0:T(8,128)(2,1)S(1)}, bf16[512,256]{1,0:T(8,128)(2,1)S(1)}, u32[]{:S(2)}, u32[]{:S(2)}) collective-permute-start(bf16[512,256]{1,0:T(8,128)(2,1)S(1)} %get-tuple-element.58.refs_2_), channel_id=1, source_target_pairs={{0,1},{1,0},{2,3},{3,2},{4,5},{5,4},{6,7},{7,6},{8,9},{9,8},{10,11... | collective-permute-start | bytes 786440 | tf_op jit(solution)/shard_map/ppermute | solution.py:352
  59.7 3.3 %grads_rest.1 = (f32[640,512]{1,0:T(8,128)S(1)}, f32[512,256]{1,0:T(8,128)S(1)}) custom-call(bf16[512,640]{1,0:T(8,128)(2,1)S(1)} %bitcast.16, bf16[512,640]{1,0:T(8,128)(2,1)S(1)} %get-tuple-element.37.refs_4_.refs_1_.refs_2_, f32[10,8,256]{2,1,0:T(8,128)S(1)} %stats_last.1.refs_3_.refs_2_, f32[640,512]{1,0:T(8,128)S(1)} %get-tuple-element.59.refs_3_, ...), custom_call_target="tpu_custom_call" | custom-call | tf_op jit(solution)/shard_map/grads_rest/pallas_call | solution.py:34
  63.0 0.0 collective-permute-done.20.other_ref
  63.0 0.7 terms_route.1
  63.7 1.5 %grads_own.1 = (f32[640,512]{1,0:T(8,128)S(1)}, f32[512,256]{1,0:T(8,128)S(1)}) custom-call(bf16[512,640]{1,0:T(8,128)(2,1)S(1)} %bitcast.17, bf16[512,640]{1,0:T(8,128)(2,1)S(1)} %get-tuple-element.37.refs_4_.refs_1_.refs_2_, f32[10,8,256]{2,1,0:T(8,128)S(1)} %stats_last.1.refs_3_.refs_2_, f32[640,512]{1,0:T(8,128)S(1)} %get-tuple-element.61.refs_3_, ...), custom_call_target="tpu_custom_call" | custom-call | tf_op jit(solution)/shard_map/grads_own/pallas_call | solution.py:34
  65.3 0.0 copy-start.8
  65.3 0.1 sum_far.1.after_ref
  65.3 2.7 %collective-permute-start.23 = (bf16[384,256]{1,0:T(8,128)(2,1)S(1)}, bf16[384,256]{1,0:T(8,128)(2,1)S(1)}, u32[]{:S(2)}, u32[]{:S(2)}) collective-permute-start(bf16[384,256]{1,0:T(8,128)(2,1)S(1)} %sum_far.1.after_ref), channel_id=1, source_target_pairs={{0,4},{1,5},{2,6},{3,7},{4,0},{5,1},{6,2},{7,3},{8,12},{9,13},{10,... | collective-permute-start | bytes 589832 | tf_op jit(solution)/shard_map/ppermute | solution.py:352
  68.0 1.1 %collective-permute-start.24 = (bf16[4,32,256]{2,1,0:T(8,128)(2,1)S(1)}, bf16[4,32,256]{2,1,0:T(8,128)(2,1)S(1)}, u32[]{:S(2)}, u32[]{:S(2)}) collective-permute-start(bf16[4,32,256]{2,1,0:T(8,128)(2,1)S(1)} %get-tuple-element.66), channel_id=1, source_target_pairs={{0,2},{1,3},{2,0},{3,1},{4,6},{5,7},{6,4},{7,5},{8,10},{9,11},{10,... | collective-permute-start | bytes 196616 | tf_op jit(solution)/shard_map/ppermute | solution.py:352
  69.2 0.6 collective-permute-start.25
  69.8 0.0 collective-permute-start.18
  69.8 1.1 %collective-permute-done.18.y_ref = s32[1,16]{1,0:T(1,128)S(1)} collective-permute-done((s32[1,16]{1,0:T(1,128)S(1)}, s32[1,16]{1,0:T(1,128)S(1)}, u32[]{:S(2)}, u32[]{:S(2)}) %collective-permute-start.18) | collective-permute-done | bytes 96 | tf_op jit(solution)/shard_map/ppermute | solution.py:352
  70.9 1.5 %collective-permute-start.19 = (s32[1,16]{1,0:T(1,128)S(1)}, s32[1,16]{1,0:T(1,128)S(1)}, u32[]{:S(2)}, u32[]{:S(2)}) collective-permute-start(s32[1,16]{1,0:T(1,128)S(1)} %add_lengths.2.x_ref), channel_id=1, source_target_pairs={{0,16},{8,24},{16,0},{24,8},{1,17},{9,25},{17,1},{25,9},{2,18},{10... | collective-permute-start | bytes 200 | tf_op jit(solution)/shard_map/ppermute | solution.py:352
  72.5 0.4 turn_queries.1.after_ref.refs_0_
  72.9 1.6 %collective-permute-done.19.y_ref = s32[1,16]{1,0:T(1,128)S(1)} collective-permute-done((s32[1,16]{1,0:T(1,128)S(1)}, s32[1,16]{1,0:T(1,128)S(1)}, u32[]{:S(2)}, u32[]{:S(2)}) %collective-permute-start.19) | collective-permute-done | bytes 96 | tf_op jit(solution)/shard_map/ppermute | solution.py:352
  74.5 0.0 collective-permute-done.23.refs_1_.refs_5_
  74.5 0.8 %collective-permute-done.25.refs_6_ = bf16[4,32,256]{2,1,0:T(8,128)(2,1)S(1)} collective-permute-done((bf16[4,32,256]{2,1,0:T(8,128)(2,1)S(1)}, bf16[4,32,256]{2,1,0:T(8,128)(2,1)S(1)}, u32[]{:S(2)}, u32[]{:S(2)}) %collective-permute-start.25) | collective-permute-done | bytes 65568 | tf_op jit(solution)/shard_map/ppermute | solution.py:352
  75.3 1.7 %over_count.1 = (bf16[512,640]{1,0:T(8,128)(2,1)}, bf16[512,256]{1,0:T(8,128)(2,1)}, bf16[256,256]{1,0:T(8,128)(2,1)}) custom-call(s32[1,32]{1,0:T(1,128)S(1)} %copy-done.6, s32[1,16]{1,0:T(1,128)S(1)} %add_lengths.3.lengths_ref, f32[512,640]{1,0:T(8,128)S(1)} %turn_queries.1.after_ref.refs_0_, f32[512,256]{1,0:T(8,128)S(1)} %get-tuple-element.64.after_ref.refs_2_.refs_1_, ...), custom_call_target="tpu_custom_call" | custom-call | tf_op jit(solution)/shard_map/over_count/pallas_call | solution.py:34
  (38 shorter events, 0.3 us)
Async XLA Ops:
  0.6 18.0 %copy-start = (bf16[1,512,640]{2,1,0:T(8,128)(2,1)S(1)}, bf16[1,512,640]{2,1,0:T(8,128)(2,1)}, u32[]{:S(2)}) copy-start(bf16[1,512,640]{2,1,0:T(8,128)(2,1)} %param.7) | copy-start | bytes 1966084
  0.6 1.0 %copy-start.1 = (bf16[1,512,256]{2,1,0:T(8,128)(2,1)S(1)}, bf16[1,512,256]{2,1,0:T(8,128)(2,1)}, u32[]{:S(2)}) copy-start(bf16[1,512,256]{2,1,0:T(8,128)(2,1)} %param.8) | copy-start | bytes 786436
  1.7 16.9 %copy-start.2 = (bf16[1,512,256]{2,1,0:T(8,128)(2,1)S(1)}, bf16[1,512,256]{2,1,0:T(8,128)(2,1)}, u32[]{:S(2)}) copy-start(bf16[1,512,256]{2,1,0:T(8,128)(2,1)} %param.8) | copy-start | bytes 786436
  1.7 10.4 %collective-permute-start = (bf16[4,32,256]{2,1,0:T(8,128)(2,1)S(1)}, bf16[4,32,256]{2,1,0:T(8,128)(2,1)S(1)}, u32[]{:S(2)}, u32[]{:S(2)}) collective-permute-start(bf16[4,32,256]{2,1,0:T(8,128)(2,1)S(1)} %get-tuple-element.40), channel_id=1, source_target_pairs={{0,2},{1,3},{2,0},{3,1},{4,6},{5,7},{6,4},{7,5},{8,10},{9,11},{10,... | collective-permute-start | bytes 196616 | tf_op jit(solution)/shard_map/ppermute | solution.py:352
  4.8 7.3 %collective-permute-start.1 = (bf16[4,32,256]{2,1,0:T(8,128)(2,1)S(1)}, bf16[4,32,256]{2,1,0:T(8,128)(2,1)S(1)}, u32[]{:S(2)}, u32[]{:S(2)}) collective-permute-start(bf16[4,32,256]{2,1,0:T(8,128)(2,1)S(1)} %get-tuple-element.41), channel_id=1, source_target_pairs={{0,4},{1,5},{2,6},{3,7},{4,0},{5,1},{6,2},{7,3},{8,12},{9,13},{10,... | collective-permute-start | bytes 196616 | tf_op jit(solution)/shard_map/ppermute | solution.py:352
  7.4 6.1 %collective-permute-start.2 = (bf16[4,32,256]{2,1,0:T(8,128)(2,1)S(1)}, bf16[4,32,256]{2,1,0:T(8,128)(2,1)S(1)}, u32[]{:S(2)}, u32[]{:S(2)}) collective-permute-start(bf16[4,32,256]{2,1,0:T(8,128)(2,1)S(1)} %get-tuple-element.42), channel_id=1, source_target_pairs={{0,6},{1,7},{2,4},{3,5},{4,2},{5,3},{6,0},{7,1},{8,14},{9,15},{10,... | collective-permute-start | bytes 196616 | tf_op jit(solution)/shard_map/ppermute | solution.py:352
  7.4 1.1 %copy-start.3 = (bf16[1,512,640]{2,1,0:T(8,128)(2,1)S(1)}, bf16[1,512,640]{2,1,0:T(8,128)(2,1)}, u32[]{:S(2)}) copy-start(bf16[1,512,640]{2,1,0:T(8,128)(2,1)} %param.10) | copy-start | bytes 1966084
  8.5 0.9 %copy-start.4 = (bf16[1,256,256]{2,1,0:T(8,128)(2,1)S(1)}, bf16[1,256,256]{2,1,0:T(8,128)(2,1)}, u32[]{:S(2)}) copy-start(bf16[1,256,256]{2,1,0:T(8,128)(2,1)} %param.9) | copy-start | bytes 393220
  9.4 0.7 copy-start.5
  10.0 0.7 copy-start.7
  10.7 0.7 copy-start.9
  13.5 11.0 %collective-permute-start.5 = (bf16[4,4,32,256]{3,2,1,0:T(8,128)(2,1)S(1)}, bf16[4,4,32,256]{3,2,1,0:T(8,128)(2,1)S(1)}, u32[]{:S(2)}, u32[]{:S(2)}) collective-permute-start(bf16[4,4,32,256]{3,2,1,0:T(8,128)(2,1)S(1)} %pairs_stack.1.refs_4_.mine_ref), channel_id=1, source_target_pairs={{0,1},{1,0},{2,3},{3,2},{4,5},{5,4},{6,7},{7,6},{8,9},{9,8},{10,11... | collective-permute-start | bytes 786440 | tf_op jit(solution)/shard_map/ppermute | solution.py:352
  15.0 7.2 %collective-permute-start.3 = (bf16[256,256]{1,0:T(8,128)(2,1)S(1)}, bf16[256,256]{1,0:T(8,128)(2,1)S(1)}, u32[]{:S(2)}, u32[]{:S(2)}) collective-permute-start(bf16[256,256]{1,0:T(8,128)(2,1)S(1)} %get-tuple-element.38.refs_2_.refs_4_), channel_id=1, source_target_pairs={{0,4},{1,5},{2,6},{3,7},{4,0},{5,1},{6,2},{7,3},{8,12},{9,13},{10,... | collective-permute-start | bytes 393224 | tf_op jit(solution)/shard_map/ppermute | solution.py:352
  16.6 6.4 %collective-permute-start.4 = (bf16[256,256]{1,0:T(8,128)(2,1)S(1)}, bf16[256,256]{1,0:T(8,128)(2,1)S(1)}, u32[]{:S(2)}, u32[]{:S(2)}) collective-permute-start(bf16[256,256]{1,0:T(8,128)(2,1)S(1)} %get-tuple-element.38.refs_2_.refs_4_), channel_id=1, source_target_pairs={{0,2},{1,3},{2,0},{3,1},{4,6},{5,7},{6,4},{7,5},{8,10},{9,11},{10,... | collective-permute-start | bytes 393224 | tf_op jit(solution)/shard_map/ppermute | solution.py:352
  18.0 9.2 %collective-permute-start.7 = (bf16[256,256]{1,0:T(8,128)(2,1)S(1)}, bf16[256,256]{1,0:T(8,128)(2,1)S(1)}, u32[]{:S(2)}, u32[]{:S(2)}) collective-permute-start(bf16[256,256]{1,0:T(8,128)(2,1)S(1)} %get-tuple-element.38.refs_2_.refs_4_), channel_id=1, source_target_pairs={{0,1},{1,0},{2,3},{3,2},{4,5},{5,4},{6,7},{7,6},{8,9},{9,8},{10,11... | collective-permute-start | bytes 393224 | tf_op jit(solution)/shard_map/ppermute | solution.py:352
  22.2 6.4 %collective-permute-start.6 = (bf16[256,256]{1,0:T(8,128)(2,1)S(1)}, bf16[256,256]{1,0:T(8,128)(2,1)S(1)}, u32[]{:S(2)}, u32[]{:S(2)}) collective-permute-start(bf16[256,256]{1,0:T(8,128)(2,1)S(1)} %pass_on.3.refs_3_.refs_5_), channel_id=1, source_target_pairs={{0,2},{1,3},{2,0},{3,1},{4,6},{5,7},{6,4},{7,5},{8,10},{9,11},{10,... | collective-permute-start | bytes 393224 | tf_op jit(solution)/shard_map/ppermute | solution.py:352
  22.3 11.4 %collective-permute-start.8 = (bf16[256,256]{1,0:T(8,128)(2,1)S(1)}, bf16[256,256]{1,0:T(8,128)(2,1)S(1)}, u32[]{:S(2)}, u32[]{:S(2)}) collective-permute-start(bf16[256,256]{1,0:T(8,128)(2,1)S(1)} %pass_on.3.refs_3_.refs_5_), channel_id=1, source_target_pairs={{0,1},{1,0},{2,3},{3,2},{4,5},{5,4},{6,7},{7,6},{8,9},{9,8},{10,11... | collective-permute-start | bytes 393224 | tf_op jit(solution)/shard_map/ppermute | solution.py:352
  23.0 11.3 %collective-permute-start.9 = (bf16[256,256]{1,0:T(8,128)(2,1)S(1)}, bf16[256,256]{1,0:T(8,128)(2,1)S(1)}, u32[]{:S(2)}, u32[]{:S(2)}) collective-permute-start(bf16[256,256]{1,0:T(8,128)(2,1)S(1)} %pass_on.4.refs_4_), channel_id=1, source_target_pairs={{0,1},{1,0},{2,3},{3,2},{4,5},{5,4},{6,7},{7,6},{8,9},{9,8},{10,11... | collective-permute-start | bytes 393224 | tf_op jit(solution)/shard_map/ppermute | solution.py:352
  25.2 9.1 %collective-permute-start.10 = (bf16[4,32,256]{2,1,0:T(8,128)(2,1)S(1)}, bf16[4,32,256]{2,1,0:T(8,128)(2,1)S(1)}, u32[]{:S(2)}, u32[]{:S(2)}) collective-permute-start(bf16[4,32,256]{2,1,0:T(8,128)(2,1)S(1)} %get-tuple-element.44), channel_id=1, source_target_pairs={{0,2},{1,3},{2,0},{3,1},{4,6},{5,7},{6,4},{7,5},{8,10},{9,11},{10,... | collective-permute-start | bytes 196616 | tf_op jit(solution)/shard_map/ppermute | solution.py:352
  27.2 7.1 %collective-permute-start.11 = (bf16[4,32,256]{2,1,0:T(8,128)(2,1)S(1)}, bf16[4,32,256]{2,1,0:T(8,128)(2,1)S(1)}, u32[]{:S(2)}, u32[]{:S(2)}) collective-permute-start(bf16[4,32,256]{2,1,0:T(8,128)(2,1)S(1)} %get-tuple-element.45), channel_id=1, source_target_pairs={{0,4},{1,5},{2,6},{3,7},{4,0},{5,1},{6,2},{7,3},{8,12},{9,13},{10,... | collective-permute-start | bytes 196616 | tf_op jit(solution)/shard_map/ppermute | solution.py:352
  28.6 6.2 %collective-permute-start.12 = (bf16[4,32,256]{2,1,0:T(8,128)(2,1)S(1)}, bf16[4,32,256]{2,1,0:T(8,128)(2,1)S(1)}, u32[]{:S(2)}, u32[]{:S(2)}) collective-permute-start(bf16[4,32,256]{2,1,0:T(8,128)(2,1)S(1)} %get-tuple-element.46), channel_id=1, source_target_pairs={{0,6},{1,7},{2,4},{3,5},{4,2},{5,3},{6,0},{7,1},{8,14},{9,15},{10,... | collective-permute-start | bytes 196616 | tf_op jit(solution)/shard_map/ppermute | solution.py:352
  31.9 2.9 %copy-start.6 = (s32[1,32]{1,0:T(1,128)S(1)}, s32[1,32]{1,0:T(1,128)}, u32[]{:S(2)}) copy-start(s32[1,32]{1,0:T(1,128)} %plan_ref.7) | copy-start | bytes 388
  33.7 5.0 %collective-permute-start.13 = (bf16[256,256]{1,0:T(8,128)(2,1)S(1)}, bf16[256,256]{1,0:T(8,128)(2,1)S(1)}, u32[]{:S(2)}, u32[]{:S(2)}) collective-permute-start(bf16[256,256]{1,0:T(8,128)(2,1)S(1)} %pass_on.5), channel_id=1, source_target_pairs={{0,1},{1,0},{2,3},{3,2},{4,5},{5,4},{6,7},{7,6},{8,9},{9,8},{10,11... | collective-permute-start | bytes 393224 | tf_op jit(solution)/shard_map/ppermute | solution.py:352
  41.8 8.5 %collective-permute-start.14 = (bf16[4,32,256]{2,1,0:T(8,128)(2,1)S(1)}, bf16[4,32,256]{2,1,0:T(8,128)(2,1)S(1)}, u32[]{:S(2)}, u32[]{:S(2)}) collective-permute-start(bf16[4,32,256]{2,1,0:T(8,128)(2,1)S(1)} %get-tuple-element.52), channel_id=1, source_target_pairs={{0,2},{1,3},{2,0},{3,1},{4,6},{5,7},{6,4},{7,5},{8,10},{9,11},{10,... | collective-permute-start | bytes 196616 | tf_op jit(solution)/shard_map/ppermute | solution.py:352
  42.5 7.8 %collective-permute-start.15 = (bf16[4,32,256]{2,1,0:T(8,128)(2,1)S(1)}, bf16[4,32,256]{2,1,0:T(8,128)(2,1)S(1)}, u32[]{:S(2)}, u32[]{:S(2)}) collective-permute-start(bf16[4,32,256]{2,1,0:T(8,128)(2,1)S(1)} %get-tuple-element.53), channel_id=1, source_target_pairs={{0,4},{1,5},{2,6},{3,7},{4,0},{5,1},{6,2},{7,3},{8,12},{9,13},{10,... | collective-permute-start | bytes 196616 | tf_op jit(solution)/shard_map/ppermute | solution.py:352
  44.8 6.1 %collective-permute-start.16 = (bf16[4,32,256]{2,1,0:T(8,128)(2,1)S(1)}, bf16[4,32,256]{2,1,0:T(8,128)(2,1)S(1)}, u32[]{:S(2)}, u32[]{:S(2)}) collective-permute-start(bf16[4,32,256]{2,1,0:T(8,128)(2,1)S(1)} %get-tuple-element.54), channel_id=1, source_target_pairs={{0,6},{1,7},{2,4},{3,5},{4,2},{5,3},{6,0},{7,1},{8,14},{9,15},{10,... | collective-permute-start | bytes 196616 | tf_op jit(solution)/shard_map/ppermute | solution.py:352
  49.7 8.7 %collective-permute-start.17 = (bf16[512,256]{1,0:T(8,128)(2,1)S(1)}, bf16[512,256]{1,0:T(8,128)(2,1)S(1)}, u32[]{:S(2)}, u32[]{:S(2)}) collective-permute-start(bf16[512,256]{1,0:T(8,128)(2,1)S(1)} %get-tuple-element.55.refs_4_), channel_id=1, source_target_pairs={{0,1},{1,0},{2,3},{3,2},{4,5},{5,4},{6,7},{7,6},{8,9},{9,8},{10,11... | collective-permute-start | bytes 786440 | tf_op jit(solution)/shard_map/ppermute | solution.py:352
  50.9 12.1 %collective-permute-start.20 = (bf16[4,4,32,256]{3,2,1,0:T(8,128)(2,1)S(1)}, bf16[4,4,32,256]{3,2,1,0:T(8,128)(2,1)S(1)}, u32[]{:S(2)}, u32[]{:S(2)}) collective-permute-start(bf16[4,4,32,256]{3,2,1,0:T(8,128)(2,1)S(1)} %terms_stack.1.refs_6_.mine_ref), channel_id=1, source_target_pairs={{0,1},{1,0},{2,3},{3,2},{4,5},{5,4},{6,7},{7,6},{8,9},{9,8},{10,11... | collective-permute-start | bytes 786440 | tf_op jit(solution)/shard_map/ppermute | solution.py:352
  58.5 6.7 %collective-permute-start.22 = (bf16[512,256]{1,0:T(8,128)(2,1)S(1)}, bf16[512,256]{1,0:T(8,128)(2,1)S(1)}, u32[]{:S(2)}, u32[]{:S(2)}) collective-permute-start(bf16[512,256]{1,0:T(8,128)(2,1)S(1)} %sum_near.1.after_ref.refs_6_), channel_id=1, source_target_pairs={{0,2},{1,3},{2,0},{3,1},{4,6},{5,7},{6,4},{7,5},{8,10},{9,11},{10,... | collective-permute-start | bytes 786440 | tf_op jit(solution)/shard_map/ppermute | solution.py:352
  58.6 6.7 %collective-permute-start.21 = (bf16[512,256]{1,0:T(8,128)(2,1)S(1)}, bf16[512,256]{1,0:T(8,128)(2,1)S(1)}, u32[]{:S(2)}, u32[]{:S(2)}) collective-permute-start(bf16[512,256]{1,0:T(8,128)(2,1)S(1)} %get-tuple-element.58.refs_2_), channel_id=1, source_target_pairs={{0,1},{1,0},{2,3},{3,2},{4,5},{5,4},{6,7},{7,6},{8,9},{9,8},{10,11... | collective-permute-start | bytes 786440 | tf_op jit(solution)/shard_map/ppermute | solution.py:352
  65.3 4.5 %copy-start.8 = (s32[1,16]{1,0:T(1,128)S(1)}, s32[1,16]{1,0:T(1,128)}, u32[]{:S(2)}) copy-start(s32[1,16]{1,0:T(1,128)} %x_ref.1) | copy-start | bytes 196
  65.3 9.1 %collective-permute-start.23 = (bf16[384,256]{1,0:T(8,128)(2,1)S(1)}, bf16[384,256]{1,0:T(8,128)(2,1)S(1)}, u32[]{:S(2)}, u32[]{:S(2)}) collective-permute-start(bf16[384,256]{1,0:T(8,128)(2,1)S(1)} %sum_far.1.after_ref), channel_id=1, source_target_pairs={{0,4},{1,5},{2,6},{3,7},{4,0},{5,1},{6,2},{7,3},{8,12},{9,13},{10,... | collective-permute-start | bytes 589832 | tf_op jit(solution)/shard_map/ppermute | solution.py:352
  68.0 6.5 %collective-permute-start.24 = (bf16[4,32,256]{2,1,0:T(8,128)(2,1)S(1)}, bf16[4,32,256]{2,1,0:T(8,128)(2,1)S(1)}, u32[]{:S(2)}, u32[]{:S(2)}) collective-permute-start(bf16[4,32,256]{2,1,0:T(8,128)(2,1)S(1)} %get-tuple-element.66), channel_id=1, source_target_pairs={{0,2},{1,3},{2,0},{3,1},{4,6},{5,7},{6,4},{7,5},{8,10},{9,11},{10,... | collective-permute-start | bytes 196616 | tf_op jit(solution)/shard_map/ppermute | solution.py:352
  69.2 6.2 %collective-permute-start.25 = (bf16[4,32,256]{2,1,0:T(8,128)(2,1)S(1)}, bf16[4,32,256]{2,1,0:T(8,128)(2,1)S(1)}, u32[]{:S(2)}, u32[]{:S(2)}) collective-permute-start(bf16[4,32,256]{2,1,0:T(8,128)(2,1)S(1)} %get-tuple-element.67), channel_id=1, source_target_pairs={{0,6},{1,7},{2,4},{3,5},{4,2},{5,3},{6,0},{7,1},{8,14},{9,15},{10,... | collective-permute-start | bytes 196616 | tf_op jit(solution)/shard_map/ppermute | solution.py:352
  69.8 1.1 %collective-permute-start.18 = (s32[1,16]{1,0:T(1,128)S(1)}, s32[1,16]{1,0:T(1,128)S(1)}, u32[]{:S(2)}, u32[]{:S(2)}) collective-permute-start(s32[1,16]{1,0:T(1,128)S(1)} %pass_lengths.1.x_ref), channel_id=1, source_target_pairs={{0,8},{8,0},{16,24},{24,16},{1,9},{9,1},{17,25},{25,17},{2,10},{10... | collective-permute-start | bytes 200 | tf_op jit(solution)/shard_map/ppermute | solution.py:352
  70.9 3.5 %collective-permute-start.19 = (s32[1,16]{1,0:T(1,128)S(1)}, s32[1,16]{1,0:T(1,128)S(1)}, u32[]{:S(2)}, u32[]{:S(2)}) collective-permute-start(s32[1,16]{1,0:T(1,128)S(1)} %add_lengths.2.x_ref), channel_id=1, source_target_pairs={{0,16},{8,24},{16,0},{24,8},{1,17},{9,25},{17,1},{25,9},{2,18},{10... | collective-permute-start | bytes 200 | tf_op jit(solution)/shard_map/ppermute | solution.py:352
